TPU v7x, 32 devices: a whole 2x2x4 slice. The times are simulated.
32 devices in a mesh: sta: 8 (over z, y), tpl: 4 (over x, core).
Axes of the slice: x: 2, y: 2, z: 4, core: 2. Of those that a mesh axis runs over, the one named last changes fastest.
Arguments:
- waveform: float32 [16, 1536], P('sta', 'tpl'), may hold values from -6 to 6
- fir_taps: float32 [64], replicated, may hold values from -0.75 to 0.75
- templates: bfloat16 [512, 16, 1024], P('tpl', 'sta'), may hold values from -6 to 6
- presence: int32 [512, 16], P('tpl', 'sta'), may hold values from 0 to 1
- moveout: int32 [512, 16], P('tpl', 'sta'), may hold values from 0 to 128
Outputs:
- network_stack: float32 [4, 128, 384], P('tpl', 'sta')
All inputs are finite; a program needn't handle non-finite values.
Results may differ from a plain program's by a relative error of at most 0.0029.
Values may be sent and summed in bfloat16 or wider, within the bound.
No kernel may reach another device: no remote copies, remote signals or barrier semaphores. Data moves between devices by JAX's collectives and lax.ppermute only.
A program may use at most 64 MiB of HBM per device.

v0:
```python
import jax
import jax.numpy as jnp
from jax import lax
from jax.sharding import PartitionSpec as P

BLK = 128
SHIFT_MOST = 128


epsilon = 1e-06


def fir_apply(extended, coeffs):
    result = lax.conv_general_dilated(
        extended[:, None, :],
        coeffs[::-1][None, None, :],
        (1,),
        "VALID",
        precision=lax.Precision.HIGHEST,
    )
    return result[:, 0, :]


def hankel(samples):
    leading = samples.shape[:-1]
    row_total = samples.shape[-1] // BLK
    row_blocks = samples.reshape(leading + (row_total, BLK))
    windows = jnp.concatenate([row_blocks[..., :-1, :], row_blocks[..., 1:, :]], axis=-1)
    tiled_win = jnp.tile(windows, (1,) * (windows.ndim - 1) + (BLK + 1,))
    flat_win = tiled_win[..., : BLK * (2 * BLK + 1)]
    return flat_win.reshape(windows.shape[:-1] + (BLK, 2 * BLK + 1))[..., :BLK]


def shards(waveform, fir_taps, templates, presence, moveout):
    tap_count = fir_taps.shape[0]
    gathered = lax.all_gather(waveform, "tpl", axis=1, tiled=True)
    extended = jnp.pad(gathered, ((0, 0), (tap_count - 1, 0)))
    filtered = fir_apply(extended, fir_taps).astype(jnp.bfloat16)
    station_count = filtered.shape[0]
    templ_len = templates.shape[2]
    block_rows = templates.shape[0]
    corr_len = filtered.shape[1] - templ_len
    out_len = corr_len - SHIFT_MOST
    time_blocks = corr_len // BLK
    lag_blocks = templ_len // BLK
    values = filtered.astype(jnp.float32)
    prefix = jnp.concatenate(
        [jnp.zeros((station_count, 1), jnp.float32), jnp.cumsum(values * values, axis=1)], axis=1
    )
    energy = prefix[:, templ_len : templ_len + corr_len] - prefix[:, :corr_len]
    root_energy = jnp.sqrt(energy)
    hankel_rows = hankel(filtered)
    templ_norm = jnp.sqrt(jnp.sum(jnp.square(templates.astype(jnp.float32)), axis=-1) + epsilon)
    lag_index = jnp.arange(out_len, dtype=jnp.int32)
    templ_split = templates.reshape(block_rows, station_count, lag_blocks, BLK)
    products = jnp.zeros((station_count, block_rows, time_blocks, BLK), jnp.float32)
    for offset in range(lag_blocks):
        products = products + jnp.einsum(
            "ksb,scbd->skcd",
            templ_split[:, :, offset, :],
            hankel_rows[:, offset : offset + time_blocks],
            preferred_element_type=jnp.float32,
        )
    products = products.reshape(station_count, block_rows, corr_len)
    correlation = products / (templ_norm.T[:, :, None] * root_energy[:, None, :])
    shifts = moveout.T
    weights = presence.T.astype(jnp.float32)
    positions = shifts[:, :, None] + lag_index[None, None, :]
    aligned = jnp.take_along_axis(correlation, positions, axis=2)
    stacked = lax.psum_scatter(
        jnp.sum(weights[:, :, None] * aligned, axis=0), "sta", scatter_dimension=0, tiled=True
    )
    return stacked[None]


def solution(mesh):
    placed = (P("sta", "tpl"), P(), P("tpl", "sta", None), P("tpl", "sta"), P("tpl", "sta"))
    return jax.shard_map(
        shards, mesh=mesh, in_specs=placed, out_specs=P("tpl", "sta", None), check_vma=False
    )
```

profile of v0, /device:TPU:0, one launch (start us, length us, event | category | flops | bytes accessed | tf_op | source)
XLA Modules:
  0.0 906.2 jit_solution(4206907341960085684)
XLA Ops:
  6.5 6.3 all_gather.3
  13.2 0.8 rev.3
  14.1 15.2 %fusion.20 = bf16[16,200,1]{0,2,1:T(2,128)(2,1)S(1)} fusion(f32[1,16,263]{1,0,2:T(1,128)S(1)} %copy.74, f32[1,1,64]{1,0,2:T(1,128)S(1)} %copy.75), kind=kOutput, calls=%fused_computation.53 | convolution fusion | flops 2457600 | bytes 23488 | tf_op jit(solution)/shard_map/conv_general_dilated | solution.py:14
  29.6 0.7 copy.79
  30.3 1.2 multiply_reduce_fusion
  31.7 2.2 tile.10
  34.0 2.1 slice.110
  36.1 6.0 reshape.53
  42.1 1.4 fusion.18
  43.5 0.6 reduce-window.6
  44.6 0.9 sqrt_bitcast_fusion
  45.5 0.2 fusion.2
  45.8 0.3 fusion.13
  46.1 0.3 convolution_add_fusion.6
  46.4 0.3 convolution_add_fusion.5
  46.7 0.3 convolution_add_fusion.4
  47.0 0.3 convolution_add_fusion.3
  47.4 0.3 convolution_add_fusion.2
  47.6 0.3 convolution_add_fusion.1
  47.9 0.3 convolution_add_fusion
  48.2 0.2 bitcast_divide_fusion
  48.4 787.1 %gather_fusion = f32[98304]{0:T(1024)S(1)} fusion(f32[2,128,512]{1,2,0:T(8,128)S(1)} %bitcast_divide_fusion, s32[98304]{0:T(1024)S(1)} %reshape.72), kind=kCustom, calls=%fused_computation | custom fusion | bytes 1966080 | tf_op jit(solution)/shard_map/jit(take_along_axis)/gather | solution.py:69
  835.7 0.9 multiply_reduce_fusion.1
  836.6 62.7 %reduce-scatter.2.cloned.1.call-done = f32[16,384]{1,0:T(8,128)} async-done(((f32[128,384]{1,0:T(8,128)}), f32[16,384]{1,0:T(8,128)}) %reduce-scatter.2.cloned.1.call-update) | async-done | bytes 24592 | tf_op jit(solution)/shard_map/reduce_scatter | solution.py:70
  (46 shorter events, 1.7 us)
Async XLA Ops:
  6.5 892.8 %reduce-scatter.2.cloned.1.call-start = ((), (), s32[]{:S(2)}) async-start(), calls=%async_computation.1 | async-start | bytes 221184 | tf_op jit(solution)/shard_map/reduce_scatter | solution.py:70
  14.1 15.3 %copy-start.7 = (pred[16,200,1]{1,0,2:T(8,128)(4,1)S(1)}, pred[16,200,1]{1,0,2:T(8,128)(4,1)}, u32[]{:S(2)}) copy-start(pred[16,200,1]{1,0,2:T(8,128)(4,1)} %constant.39) | copy-start | bytes 9604
  14.1 15.5 %copy-start = (bf16[128,2,1024]{2,1,0:T(2,128)(2,1)S(1)}, bf16[128,2,1024]{2,1,0:T(2,128)(2,1)}, u32[]{:S(2)}) copy-start(bf16[128,2,1024]{2,1,0:T(2,128)(2,1)} %param.7) | copy-start | bytes 1572868
  42.1 3.4 copy-start.6
  43.5 2.6 copy-start.5
  43.5 2.9 copy-start.4
  45.7 1.0 copy-start.3
  46.1 1.0 copy-start.2
  46.4 1.0 copy-start.1
  48.4 787.2 %copy-start.8 = (s32[128,2]{0,1:T(2,128)S(1)}, s32[128,2]{0,1:T(2,128)}, u32[]{:S(2)}) copy-start(s32[128,2]{0,1:T(2,128)} %param.8) | copy-start | bytes 3076
Sparse Core Ops, SparseCore 0:
  836.7 62.5 reduce-scatter.1
where the time goes:
time: 906 us
  local copies, waits for them, and re-layouts  802 us (89%)
  waiting for transfers between devices  62.8 us (7%)
  matrix products  17.5 us (2%)
  between operations  13.7 us (2%)
    gather x3, local copies, waits for them, and re-layouts, shards(): aligned = jnp.take_along_axis(correlation, positions, axis=2)  787 us
    reduce_scatter x1, waiting for transfers between devices, shards(): lax.psum_scatter(jnp.sum(weights[:, :, None] * aligned, axis=0), 'sta', s...  62.7 us
  transfers between devices with their start and end apart: 1, of which 1 were waited for; matrix products, arithmetic and copies ran while one was open for 0% of the time, Pallas kernels for 0%

commit v1 on v0

v1 whole, which is shorter than its diff:
```python
import functools

import jax
import jax.numpy as jnp
from jax import lax
from jax.experimental import pallas as pl
from jax.experimental.pallas import tpu as pltpu
from jax.sharding import PartitionSpec as P

SHIFT_MOST = 128
LANES = 128
epsilon = 1e-06


def lane_gather(values, index):
    return jnp.take_along_axis(values, index, axis=1, mode="promise_in_bounds")


def prep_kernel(templ_ref, presence_ref, moveout_ref, rows_ref, scale_ref, shift_ref):
    stations, block_rows, _ = rows_ref.shape
    for s in range(stations):
        rows = templ_ref[:, s, :]
        rows_ref[s] = rows
        wide = rows.astype(jnp.float32)
        norm = jnp.sqrt(jnp.sum(wide * wide, axis=1, keepdims=True) + epsilon)
        used = jnp.broadcast_to(presence_ref[s : s + 1, :].astype(jnp.float32), (LANES, block_rows)).T
        scale_ref[s] = used / norm
        shift_ref[s] = jnp.broadcast_to(moveout_ref[s : s + 1, :], (LANES, block_rows)).T


def main_kernel(wave_ref, taps_ref, rows_ref, scale_ref, shift_ref, out_ref, hankel_ref):
    stations, block_rows, templ_len = rows_ref.shape
    taps = taps_ref.shape[0]
    samples = wave_ref.shape[1]
    out_len = out_ref.shape[1]
    corr_len = out_len + SHIFT_MOST
    columns = samples // LANES
    lane = lax.broadcasted_iota(jnp.int32, (LANES, LANES), 1)
    row = lax.broadcasted_iota(jnp.int32, (LANES, LANES), 0)
    ahead = lane + row
    ahead_index, ahead_wraps = ahead & (LANES - 1), ahead >= LANES
    back = (lane - row)[:taps]
    back_index, back_wraps = back & (LANES - 1), back < 0
    coeffs = taps_ref[...]
    total = None
    for s in range(stations):
        series = []
        before = jnp.zeros((taps, LANES), jnp.float32)
        for c in range(columns):
            piece = jnp.broadcast_to(wave_ref[s : s + 1, c * LANES : (c + 1) * LANES], (taps, LANES))
            moved = lane_gather(piece, back_index)
            series.append(jnp.sum(coeffs * jnp.where(back_wraps, before, moved), axis=0, keepdims=True))
            before = moved
        squares = []
        prior = None
        for c in range(columns):
            rounded = series[c].astype(jnp.bfloat16).astype(jnp.float32)
            moved = lane_gather(jnp.broadcast_to(rounded, (LANES, LANES)), ahead_index)
            if prior is not None:
                joined = jnp.where(ahead_wraps, moved, prior)
                hankel_ref[s, :, (c - 1) * LANES : c * LANES] = joined.astype(jnp.bfloat16)
                squares.append(jnp.sum(joined * joined, axis=0, keepdims=True))
            prior = moved
        lags = templ_len // LANES
        energy = []
        for t in range(corr_len // LANES):
            part = squares[t]
            for j in range(1, lags):
                part = part + squares[t + j]
            energy.append(part)
        inverse = lax.rsqrt(jnp.concatenate(energy, axis=1))
        raw = None
        for j in range(0, lags, 2):
            window = jnp.concatenate(
                [hankel_ref[s, :, (j + h) * LANES : (j + h) * LANES + corr_len] for h in range(2)], axis=0
            )
            part = jnp.dot(
                rows_ref[s, :, j * LANES : (j + 2) * LANES], window, preferred_element_type=jnp.float32
            )
            raw = part if raw is None else raw + part
        correlation = raw * inverse
        moved_lane = lane[:block_rows] + shift_ref[s]
        index, wraps = moved_lane & (LANES - 1), moved_lane >= LANES
        moved = [
            lane_gather(correlation[:, c * LANES : (c + 1) * LANES], index) for c in range(corr_len // LANES)
        ]
        scale = scale_ref[s]
        aligned = [scale * jnp.where(wraps, moved[c + 1], moved[c]) for c in range(out_len // LANES)]
        total = aligned if total is None else [a + b for a, b in zip(total, aligned)]
    for c, part in enumerate(total):
        out_ref[:, c * LANES : (c + 1) * LANES] = part


def shards(waveform, fir_taps, templates, presence, moveout):
    block_rows, stations, templ_len = templates.shape
    owners = lax.axis_size("sta")
    me = lax.axis_index("sta")
    vmem = pl.BlockSpec(memory_space=pltpu.VMEM)
    rows, scale, shift = pl.pallas_call(
        prep_kernel,
        out_shape=(
            jax.ShapeDtypeStruct((stations, block_rows, templ_len), jnp.bfloat16),
            jax.ShapeDtypeStruct((stations, block_rows, LANES), jnp.float32),
            jax.ShapeDtypeStruct((stations, block_rows, LANES), jnp.int32),
        ),
        in_specs=[vmem] * 3,
        out_specs=(vmem,) * 3,
    )(templates, presence.T, moveout.T)
    wave = lax.all_gather(waveform, "tpl", axis=1, tiled=True)
    samples = wave.shape[1]
    out_len = samples - templ_len - SHIFT_MOST
    stack = pl.pallas_call(
        main_kernel,
        out_shape=jax.ShapeDtypeStruct((block_rows, out_len), jnp.float32),
        in_specs=[vmem] * 5,
        out_specs=vmem,
        scratch_shapes=[pltpu.VMEM((stations, LANES, samples), jnp.bfloat16)],
    )(wave, fir_taps[:, None], rows, scale, shift)
    stack = stack.reshape(owners, block_rows // owners, out_len)
    bit = 1
    while bit < owners:
        half = stack.shape[0] // 2
        pairs = stack.reshape(half, 2, -1, out_len)
        side = (me // bit) % 2
        keep = lax.dynamic_index_in_dim(pairs, side, 1, keepdims=False)
        send = lax.dynamic_index_in_dim(pairs, 1 - side, 1, keepdims=False).astype(jnp.bfloat16)
        got = lax.ppermute(send, "sta", [(i, i ^ bit) for i in range(owners)])
        stack = keep + got.astype(jnp.float32)
        bit *= 2
    return stack.reshape(1, block_rows // owners, out_len)


def solution(mesh):
    placed = (P("sta", "tpl"), P(), P("tpl", "sta", None), P("tpl", "sta"), P("tpl", "sta"))
    return jax.shard_map(
        shards, mesh=mesh, in_specs=placed, out_specs=P("tpl", "sta", None), check_vma=False
    )
```

time: 906 us -> 31.3 us (0.03)
  local copies, waits for them, and re-layouts: 802 us -> 2.97 us
  waiting for transfers between devices: 62.8 us -> 5.78 us
  matrix products: 17.5 us -> 0 us
  between operations: 13.7 us -> 0.03 us
    gather x3 -> x0, local copies, waits for them, and re-layouts: 787 us -> none  [shards(): aligned = jnp.take_along_axis(correlation, positions, axis=2)]
    reduce_scatter x1 -> x0, waiting for transfers between devices: 62.7 us -> none  [shards(): lax.psum_scatter(jnp.sum(weights[:, :, None] * aligned, axis=0), 'sta', s...]
    conv_general_dilated x1 -> x0, matrix products: 15.2 us -> none  [fir_apply(): lax.conv_general_dilated(extended[:, None, :], coeffs[::-1][None, None, :...]
  transfers between devices with their start and end apart: 1 -> 3, of which waited for: 1 -> 3; matrix products, arithmetic and copies ran while one was open for 0% -> 0% of each run, Pallas kernels for 0% -> 0%
where the time goes in v1:
time: 31.3 us; the launch traced here: 31.1 us
  Pallas kernels  7.22 us (23%)
  starting transfers between devices  7.01 us (22%)
  blocking collectives  6.53 us (21%)
  waiting for transfers between devices  5.78 us (18%)
  local copies, waits for them, and re-layouts  2.97 us (9%)
  other arithmetic  1.52 us (5%)
    ppermute x3, starting transfers between devices, shards(): got = lax.ppermute(send, 'sta', [(i, i ^ bit) for i in range(owners)])  7.01 us
    all_gather x1, blocking collectives, shards(): wave = lax.all_gather(waveform, 'tpl', axis=1, tiled=True)  6.53 us
    ppermute x3, waiting for transfers between devices, shards(): got = lax.ppermute(send, 'sta', [(i, i ^ bit) for i in range(owners)])  5.78 us
    pallas_call x1, Pallas kernels, shards(): pl.pallas_call(prep_kernel, out_shape=(jax.ShapeDtypeStruct((stations, bl...  3.62 us
    pallas_call x1, Pallas kernels, shards(): pl.pallas_call(main_kernel, out_shape=jax.ShapeDtypeStruct((block_rows, o...  3.6 us
    add x3, other arithmetic, shards(): stack = keep + got.astype(jnp.float32)  1.52 us
    unnamed x4, local copies, waits for them, and re-layouts  1.34 us
    convert_element_type x3, local copies, waits for them, and re-layouts, shards(): lax.dynamic_index_in_dim(pairs, 1 - side, 1, keepdims=False)  0.93 us
  transfers between devices with their start and end apart: 3, of which 3 were waited for; matrix products, arithmetic and copies ran while one was open for 0% of the time, Pallas kernels for 0%

profile of v1, /device:TPU:0, one launch (start us, length us, event | category | flops | bytes accessed | tf_op | source)
XLA Modules:
  0.0 31.1 jit_solution(7579885018759226349)
XLA Ops:
  0.0 0.0 copy-start
  0.0 0.7 %copy-done = f32[2,384]{1,0:T(2,128)S(1)} copy-done((f32[2,384]{1,0:T(2,128)S(1)}, f32[2,384]{1,0:T(2,128)}, u32[]{:S(2)}) %copy-start) | copy-done | bytes 3096
  0.7 6.5 %all_gather.3.wave_ref = f32[2,1536]{1,0:T(2,128)} all-gather(f32[2,384]{1,0:T(2,128)S(1)} %copy-done), channel_id=1, replica_groups=mesh['sta'=8,'tpl'=4] {'tpl'}, dimensions={1}, use_global_device_ids=true | all-gather | bytes 15360 | tf_op jit(solution)/shard_map/all_gather | solution.py:109
  7.2 0.0 copy-start.1
  7.2 0.7 %copy-done.1 = f32[64]{0:T(128)S(1)} copy-done((f32[64]{0:T(128)S(1)}, f32[64]{0:T(128)}, u32[]{:S(2)}) %copy-start.1) | copy-done | bytes 280
  7.9 0.7 %copy.7.taps_ref = f32[64,1]{1,0:T(8,128)} copy(f32[64,1]{0,1:T(1,128)S(1)} %bitcast.23) | data formatting | bytes 512 | tf_op jit(solution)/shard_map/broadcast_in_dim | solution.py:118
  8.6 3.6 %shard_map.55 = (bf16[2,128,1024]{2,1,0:T(8,128)(2,1)}, f32[2,128,128]{2,1,0:T(8,128)}, s32[2,128,128]{2,1,0:T(8,128)}) custom-call(bf16[128,2,1024]{2,1,0:T(2,128)(2,1)} %templ_ref.1, s32[2,128]{1,0:T(2,128)} %bitcast.21, s32[2,128]{1,0:T(2,128)} %bitcast.22), custom_call_target="tpu_custom_call" | custom-call | tf_op jit(solution)/shard_map/pallas_call | solution.py:99
  12.2 3.6 %shard_map.56 = f32[128,384]{1,0:T(8,128)} custom-call(f32[2,1536]{1,0:T(2,128)} %all_gather.3.wave_ref, f32[64,1]{1,0:T(8,128)} %copy.7.taps_ref, bf16[2,128,1024]{2,1,0:T(8,128)(2,1)} %get-tuple-element.8.rows_ref, f32[2,128,128]{2,1,0:T(8,128)} %get-tuple-element.9.scale_ref, s32[2,128,128]{2,1,0:T(8,128)} %get-tuple-element.10.shift_ref), custom_call_target="tpu_custom_call" | custom-call | tf_op jit(solution)/shard_map/pallas_call | solution.py:112
  15.8 0.9 %fusion = bf16[4,16,384]{2,1,0:T(8,128)(2,1)S(1)} fusion(f32[4,2,16,384]{3,2,1,0:T(8,128)} %bitcast.17, s32[]{:T(128)S(6)} %select_n.46), kind=kLoop, calls=%fused_computation.2 | loop fusion | bytes 98308 | tf_op jit(solution)/shard_map/convert_element_type | solution.py:126
  16.7 2.0 %collective-permute-start = (bf16[4,16,384]{2,1,0:T(8,128)(2,1)S(1)}, bf16[4,16,384]{2,1,0:T(8,128)(2,1)S(1)}, u32[]{:S(2)}, u32[]{:S(2)}) collective-permute-start(bf16[4,16,384]{2,1,0:T(8,128)(2,1)S(1)} %fusion), channel_id=1, source_target_pairs={{0,4},{4,0},{8,12},{12,8},{16,20},{20,16},{24,28},{28,24},{1,5},{5... | collective-permute-start | bytes 147464 | tf_op jit(solution)/shard_map/ppermute | solution.py:127
  18.7 2.2 %collective-permute-done = bf16[4,16,384]{2,1,0:T(8,128)(2,1)S(1)} collective-permute-done((bf16[4,16,384]{2,1,0:T(8,128)(2,1)S(1)}, bf16[4,16,384]{2,1,0:T(8,128)(2,1)S(1)}, u32[]{:S(2)}, u32[]{:S(2)}) %collective-permute-start) | collective-permute-done | bytes 49184 | tf_op jit(solution)/shard_map/ppermute | solution.py:127
  20.9 0.9 %bitcast_add_fusion = f32[4,16,384]{2,1,0:T(8,128)S(1)} fusion(bf16[4,16,384]{2,1,0:T(8,128)(2,1)S(1)} %collective-permute-done, f32[4,2,16,384]{3,2,1,0:T(8,128)} %bitcast.18, s32[]{:T(128)S(6)} %select_n.45), kind=kLoop, calls=%fused_computation.1 | loop fusion | flops 49152 | bytes 245764 | tf_op jit(solution)/shard_map/add | solution.py:128
  21.9 2.0 %collective-permute-start.1 = (bf16[2,16,384]{2,1,0:T(8,128)(2,1)S(1)}, bf16[2,16,384]{2,1,0:T(8,128)(2,1)S(1)}, u32[]{:S(2)}, u32[]{:S(2)}) collective-permute-start(bf16[2,16,384]{2,1,0:T(8,128)(2,1)S(1)} %fusion.1), channel_id=1, source_target_pairs={{0,8},{4,12},{8,0},{12,4},{16,24},{20,28},{24,16},{28,20},{1,9},{5... | collective-permute-start | bytes 73736 | tf_op jit(solution)/shard_map/ppermute | solution.py:127
  23.9 1.9 %collective-permute-done.1 = bf16[2,16,384]{2,1,0:T(8,128)(2,1)S(1)} collective-permute-done((bf16[2,16,384]{2,1,0:T(8,128)(2,1)S(1)}, bf16[2,16,384]{2,1,0:T(8,128)(2,1)S(1)}, u32[]{:S(2)}, u32[]{:S(2)}) %collective-permute-start.1) | collective-permute-done | bytes 24608 | tf_op jit(solution)/shard_map/ppermute | solution.py:127
  25.8 3.0 %collective-permute-start.2 = (bf16[1,16,384]{2,1,0:T(8,128)(2,1)S(1)}, bf16[1,16,384]{2,1,0:T(8,128)(2,1)S(1)}, u32[]{:S(2)}, u32[]{:S(2)}) collective-permute-start(bf16[1,16,384]{2,1,0:T(8,128)(2,1)S(1)} %dynamic-slice_convert_fusion.1), channel_id=1, source_target_pairs={{0,16},{4,20},{8,24},{12,28},{16,0},{20,4},{24,8},{28,12},{1,17},{... | collective-permute-start | bytes 36872 | tf_op jit(solution)/shard_map/ppermute | solution.py:127
  28.8 1.7 %collective-permute-done.2 = bf16[1,16,384]{2,1,0:T(8,128)(2,1)S(1)} collective-permute-done((bf16[1,16,384]{2,1,0:T(8,128)(2,1)S(1)}, bf16[1,16,384]{2,1,0:T(8,128)(2,1)S(1)}, u32[]{:S(2)}, u32[]{:S(2)}) %collective-permute-start.2) | collective-permute-done | bytes 12320 | tf_op jit(solution)/shard_map/ppermute | solution.py:127
  30.5 0.6 %convert_add_fusion = f32[1,16,384]{2,1,0:T(8,128)} fusion(bf16[1,16,384]{2,1,0:T(8,128)(2,1)S(1)} %collective-permute-done.2, f32[2,16,384]{2,1,0:T(8,128)S(1)} %bitcast_add_fusion.1, s32[]{:T(128)S(6)} %select_n.53), kind=kLoop, calls=%fused_computation.6 | loop fusion | flops 12288 | bytes 61444 | tf_op jit(solution)/shard_map/add | solution.py:128
  (3 shorter events, 0.0 us)
Async XLA Ops:
  0.0 0.7 %copy-start = (f32[2,384]{1,0:T(2,128)S(1)}, f32[2,384]{1,0:T(2,128)}, u32[]{:S(2)}) copy-start(f32[2,384]{1,0:T(2,128)} %param.5) | copy-start | bytes 9220
  7.2 0.7 %copy-start.1 = (f32[64]{0:T(128)S(1)}, f32[64]{0:T(128)}, u32[]{:S(2)}) copy-start(f32[64]{0:T(128)} %param.6) | copy-start | bytes 772
  16.7 4.2 %collective-permute-start = (bf16[4,16,384]{2,1,0:T(8,128)(2,1)S(1)}, bf16[4,16,384]{2,1,0:T(8,128)(2,1)S(1)}, u32[]{:S(2)}, u32[]{:S(2)}) collective-permute-start(bf16[4,16,384]{2,1,0:T(8,128)(2,1)S(1)} %fusion), channel_id=1, source_target_pairs={{0,4},{4,0},{8,12},{12,8},{16,20},{20,16},{24,28},{28,24},{1,5},{5... | collective-permute-start | bytes 147464 | tf_op jit(solution)/shard_map/ppermute | solution.py:127
  21.9 3.9 %collective-permute-start.1 = (bf16[2,16,384]{2,1,0:T(8,128)(2,1)S(1)}, bf16[2,16,384]{2,1,0:T(8,128)(2,1)S(1)}, u32[]{:S(2)}, u32[]{:S(2)}) collective-permute-start(bf16[2,16,384]{2,1,0:T(8,128)(2,1)S(1)} %fusion.1), channel_id=1, source_target_pairs={{0,8},{4,12},{8,0},{12,4},{16,24},{20,28},{24,16},{28,20},{1,9},{5... | collective-permute-start | bytes 73736 | tf_op jit(solution)/shard_map/ppermute | solution.py:127
  25.8 4.7 %collective-permute-start.2 = (bf16[1,16,384]{2,1,0:T(8,128)(2,1)S(1)}, bf16[1,16,384]{2,1,0:T(8,128)(2,1)S(1)}, u32[]{:S(2)}, u32[]{:S(2)}) collective-permute-start(bf16[1,16,384]{2,1,0:T(8,128)(2,1)S(1)} %dynamic-slice_convert_fusion.1), channel_id=1, source_target_pairs={{0,16},{4,20},{8,24},{12,28},{16,0},{20,4},{24,8},{28,12},{1,17},{... | collective-permute-start | bytes 36872 | tf_op jit(solution)/shard_map/ppermute | solution.py:127

commit v2 on v1

v2 whole, which is shorter than its diff:
```python
import functools

import jax
import jax.numpy as jnp
from jax import lax
from jax.experimental import pallas as pl
from jax.experimental.pallas import tpu as pltpu
from jax.sharding import PartitionSpec as P

SHIFT_MOST = 128
LANES = 128
CHUNKS = 4
epsilon = 1e-06


def lane_gather(values, index):
    return jnp.take_along_axis(values, index, axis=1, mode="promise_in_bounds")


def as_column(row):
    return jnp.broadcast_to(row, (LANES, row.shape[1])).T


def rows_kernel(templ_hbm, rows_ref, norm_ref, templ_ref, sems):
    groups, _, owned, stations, _ = templ_ref.shape
    per = groups // CHUNKS if groups % CHUNKS == 0 else groups
    starts = range(0, groups, per)
    chunks = [
        pltpu.make_async_copy(templ_hbm.at[pl.ds(g, per)], templ_ref.at[pl.ds(g, per)], sems.at[g // per])
        for g in starts
    ]
    for copy in chunks:
        copy.start()
    for copy, g in zip(chunks, starts):
        copy.wait()
        at = g * owned
        for s in range(stations):
            for b in range(2):
                rows = templ_ref[g : g + per, b, :, s, :].reshape(per * owned, -1)
                rows_ref[s, b, at : at + per * owned] = rows
                wide = rows.astype(jnp.float32)
                total = jnp.sum(wide * wide, axis=1, keepdims=True)
                norm_ref[s, b, at : at + per * owned] = jnp.broadcast_to(
                    lax.rsqrt(total + epsilon), (per * owned, LANES)
                )


def columns_kernel(owners, wave_in, taps_ref, presence_ref, moveout_ref, wave_ref, coeffs_ref, used_ref, shift_ref):
    stations, _, half_rows, _ = used_ref.shape
    owned = half_rows * 2 // owners
    wave_ref[...] = wave_in[...]
    coeffs_ref[...] = as_column(taps_ref[...])
    place = lax.broadcasted_iota(jnp.int32, (LANES, half_rows * 2), 1)
    half, rest = place // half_rows, place % half_rows
    old = (rest // owned * 2 + half) * owned + rest % owned
    for s in range(stations):
        shift = lane_gather(jnp.broadcast_to(moveout_ref[s : s + 1, :], old.shape), old)
        shift_ref[s] = shift.T.reshape(shift_ref.shape[1:])
        used = lane_gather(jnp.broadcast_to(presence_ref[s : s + 1, :], old.shape), old)
        used_ref[s] = used.astype(jnp.float32).T.reshape(used_ref.shape[1:])


def correlate(rows_of, scale_of, shift_of, window_of, inverse_of, stations, templ_len, out_len):
    total = None
    for s in range(stations):
        raw = None
        for j in range(0, templ_len // LANES, 2):
            part = jnp.dot(rows_of(s, j), window_of(s, j), preferred_element_type=jnp.float32)
            raw = part if raw is None else raw + part
        correlation = raw * inverse_of(s)
        shift = shift_of(s)
        moved_lane = lax.broadcasted_iota(jnp.int32, shift.shape, 1) + shift
        index, wraps = moved_lane & (LANES - 1), moved_lane >= LANES
        moved = [
            lane_gather(correlation[:, at : at + LANES], index) for at in range(0, out_len + SHIFT_MOST, LANES)
        ]
        scale = scale_of(s)
        aligned = [scale * jnp.where(wraps, moved[c + 1], moved[c]) for c in range(out_len // LANES)]
        total = aligned if total is None else [a + b for a, b in zip(total, aligned)]
    return total


def half_of(half, rows_ref, norm_ref, used_ref, shift_ref, hankel_ref, inverse_ref, out_ref):
    stations, _, _, templ_len = rows_ref.shape
    out_len = out_ref.shape[2]
    corr_len = out_len + SHIFT_MOST

    def window(s, j):
        at = j * LANES
        return jnp.concatenate(
            [hankel_ref[s, :, at : at + corr_len], hankel_ref[s, :, at + LANES : at + LANES + corr_len]], axis=0
        )

    total = correlate(
        lambda s, j: rows_ref[s, half, :, j * LANES : (j + 2) * LANES],
        lambda s: norm_ref[s, half] * used_ref[s, half],
        lambda s: shift_ref[s, half],
        window,
        lambda s: inverse_ref[s : s + 1, :],
        stations, templ_len, out_len,
    )
    for c, part in enumerate(total):
        out_ref[:, :, c * LANES : (c + 1) * LANES] = part.astype(out_ref.dtype).reshape(
            out_ref.shape[0], out_ref.shape[1], LANES
        )


def send_kernel(*refs):
    *segment_refs, coeffs_ref, rows_ref, norm_ref, used_ref, shift_ref, send_ref, hankel_ref, inverse_ref, wave_ref = refs
    stations, templ_len = rows_ref.shape[0], rows_ref.shape[3]
    segments = len(segment_refs)
    seg_len = segment_refs[0].shape[1]
    taps = coeffs_ref.shape[0]
    corr_len = inverse_ref.shape[1]
    columns = segments * seg_len // LANES
    tpl = lax.axis_index("tpl")
    for distance, segment_ref in enumerate(segment_refs):
        wave_ref[tpl ^ distance] = segment_ref[...]
    lane = lax.broadcasted_iota(jnp.int32, (LANES, LANES), 1)
    row = lax.broadcasted_iota(jnp.int32, (LANES, LANES), 0)
    ahead = lane + row
    ahead_index, ahead_wraps = ahead & (LANES - 1), ahead >= LANES
    back = (lane - row)[:taps]
    back_index, back_wraps = back & (LANES - 1), back < 0
    coeffs = coeffs_ref[...]
    for s in range(stations):
        series = []
        before = jnp.zeros((taps, LANES), jnp.float32)
        for c in range(columns):
            at = c * LANES
            piece = wave_ref[at // seg_len, s : s + 1, at % seg_len : at % seg_len + LANES]
            moved = lane_gather(jnp.broadcast_to(piece, (taps, LANES)), back_index)
            series.append(jnp.sum(coeffs * jnp.where(back_wraps, before, moved), axis=0, keepdims=True))
            before = moved
        squares = []
        prior = None
        for c in range(columns):
            rounded = series[c].astype(jnp.bfloat16).astype(jnp.float32)
            moved = lane_gather(jnp.broadcast_to(rounded, (LANES, LANES)), ahead_index)
            if prior is not None:
                joined = jnp.where(ahead_wraps, moved, prior)
                hankel_ref[s, :, (c - 1) * LANES : c * LANES] = joined.astype(jnp.bfloat16)
                squares.append(jnp.sum(joined * joined, axis=0, keepdims=True))
            prior = moved
        for t in range(corr_len // LANES):
            part = squares[t]
            for j in range(1, templ_len // LANES):
                part = part + squares[t + j]
            inverse_ref[s : s + 1, t * LANES : (t + 1) * LANES] = lax.rsqrt(part)
    half_of(1 - (lax.axis_index("sta") & 1), rows_ref, norm_ref, used_ref, shift_ref, hankel_ref, inverse_ref, send_ref)


def keep_kernel(rows_ref, norm_ref, used_ref, shift_ref, hankel_ref, inverse_ref, keep_ref):
    half_of(lax.axis_index("sta") & 1, rows_ref, norm_ref, used_ref, shift_ref, hankel_ref, inverse_ref, keep_ref)


def flip(value, axis, bit):
    return lax.ppermute(value, axis, [(i, i ^ bit) for i in range(lax.axis_size(axis))])


def shards(waveform, fir_taps, templates, presence, moveout):
    block_rows, stations, templ_len = templates.shape
    owners, segments = lax.axis_size("sta"), lax.axis_size("tpl")
    sta = lax.axis_index("sta")
    samples = segments * waveform.shape[1]
    corr_len = samples - templ_len
    out_len = corr_len - SHIFT_MOST
    owned = block_rows // owners
    half_rows = block_rows // 2
    vmem = pl.BlockSpec(memory_space=pltpu.VMEM)
    hbm = pl.BlockSpec(memory_space=pltpu.HBM)
    params = pltpu.CompilerParams(vmem_limit_bytes=16 * 1024 * 1024)
    prep_params = pltpu.CompilerParams(vmem_limit_bytes=53 * 1024 * 1024)

    def cost(flops):
        return pl.CostEstimate(flops=flops, bytes_accessed=1 << 20, transcendentals=0)

    paired = (owners // 2, 2, owned, stations, templ_len)
    rows, norm = pl.pallas_call(
        rows_kernel,
        out_shape=(
            jax.ShapeDtypeStruct((stations, 2, half_rows, templ_len), jnp.bfloat16),
            jax.ShapeDtypeStruct((stations, 2, half_rows, LANES), jnp.float32),
        ),
        in_specs=[hbm],
        out_specs=(vmem,) * 2,
        scratch_shapes=[pltpu.VMEM(paired, jnp.bfloat16), pltpu.SemaphoreType.DMA((CHUNKS,))],
        compiler_params=prep_params,
        cost_estimate=cost(1 << 20),
        name="template_rows",
    )(templates.reshape(paired))
    own, coeffs, used, shift = pl.pallas_call(
        functools.partial(columns_kernel, owners),
        out_shape=(
            jax.ShapeDtypeStruct(waveform.shape, jnp.float32),
            jax.ShapeDtypeStruct((fir_taps.shape[0], LANES), jnp.float32),
            jax.ShapeDtypeStruct((stations, 2, half_rows, LANES), jnp.float32),
            jax.ShapeDtypeStruct((stations, 2, half_rows, LANES), jnp.int32),
        ),
        in_specs=[vmem] * 4,
        out_specs=(vmem,) * 4,
        compiler_params=params,
        cost_estimate=cost(1 << 20),
        name="columns",
    )(waveform, fir_taps[None, :], presence.T, moveout.T)
    bit = segments // 2
    sent = {0: waveform}
    while bit >= 1:
        for d, piece in list(sent.items()):
            sent[d ^ bit] = flip(piece, "tpl", bit)
        if bit == segments // 2:
            sent[bit], rows, norm = lax.optimization_barrier((sent[bit], rows, norm))
        bit //= 2
    sent[0] = own
    send, hankel, inverse = pl.pallas_call(
        send_kernel,
        out_shape=(
            jax.ShapeDtypeStruct((owners // 2, owned, out_len), jnp.bfloat16),
            jax.ShapeDtypeStruct((stations, LANES, samples), jnp.bfloat16),
            jax.ShapeDtypeStruct((stations, corr_len), jnp.float32),
        ),
        in_specs=[vmem] * (segments + 5),
        out_specs=(vmem,) * 3,
        scratch_shapes=[pltpu.VMEM((segments,) + waveform.shape, jnp.float32)],
        compiler_params=params,
        cost_estimate=cost(1 << 20),
        name="send_half",
    )(*[sent[d] for d in range(segments)], coeffs, rows, norm, used, shift)
    keep = pl.pallas_call(
        keep_kernel,
        out_shape=jax.ShapeDtypeStruct((owners // 2, owned, out_len), jnp.float32),
        in_specs=[vmem] * 6,
        out_specs=vmem,
        compiler_params=params,
        cost_estimate=cost(1 << 20),
        name="keep_half",
    )(rows, norm, used, shift, hankel, inverse)
    stack = keep
    bit = 1
    while True:
        stack = stack + flip(send, "sta", bit).astype(jnp.float32)
        bit *= 2
        if bit >= owners:
            break
        pairs = stack.reshape(stack.shape[0] // 2, 2, owned, out_len)
        side = (sta // bit) % 2
        stack = lax.dynamic_index_in_dim(pairs, side, 1, keepdims=False)
        send = lax.dynamic_index_in_dim(pairs, 1 - side, 1, keepdims=False).astype(jnp.bfloat16)
    return stack


def solution(mesh):
    placed = (P("sta", "tpl"), P(), P("tpl", "sta", None), P("tpl", "sta"), P("tpl", "sta"))
    return jax.shard_map(
        shards, mesh=mesh, in_specs=placed, out_specs=P("tpl", "sta", None), check_vma=False
    )
```

time: 31.3 us -> 22.1 us (0.71)
  blocking collectives: 6.53 us -> 0 us
  starting transfers between devices: 7.01 us -> 9.4 us
  Pallas kernels: 7.22 us -> 4.89 us
  local copies, waits for them, and re-layouts: 2.97 us -> 0.71 us
  other arithmetic: 1.52 us -> 0.63 us
  waiting for transfers between devices: 5.78 us -> 6.24 us
    all_gather x1 -> x0, blocking collectives: 6.53 us -> none  [shards(): wave = lax.all_gather(waveform, 'tpl', axis=1, tiled=True)]
    ppermute x3 -> x6, starting transfers between devices: 7.01 us -> 9.4 us  [flip(): lax.ppermute(value, axis, [(i, i ^ bit) for i in range(lax.axis_size(axis...]
    pallas_call x2 -> x4, Pallas kernels: 7.22 us -> 4.89 us  [the longest x1 2.55 us: shards(): pl.pallas_call(rows_kernel, out_shape=(jax.ShapeDtypeStruct((stations, 2,...]
    convert_element_type x3 -> x2, local copies, waits for them, and re-layouts: 0.93 us -> 0.03 us  [shards(): lax.dynamic_index_in_dim(pairs, 1 - side, 1, keepdims=False)]
    add x3, other arithmetic: 1.52 us -> 0.63 us  [shards(): stack = stack + flip(send, 'sta', bit).astype(jnp.float32)]
    broadcast_in_dim x1 -> x0, local copies, waits for them, and re-layouts: 0.7 us -> none  [shards(): fir_taps[:, None]]
    unnamed x4 -> x8, local copies, waits for them, and re-layouts: 1.34 us -> 0.69 us
    ppermute x3 -> x6, waiting for transfers between devices: 5.78 us -> 6.24 us  [flip(): lax.ppermute(value, axis, [(i, i ^ bit) for i in range(lax.axis_size(axis...]
  transfers between devices with their start and end apart: 3 -> 6, of which waited for: 3 -> 3; matrix products, arithmetic and copies ran while one was open for 0% -> 0% of each run, Pallas kernels for 0% -> 15%
where the time goes in v2:
time: 22.1 us; the launch traced here: 22 us
  starting transfers between devices  9.4 us (43%)
  waiting for transfers between devices  6.24 us (28%)
  Pallas kernels  4.89 us (22%)
  local copies, waits for them, and re-layouts  0.71 us (3%)
  other arithmetic  0.63 us (3%)
    ppermute x6, starting transfers between devices, flip(): lax.ppermute(value, axis, [(i, i ^ bit) for i in range(lax.axis_size(axis...  9.4 us
    ppermute x6, waiting for transfers between devices, flip(): lax.ppermute(value, axis, [(i, i ^ bit) for i in range(lax.axis_size(axis...  6.24 us
    pallas_call x1, Pallas kernels, shards(): pl.pallas_call(rows_kernel, out_shape=(jax.ShapeDtypeStruct((stations, 2,...  2.55 us
    pallas_call x1, Pallas kernels, shards(): pl.pallas_call(send_kernel, out_shape=(jax.ShapeDtypeStruct((owners // 2,...  1.54 us
    unnamed x8, local copies, waits for them, and re-layouts  0.69 us
    add x3, other arithmetic, shards(): stack = stack + flip(send, 'sta', bit).astype(jnp.float32)  0.63 us
    pallas_call x1, Pallas kernels, shards(): pl.pallas_call(keep_kernel, out_shape=jax.ShapeDtypeStruct((owners // 2,...  0.58 us
  transfers between devices with their start and end apart: 6, of which 3 were waited for; matrix products, arithmetic and copies ran while one was open for 0% of the time, Pallas kernels for 15%

profile of v2, /device:TPU:0, one launch (start us, length us, event | category | flops | bytes accessed | tf_op | source)
XLA Modules:
  0.0 22.0 jit_solution(18318089597762287558)
XLA Ops:
  0.0 2.9 %collective-permute-start = (f32[2,384]{1,0:T(2,128)}, f32[2,384]{1,0:T(2,128)S(1)}, u32[]{:S(2)}, u32[]{:S(2)}) collective-permute-start(f32[2,384]{1,0:T(2,128)} %wave_in.1), channel_id=1, source_target_pairs={{0,2},{1,3},{2,0},{3,1},{4,6},{5,7},{6,4},{7,5},{8,10},{9,11},{10,... | collective-permute-start | bytes 9224 | tf_op jit(solution)/shard_map/ppermute | solution.py:158
  2.9 0.0 collective-permute-start.1
  2.9 2.5 %template_rows.1 = (bf16[2,2,64,1024]{3,2,1,0:T(8,128)(2,1)S(1)}, f32[2,2,64,128]{3,2,1,0:T(8,128)S(1)}) custom-call(bf16[4,2,16,2,1024]{4,3,2,1,0:T(2,128)(2,1)} %bitcast.16), custom_call_target="tpu_custom_call" | custom-call | flops 1048576 | bytes 1048576 | tf_op jit(solution)/shard_map/template_rows/pallas_call | solution.py:179
  5.5 0.0 collective-permute-done.refs_2_
  5.5 0.0 copy-start.2
  5.5 0.0 copy-start
  5.5 0.6 %collective-permute-start.2 = (f32[2,384]{1,0:T(2,128)S(1)}, f32[2,384]{1,0:T(2,128)S(1)}, u32[]{:S(2)}, u32[]{:S(2)}) collective-permute-start(f32[2,384]{1,0:T(2,128)S(1)} %collective-permute-done.refs_2_), channel_id=1, source_target_pairs={{0,1},{1,0},{2,3},{3,2},{4,5},{5,4},{6,7},{7,6},{8,9},{9,8},{10,11... | collective-permute-start | bytes 9224 | tf_op jit(solution)/shard_map/ppermute | solution.py:158
  6.1 0.0 copy-start.1
  6.1 0.1 copy-done.2
  6.2 0.0 copy-done
  6.2 0.6 %copy-done.1 = s32[128,2]{0,1:T(2,128)S(1)} copy-done((s32[128,2]{0,1:T(2,128)S(1)}, s32[128,2]{0,1:T(2,128)}, u32[]{:S(2)}) %copy-start.1) | copy-done | bytes 1048
  6.8 0.0 copy-done.3
  6.8 0.2 columns.1
  7.0 0.0 collective-permute-done.1.refs_1_
  7.0 0.0 collective-permute-done.2.refs_3_
  7.0 1.5 %send_half.1 = (bf16[4,16,384]{2,1,0:T(8,128)(2,1)S(1)}, bf16[2,128,1536]{2,1,0:T(8,128)(2,1)S(1)}, f32[2,512]{1,0:T(2,128)S(1)}) custom-call(f32[2,384]{1,0:T(2,128)S(1)} %get-tuple-element.23.refs_0_, f32[2,384]{1,0:T(2,128)S(1)} %collective-permute-done.1.refs_1_, f32[2,384]{1,0:T(2,128)S(1)} %collective-permute-done.refs_2_, ...), custom_call_target="tpu_custom_call" | custom-call | flops 1048576 | bytes 1048576 | tf_op jit(solution)/shard_map/send_half/pallas_call | solution.py:215
  8.6 1.6 %collective-permute-start.3 = (bf16[4,16,384]{2,1,0:T(8,128)(2,1)S(1)}, bf16[4,16,384]{2,1,0:T(8,128)(2,1)S(1)}, u32[]{:S(2)}, u32[]{:S(2)}) collective-permute-start(bf16[4,16,384]{2,1,0:T(8,128)(2,1)S(1)} %get-tuple-element.28), channel_id=1, source_target_pairs={{0,4},{4,0},{8,12},{12,8},{16,20},{20,16},{24,28},{28,24},{1,5},{5... | collective-permute-start | bytes 147464 | tf_op jit(solution)/shard_map/ppermute | solution.py:158
  10.2 0.6 %keep_half.1 = f32[4,16,384]{2,1,0:T(8,128)S(1)} custom-call(bf16[2,2,64,1024]{3,2,1,0:T(8,128)(2,1)S(1)} %get-tuple-element.19.refs_5_.rows_ref, f32[2,2,64,128]{3,2,1,0:T(8,128)S(1)} %get-tuple-element.20.refs_6_.norm_ref, f32[2,2,64,128]{3,2,1,0:T(8,128)S(1)} %get-tuple-element.21.refs_7_.used_ref, ...), custom_call_target="tpu_custom_call" | custom-call | flops 1048576 | bytes 1048576 | tf_op jit(solution)/shard_map/keep_half/pallas_call | solution.py:229
  10.7 2.0 %collective-permute-done.3 = bf16[4,16,384]{2,1,0:T(8,128)(2,1)S(1)} collective-permute-done((bf16[4,16,384]{2,1,0:T(8,128)(2,1)S(1)}, bf16[4,16,384]{2,1,0:T(8,128)(2,1)S(1)}, u32[]{:S(2)}, u32[]{:S(2)}) %collective-permute-start.3) | collective-permute-done | bytes 49184 | tf_op jit(solution)/shard_map/ppermute | solution.py:158
  12.8 1.6 %collective-permute-start.4 = (bf16[2,16,384]{2,1,0:T(8,128)(2,1)S(1)}, bf16[2,16,384]{2,1,0:T(8,128)(2,1)S(1)}, u32[]{:S(2)}, u32[]{:S(2)}) collective-permute-start(bf16[2,16,384]{2,1,0:T(8,128)(2,1)S(1)} %fusion), channel_id=1, source_target_pairs={{0,8},{4,12},{8,0},{12,4},{16,24},{20,28},{24,16},{28,20},{1,9},{5... | collective-permute-start | bytes 73736 | tf_op jit(solution)/shard_map/ppermute | solution.py:158
  14.4 2.2 %collective-permute-done.4 = bf16[2,16,384]{2,1,0:T(8,128)(2,1)S(1)} collective-permute-done((bf16[2,16,384]{2,1,0:T(8,128)(2,1)S(1)}, bf16[2,16,384]{2,1,0:T(8,128)(2,1)S(1)}, u32[]{:S(2)}, u32[]{:S(2)}) %collective-permute-start.4) | collective-permute-done | bytes 24608 | tf_op jit(solution)/shard_map/ppermute | solution.py:158
  16.7 2.7 %collective-permute-start.5 = (bf16[1,16,384]{2,1,0:T(8,128)(2,1)S(1)}, bf16[1,16,384]{2,1,0:T(8,128)(2,1)S(1)}, u32[]{:S(2)}, u32[]{:S(2)}) collective-permute-start(bf16[1,16,384]{2,1,0:T(8,128)(2,1)S(1)} %dynamic-slice_convert_fusion), channel_id=1, source_target_pairs={{0,16},{4,20},{8,24},{12,28},{16,0},{20,4},{24,8},{28,12},{1,17},{... | collective-permute-start | bytes 36872 | tf_op jit(solution)/shard_map/ppermute | solution.py:158
  19.3 2.0 %collective-permute-done.5 = bf16[1,16,384]{2,1,0:T(8,128)(2,1)S(1)} collective-permute-done((bf16[1,16,384]{2,1,0:T(8,128)(2,1)S(1)}, bf16[1,16,384]{2,1,0:T(8,128)(2,1)S(1)}, u32[]{:S(2)}, u32[]{:S(2)}) %collective-permute-start.5) | collective-permute-done | bytes 12320 | tf_op jit(solution)/shard_map/ppermute | solution.py:158
  21.3 0.6 %convert_add_fusion.1 = f32[1,16,384]{2,1,0:T(8,128)} fusion(bf16[1,16,384]{2,1,0:T(8,128)(2,1)S(1)} %collective-permute-done.5, f32[2,16,384]{2,1,0:T(8,128)S(1)} %bitcast_add_fusion, s32[]{:T(128)S(6)} %select_n.38), kind=kLoop, calls=%fused_computation.4 | loop fusion | flops 12288 | bytes 61444 | tf_op jit(solution)/shard_map/add | solution.py:241
  (5 shorter events, 0.0 us)
Async XLA Ops:
  0.0 5.5 %collective-permute-start = (f32[2,384]{1,0:T(2,128)}, f32[2,384]{1,0:T(2,128)S(1)}, u32[]{:S(2)}, u32[]{:S(2)}) collective-permute-start(f32[2,384]{1,0:T(2,128)} %wave_in.1), channel_id=1, source_target_pairs={{0,2},{1,3},{2,0},{3,1},{4,6},{5,7},{6,4},{7,5},{8,10},{9,11},{10,... | collective-permute-start | bytes 9224 | tf_op jit(solution)/shard_map/ppermute | solution.py:158
  2.9 4.1 %collective-permute-start.1 = (f32[2,384]{1,0:T(2,128)}, f32[2,384]{1,0:T(2,128)S(1)}, u32[]{:S(2)}, u32[]{:S(2)}) collective-permute-start(f32[2,384]{1,0:T(2,128)} %wave_in.1), channel_id=1, source_target_pairs={{0,1},{1,0},{2,3},{3,2},{4,5},{5,4},{6,7},{7,6},{8,9},{9,8},{10,11... | collective-permute-start | bytes 9224 | tf_op jit(solution)/shard_map/ppermute | solution.py:158
  5.5 0.7 %copy-start.2 = (s32[128,2]{0,1:T(2,128)S(1)}, s32[128,2]{0,1:T(2,128)}, u32[]{:S(2)}) copy-start(s32[128,2]{0,1:T(2,128)} %param.9) | copy-start | bytes 3076
  5.5 0.7 %copy-start = (f32[2,384]{1,0:T(2,128)S(1)}, f32[2,384]{1,0:T(2,128)}, u32[]{:S(2)}) copy-start(f32[2,384]{1,0:T(2,128)} %wave_in.1) | copy-start | bytes 9220
  5.5 1.5 %collective-permute-start.2 = (f32[2,384]{1,0:T(2,128)S(1)}, f32[2,384]{1,0:T(2,128)S(1)}, u32[]{:S(2)}, u32[]{:S(2)}) collective-permute-start(f32[2,384]{1,0:T(2,128)S(1)} %collective-permute-done.refs_2_), channel_id=1, source_target_pairs={{0,1},{1,0},{2,3},{3,2},{4,5},{5,4},{6,7},{7,6},{8,9},{9,8},{10,11... | collective-permute-start | bytes 9224 | tf_op jit(solution)/shard_map/ppermute | solution.py:158
  6.1 0.7 %copy-start.1 = (s32[128,2]{0,1:T(2,128)S(1)}, s32[128,2]{0,1:T(2,128)}, u32[]{:S(2)}) copy-start(s32[128,2]{0,1:T(2,128)} %param.8) | copy-start | bytes 3076
  6.1 0.7 %copy-start.3 = (f32[64]{0:T(128)S(1)}, f32[64]{0:T(128)}, u32[]{:S(2)}) copy-start(f32[64]{0:T(128)} %param.6) | copy-start | bytes 772
  8.6 4.2 %collective-permute-start.3 = (bf16[4,16,384]{2,1,0:T(8,128)(2,1)S(1)}, bf16[4,16,384]{2,1,0:T(8,128)(2,1)S(1)}, u32[]{:S(2)}, u32[]{:S(2)}) collective-permute-start(bf16[4,16,384]{2,1,0:T(8,128)(2,1)S(1)} %get-tuple-element.28), channel_id=1, source_target_pairs={{0,4},{4,0},{8,12},{12,8},{16,20},{20,16},{24,28},{28,24},{1,5},{5... | collective-permute-start | bytes 147464 | tf_op jit(solution)/shard_map/ppermute | solution.py:158
  12.8 3.9 %collective-permute-start.4 = (bf16[2,16,384]{2,1,0:T(8,128)(2,1)S(1)}, bf16[2,16,384]{2,1,0:T(8,128)(2,1)S(1)}, u32[]{:S(2)}, u32[]{:S(2)}) collective-permute-start(bf16[2,16,384]{2,1,0:T(8,128)(2,1)S(1)} %fusion), channel_id=1, source_target_pairs={{0,8},{4,12},{8,0},{12,4},{16,24},{20,28},{24,16},{28,20},{1,9},{5... | collective-permute-start | bytes 73736 | tf_op jit(solution)/shard_map/ppermute | solution.py:158
  16.7 4.7 %collective-permute-start.5 = (bf16[1,16,384]{2,1,0:T(8,128)(2,1)S(1)}, bf16[1,16,384]{2,1,0:T(8,128)(2,1)S(1)}, u32[]{:S(2)}, u32[]{:S(2)}) collective-permute-start(bf16[1,16,384]{2,1,0:T(8,128)(2,1)S(1)} %dynamic-slice_convert_fusion), channel_id=1, source_target_pairs={{0,16},{4,20},{8,24},{12,28},{16,0},{20,4},{24,8},{28,12},{1,17},{... | collective-permute-start | bytes 36872 | tf_op jit(solution)/shard_map/ppermute | solution.py:158

commit v3 on v0

v3 whole, which is shorter than its diff:
```python
import functools

import jax
import jax.numpy as jnp
from jax import lax
from jax.experimental import pallas as pl
from jax.experimental.pallas import tpu as pltpu
from jax.sharding import PartitionSpec as P

SHIFT_MOST = 128
LANES = 128
PAIR = 2 * LANES
epsilon = 1e-06


def lane_gather(values, index):
    return jnp.take_along_axis(values, index, axis=1, mode="promise_in_bounds")


def as_column(row):
    return jnp.broadcast_to(row, (LANES, row.shape[1])).T


def columns_kernel(owners, wave_in, taps_in, presence_ref, moveout_ref, wave_ref, toeplitz_ref, used_ref, shift_ref, row_ref):
    stations, _, half_rows, _ = used_ref.shape
    owned = half_rows * 2 // owners
    taps = taps_in.shape[1]
    wave_ref[...] = wave_in[...]
    row_ref[...] = jnp.zeros_like(row_ref)
    row_ref[0:1, 0:taps] = taps_in[...]
    sample = lax.broadcasted_iota(jnp.int32, (PAIR, LANES), 0)
    lane = lax.broadcasted_iota(jnp.int32, (PAIR, LANES), 1)
    tap = PAIR - 1 - lane - sample
    picked = lane_gather(jnp.broadcast_to(row_ref[0:1, :], (PAIR, LANES)), tap & (LANES - 1))
    toeplitz_ref[...] = jnp.where((tap >= 0) & (tap < taps), picked, 0.0)
    place = lax.broadcasted_iota(jnp.int32, (LANES, half_rows * 2), 1)
    half, rest = place // half_rows, place % half_rows
    old = (rest // owned * 2 + half) * owned + rest % owned
    for s in range(stations):
        shift = lane_gather(jnp.broadcast_to(moveout_ref[s : s + 1, :], old.shape), old)
        shift_ref[s] = shift.T.reshape(shift_ref.shape[1:])
        used = lane_gather(jnp.broadcast_to(presence_ref[s : s + 1, :], old.shape), old)
        used_ref[s] = used.astype(jnp.float32).T.reshape(used_ref.shape[1:])


def stack_half(half, rows_ref, used_ref, shift_ref, hankel_ref, inverse_ref, out_ref):
    stations, groups, _, owned, templ_len = rows_ref.shape
    half_rows = groups * owned
    corr_len = inverse_ref.shape[1]
    out_len = out_ref.shape[2]
    lag_pairs, time_pairs = templ_len // PAIR, corr_len // PAIR
    total = None
    for s in range(stations):
        rows = rows_ref[s, :, half].reshape(half_rows, templ_len)
        raw = [None] * time_pairs
        for offset in range(1, lag_pairs + time_pairs):
            uses = [(j, offset - lag_pairs + j) for j in range(lag_pairs) if 0 <= offset - lag_pairs + j < time_pairs]
            at = offset * PAIR
            window = jnp.concatenate(
                [hankel_ref[s, :, at : at + PAIR], hankel_ref[s, :, at - LANES : at - LANES + PAIR]], axis=0
            )
            left = jnp.concatenate([rows[:, j * PAIR : (j + 1) * PAIR] for j, _ in uses], axis=0)
            product = jnp.dot(left, window, preferred_element_type=jnp.float32)
            for k, (_, t) in enumerate(uses):
                part = product[k * half_rows : (k + 1) * half_rows]
                raw[t] = part if raw[t] is None else raw[t] + part
        correlation = jnp.concatenate(raw, axis=1) * inverse_ref[s : s + 1, :]
        wide = rows.astype(jnp.float32)
        norm = lax.rsqrt(jnp.sum(wide * wide, axis=1, keepdims=True) + epsilon)
        shift = shift_ref[s, half]
        place = PAIR - 1 - lax.broadcasted_iota(jnp.int32, shift.shape, 1) - shift
        index, later = place & (LANES - 1), place >= LANES
        moved = [lane_gather(correlation[:, at : at + LANES], index) for at in range(0, corr_len, LANES)]
        last = corr_len // LANES - 1
        scale = norm * used_ref[s, half]
        aligned = [scale * jnp.where(later, moved[last - c], moved[last - 1 - c]) for c in range(out_len // LANES)]
        total = aligned if total is None else [a + b for a, b in zip(total, aligned)]
    for c, part in enumerate(total):
        out_ref[:, :, c * LANES : (c + 1) * LANES] = part.astype(out_ref.dtype).reshape(groups, owned, LANES)


def send_kernel(*refs):
    *segment_refs, toeplitz_ref, rows_ref, used_ref, shift_ref = refs[:-7]
    send_ref, hankel_ref, inverse_ref, wave_ref, series_ref, sums_of_ref, sums_ref = refs[-7:]
    stations, templ_len = rows_ref.shape[0], rows_ref.shape[-1]
    corr_len = inverse_ref.shape[1]
    seg_len = segment_refs[0].shape[1]
    blocks = len(segment_refs) * seg_len // LANES
    lags, times = templ_len // LANES, corr_len // LANES
    tpl = lax.axis_index("tpl")
    for distance, segment_ref in enumerate(segment_refs):
        wave_ref[tpl ^ distance] = segment_ref[...]
    places = [(c * LANES // seg_len, c * LANES % seg_len) for c in range(blocks)]
    block = jnp.concatenate([wave_ref[g, :, at : at + LANES] for g, at in places], axis=0)
    before = jnp.concatenate([jnp.zeros((stations, LANES), jnp.float32), block[:-stations]], axis=0)
    filtered = jnp.dot(
        jnp.concatenate([before, block], axis=1),
        toeplitz_ref[...],
        precision=lax.Precision.HIGHEST,
        preferred_element_type=jnp.float32,
    )
    series = filtered.astype(jnp.bfloat16).astype(jnp.float32)
    series_ref[...] = series
    row = lax.broadcasted_iota(jnp.int32, (LANES, LANES), 0)
    lane = lax.broadcasted_iota(jnp.int32, (LANES, LANES), 1)
    one = jnp.ones((LANES, LANES), jnp.float32)
    sums_of_ref[...] = jnp.concatenate(
        [jnp.where(row <= lane, one, 0.0), jnp.where(row > lane, one, 0.0), one], axis=1
    ).astype(jnp.bfloat16)
    squares = series * series
    high = squares.astype(jnp.bfloat16)
    low = (squares - high.astype(jnp.float32)).astype(jnp.bfloat16)
    sums_ref[...] = jnp.dot(high, sums_of_ref[...], preferred_element_type=jnp.float32) + jnp.dot(
        low, sums_of_ref[...], preferred_element_type=jnp.float32
    )

    def sums(c, kind):
        return sums_ref[c * stations : (c + 1) * stations, kind * LANES : (kind + 1) * LANES]

    for t in range(times):
        energy = sums(t, 0) + sums(t + lags, 1)
        for c in range(t + 1, t + lags):
            energy = energy + sums(c, 2)
        at = (times - 1 - t) * LANES
        inverse_ref[:, at : at + LANES] = lax.rsqrt(energy)
    for s in range(stations):
        whole = jnp.concatenate(
            [series_ref[c * stations + s : c * stations + s + 1, :] for c in reversed(range(blocks))], axis=1
        )
        ahead = pltpu.roll(
            jnp.broadcast_to(whole, (LANES, blocks * LANES)), 0, 1, stride=1, stride_axis=0
        )
        for c in range(1, blocks):
            hankel_ref[s, :, c * LANES : (c + 1) * LANES] = ahead[:, c * LANES : (c + 1) * LANES].astype(jnp.bfloat16)
    stack_half(1 - (lax.axis_index("sta") & 1), rows_ref, used_ref, shift_ref, hankel_ref, inverse_ref, send_ref)


def keep_kernel(rows_ref, used_ref, shift_ref, hankel_ref, inverse_ref, keep_ref):
    stack_half(lax.axis_index("sta") & 1, rows_ref, used_ref, shift_ref, hankel_ref, inverse_ref, keep_ref)


def flip(value, axis, mask):
    return lax.ppermute(value, axis, [(i, i ^ mask) for i in range(lax.axis_size(axis))])


def shards(waveform, fir_taps, templates, presence, moveout):
    block_rows, stations, templ_len = templates.shape
    owners, segments = lax.axis_size("sta"), lax.axis_size("tpl")
    sta = lax.axis_index("sta")
    samples = segments * waveform.shape[1]
    corr_len = samples - templ_len
    out_len = corr_len - SHIFT_MOST
    owned = block_rows // owners
    half_rows = block_rows // 2
    vmem = pl.BlockSpec(memory_space=pltpu.VMEM)
    options = dict(
        compiler_params=pltpu.CompilerParams(vmem_limit_bytes=16 * 1024 * 1024),
        cost_estimate=pl.CostEstimate(flops=1 << 20, bytes_accessed=1 << 20, transcendentals=0),
    )
    rows = templates.transpose(1, 0, 2).reshape(stations, owners // 2, 2, owned, templ_len)
    own, toeplitz, used, shift = pl.pallas_call(
        functools.partial(columns_kernel, owners),
        out_shape=(
            jax.ShapeDtypeStruct(waveform.shape, jnp.float32),
            jax.ShapeDtypeStruct((PAIR, LANES), jnp.float32),
            jax.ShapeDtypeStruct((stations, 2, half_rows, LANES), jnp.float32),
            jax.ShapeDtypeStruct((stations, 2, half_rows, LANES), jnp.int32),
        ),
        in_specs=[vmem] * 4,
        out_specs=(vmem,) * 4,
        scratch_shapes=[pltpu.VMEM((8, LANES), jnp.float32)],
        name="columns",
        **options,
    )(waveform, fir_taps[None, :], presence.T, moveout.T)
    sent = {0: waveform}
    bit = segments // 2
    while bit >= 1:
        mask = bit | 1
        for d, piece in list(sent.items()):
            sent[d ^ mask] = flip(piece, "tpl", mask)
        if bit == segments // 2:
            sent[mask], rows = lax.optimization_barrier((sent[mask], rows))
        bit //= 2
    sent[0] = own
    send, hankel, inverse = pl.pallas_call(
        send_kernel,
        out_shape=(
            jax.ShapeDtypeStruct((owners // 2, owned, out_len), jnp.bfloat16),
            jax.ShapeDtypeStruct((stations, LANES, samples), jnp.bfloat16),
            jax.ShapeDtypeStruct((stations, corr_len), jnp.float32),
        ),
        in_specs=[vmem] * (segments + 4),
        out_specs=(vmem,) * 3,
        scratch_shapes=[
            pltpu.VMEM((segments,) + waveform.shape, jnp.float32),
            pltpu.VMEM((samples // LANES * stations, LANES), jnp.float32),
            pltpu.VMEM((LANES, 3 * LANES), jnp.bfloat16),
            pltpu.VMEM((samples // LANES * stations, 3 * LANES), jnp.float32),
        ],
        name="send_half",
        **options,
    )(*[sent[d] for d in range(segments)], toeplitz, rows, used, shift)
    stack = pl.pallas_call(
        keep_kernel,
        out_shape=jax.ShapeDtypeStruct((owners // 2, owned, out_len), jnp.float32),
        in_specs=[vmem] * 5,
        out_specs=vmem,
        name="keep_half",
        **options,
    )(rows, used, shift, hankel, inverse)
    bit = 1
    while True:
        stack = stack + flip(send, "sta", bit).astype(jnp.float32)
        bit *= 2
        if bit >= owners:
            break
        pairs = stack.reshape(stack.shape[0] // 2, 2, owned, out_len)
        side = (sta // bit) % 2
        stack = lax.dynamic_index_in_dim(pairs, side, 1, keepdims=False)
        send = lax.dynamic_index_in_dim(pairs, 1 - side, 1, keepdims=False).astype(jnp.bfloat16)
    return stack


def solution(mesh):
    placed = (P("sta", "tpl"), P(), P("tpl", "sta", None), P("tpl", "sta"), P("tpl", "sta"))
    return jax.shard_map(
        shards, mesh=mesh, in_specs=placed, out_specs=P("tpl", "sta", None), check_vma=False
    )
```

time: 906 us -> 20.1 us (0.02)
  local copies, waits for them, and re-layouts: 802 us -> 1.87 us
  waiting for transfers between devices: 62.8 us -> 5.26 us
  matrix products: 17.5 us -> 0 us
  between operations: 13.7 us -> 0.07 us
  starting transfers between devices: 0.01 us -> 10.2 us
    gather x3 -> x0, local copies, waits for them, and re-layouts: 787 us -> none  [shards(): aligned = jnp.take_along_axis(correlation, positions, axis=2)]
    reduce_scatter x1 -> x0, waiting for transfers between devices: 62.7 us -> none  [shards(): lax.psum_scatter(jnp.sum(weights[:, :, None] * aligned, axis=0), 'sta', s...]
    conv_general_dilated x1 -> x0, matrix products: 15.2 us -> none  [fir_apply(): lax.conv_general_dilated(extended[:, None, :], coeffs[::-1][None, None, :...]
    ppermute x0 -> x6, starting transfers between devices: none -> 10.2 us  [flip(): lax.ppermute(value, axis, [(i, i ^ mask) for i in range(lax.axis_size(axi...]
  transfers between devices with their start and end apart: 1 -> 6, of which waited for: 1 -> 3; matrix products, arithmetic and copies ran while one was open for 0% -> 6% of each run, Pallas kernels for 0% -> 4%
where the time goes in v3:
time: 20.1 us; the launch traced here: 19.9 us
  starting transfers between devices  10.2 us (51%)
  waiting for transfers between devices  5.26 us (26%)
  local copies, waits for them, and re-layouts  1.87 us (9%)
  Pallas kernels  1.84 us (9%)
  other arithmetic  0.63 us (3%)
    ppermute x6, starting transfers between devices, flip(): lax.ppermute(value, axis, [(i, i ^ mask) for i in range(lax.axis_size(axi...  10.2 us
    ppermute x6, waiting for transfers between devices, flip(): lax.ppermute(value, axis, [(i, i ^ mask) for i in range(lax.axis_size(axi...  5.26 us
    transpose x1, local copies, waits for them, and re-layouts, shards(): templates.transpose(1, 0, 2)  1.16 us
    pallas_call x1, Pallas kernels, shards(): pl.pallas_call(send_kernel, out_shape=(jax.ShapeDtypeStruct((owners // 2,...  0.98 us
    unnamed x8, local copies, waits for them, and re-layouts  0.68 us
    add x3, other arithmetic, shards(): stack = stack + flip(send, 'sta', bit).astype(jnp.float32)  0.63 us
    pallas_call x1, Pallas kernels, shards(): pl.pallas_call(keep_kernel, out_shape=jax.ShapeDtypeStruct((owners // 2,...  0.58 us
  transfers between devices with their start and end apart: 6, of which 3 were waited for; matrix products, arithmetic and copies ran while one was open for 6% of the time, Pallas kernels for 4%

profile of v3, /device:TPU:0, one launch (start us, length us, event | category | flops | bytes accessed | tf_op | source)
XLA Modules:
  0.0 19.9 jit_solution(17088454407035398500)
XLA Ops:
  0.0 2.4 %collective-permute-start = (f32[2,384]{1,0:T(2,128)}, f32[2,384]{1,0:T(2,128)S(1)}, u32[]{:S(2)}, u32[]{:S(2)}) collective-permute-start(f32[2,384]{1,0:T(2,128)} %wave_in.1), channel_id=1, source_target_pairs={{0,3},{1,2},{2,1},{3,0},{4,7},{5,6},{6,5},{7,4},{8,11},{9,10},{10,... | collective-permute-start | bytes 9224 | tf_op jit(solution)/shard_map/ppermute | solution.py:143
  2.4 0.7 %collective-permute-start.1 = (f32[2,384]{1,0:T(2,128)}, f32[2,384]{1,0:T(2,128)S(1)}, u32[]{:S(2)}, u32[]{:S(2)}) collective-permute-start(f32[2,384]{1,0:T(2,128)} %wave_in.1), channel_id=1, source_target_pairs={{0,1},{1,0},{2,3},{3,2},{4,5},{5,4},{6,7},{7,6},{8,9},{9,8},{10,11... | collective-permute-start | bytes 9224 | tf_op jit(solution)/shard_map/ppermute | solution.py:143
  3.1 0.0 copy-start.2
  3.1 1.2 %copy.6 = bf16[2,128,1024]{2,1,0:T(8,128)(2,1)S(1)} copy(bf16[2,128,1024]{2,0,1:T(2,128)(2,1)} %bitcast.19) | data formatting | bytes 1048576 | tf_op jit(solution)/shard_map/transpose | solution.py:160
  4.2 0.0 collective-permute-done.refs_3_
  4.2 0.0 copy-start
  4.2 0.3 %collective-permute-start.2 = (f32[2,384]{1,0:T(2,128)S(1)}, f32[2,384]{1,0:T(2,128)S(1)}, u32[]{:S(2)}, u32[]{:S(2)}) collective-permute-start(f32[2,384]{1,0:T(2,128)S(1)} %collective-permute-done.refs_3_), channel_id=1, source_target_pairs={{0,1},{1,0},{2,3},{3,2},{4,5},{5,4},{6,7},{7,6},{8,9},{9,8},{10,11... | collective-permute-start | bytes 9224 | tf_op jit(solution)/shard_map/ppermute | solution.py:143
  4.5 0.0 copy-start.1
  4.6 0.0 copy-done.2
  4.6 0.4 %copy-done = f32[2,384]{1,0:T(2,128)S(1)} copy-done((f32[2,384]{1,0:T(2,128)S(1)}, f32[2,384]{1,0:T(2,128)}, u32[]{:S(2)}) %copy-start) | copy-done | bytes 3096
  4.9 0.3 %copy-done.1 = s32[128,2]{0,1:T(2,128)S(1)} copy-done((s32[128,2]{0,1:T(2,128)S(1)}, s32[128,2]{0,1:T(2,128)}, u32[]{:S(2)}) %copy-start.1) | copy-done | bytes 1048
  5.2 0.0 copy-done.3
  5.2 0.3 %columns.1 = (f32[2,384]{1,0:T(2,128)S(1)}, f32[256,128]{1,0:T(8,128)S(1)}, f32[2,2,64,128]{3,2,1,0:T(8,128)S(1)}, s32[2,2,64,128]{3,2,1,0:T(8,128)S(1)}) custom-call(f32[2,384]{1,0:T(2,128)S(1)} %copy-done, f32[1,64]{1,0:T(1,128)S(1)} %bitcast.18, s32[2,128]{1,0:T(2,128)S(1)} %bitcast.16, s32[2,128]{1,0:T(2,128)S(1)} %bitcast.17), custom_call_target="tpu_custom_call" | custom-call | flops 1048576 | bytes 1048576 | tf_op jit(solution)/shard_map/columns/pallas_call | solution.py:161
  5.5 0.0 collective-permute-done.1.refs_1_
  5.5 0.0 collective-permute-done.2.refs_2_
  5.5 1.0 %send_half.1 = (bf16[4,16,384]{2,1,0:T(8,128)(2,1)S(1)}, bf16[2,128,1536]{2,1,0:T(8,128)(2,1)S(1)}, f32[2,512]{1,0:T(2,128)S(1)}) custom-call(f32[2,384]{1,0:T(2,128)S(1)} %get-tuple-element.17.refs_0_, f32[2,384]{1,0:T(2,128)S(1)} %collective-permute-done.1.refs_1_, f32[2,384]{1,0:T(2,128)S(1)} %collective-permute-done.2.refs_2_, ...), custom_call_target="tpu_custom_call" | custom-call | flops 1048576 | bytes 1048576 | tf_op jit(solution)/shard_map/send_half/pallas_call | solution.py:185
  6.5 1.9 %collective-permute-start.3 = (bf16[4,16,384]{2,1,0:T(8,128)(2,1)S(1)}, bf16[4,16,384]{2,1,0:T(8,128)(2,1)S(1)}, u32[]{:S(2)}, u32[]{:S(2)}) collective-permute-start(bf16[4,16,384]{2,1,0:T(8,128)(2,1)S(1)} %get-tuple-element.22), channel_id=1, source_target_pairs={{0,4},{4,0},{8,12},{12,8},{16,20},{20,16},{24,28},{28,24},{1,5},{5... | collective-permute-start | bytes 147464 | tf_op jit(solution)/shard_map/ppermute | solution.py:143
  8.4 0.6 %keep_half.1 = f32[4,16,384]{2,1,0:T(8,128)S(1)} custom-call(bf16[2,4,2,16,1024]{4,3,2,1,0:T(8,128)(2,1)S(1)} %bitcast.15, f32[2,2,64,128]{3,2,1,0:T(8,128)S(1)} %get-tuple-element.15.refs_6_.used_ref, s32[2,2,64,128]{3,2,1,0:T(8,128)S(1)} %get-tuple-element.16.refs_7_.shift_ref, bf16[2,128,1536]{2,1,0:T(8,128)(2,1)S(1)} %get-tuple-element.20.hankel_ref, ...), custom_call_target="tpu_custom_call" | custom-call | flops 1048576 | bytes 1048576 | tf_op jit(solution)/shard_map/keep_half/pallas_call | solution.py:203
  9.0 1.7 %collective-permute-done.3 = bf16[4,16,384]{2,1,0:T(8,128)(2,1)S(1)} collective-permute-done((bf16[4,16,384]{2,1,0:T(8,128)(2,1)S(1)}, bf16[4,16,384]{2,1,0:T(8,128)(2,1)S(1)}, u32[]{:S(2)}, u32[]{:S(2)}) %collective-permute-start.3) | collective-permute-done | bytes 49184 | tf_op jit(solution)/shard_map/ppermute | solution.py:143
  10.7 2.0 %collective-permute-start.4 = (bf16[2,16,384]{2,1,0:T(8,128)(2,1)S(1)}, bf16[2,16,384]{2,1,0:T(8,128)(2,1)S(1)}, u32[]{:S(2)}, u32[]{:S(2)}) collective-permute-start(bf16[2,16,384]{2,1,0:T(8,128)(2,1)S(1)} %fusion), channel_id=1, source_target_pairs={{0,8},{4,12},{8,0},{12,4},{16,24},{20,28},{24,16},{28,20},{1,9},{5... | collective-permute-start | bytes 73736 | tf_op jit(solution)/shard_map/ppermute | solution.py:143
  12.7 1.9 %collective-permute-done.4 = bf16[2,16,384]{2,1,0:T(8,128)(2,1)S(1)} collective-permute-done((bf16[2,16,384]{2,1,0:T(8,128)(2,1)S(1)}, bf16[2,16,384]{2,1,0:T(8,128)(2,1)S(1)}, u32[]{:S(2)}, u32[]{:S(2)}) %collective-permute-start.4) | collective-permute-done | bytes 24608 | tf_op jit(solution)/shard_map/ppermute | solution.py:143
  14.6 3.0 %collective-permute-start.5 = (bf16[1,16,384]{2,1,0:T(8,128)(2,1)S(1)}, bf16[1,16,384]{2,1,0:T(8,128)(2,1)S(1)}, u32[]{:S(2)}, u32[]{:S(2)}) collective-permute-start(bf16[1,16,384]{2,1,0:T(8,128)(2,1)S(1)} %dynamic-slice_convert_fusion), channel_id=1, source_target_pairs={{0,16},{4,20},{8,24},{12,28},{16,0},{20,4},{24,8},{28,12},{1,17},{... | collective-permute-start | bytes 36872 | tf_op jit(solution)/shard_map/ppermute | solution.py:143
  17.6 1.7 %collective-permute-done.5 = bf16[1,16,384]{2,1,0:T(8,128)(2,1)S(1)} collective-permute-done((bf16[1,16,384]{2,1,0:T(8,128)(2,1)S(1)}, bf16[1,16,384]{2,1,0:T(8,128)(2,1)S(1)}, u32[]{:S(2)}, u32[]{:S(2)}) %collective-permute-start.5) | collective-permute-done | bytes 12320 | tf_op jit(solution)/shard_map/ppermute | solution.py:143
  19.3 0.6 %convert_add_fusion.1 = f32[1,16,384]{2,1,0:T(8,128)} fusion(bf16[1,16,384]{2,1,0:T(8,128)(2,1)S(1)} %collective-permute-done.5, f32[2,16,384]{2,1,0:T(8,128)S(1)} %bitcast_add_fusion, s32[]{:T(128)S(6)} %select_n.38), kind=kLoop, calls=%fused_computation.4 | loop fusion | flops 12288 | bytes 61444 | tf_op jit(solution)/shard_map/add | solution.py:213
  (5 shorter events, 0.0 us)
Async XLA Ops:
  0.0 4.2 %collective-permute-start = (f32[2,384]{1,0:T(2,128)}, f32[2,384]{1,0:T(2,128)S(1)}, u32[]{:S(2)}, u32[]{:S(2)}) collective-permute-start(f32[2,384]{1,0:T(2,128)} %wave_in.1), channel_id=1, source_target_pairs={{0,3},{1,2},{2,1},{3,0},{4,7},{5,6},{6,5},{7,4},{8,11},{9,10},{10,... | collective-permute-start | bytes 9224 | tf_op jit(solution)/shard_map/ppermute | solution.py:143
  2.4 3.1 %collective-permute-start.1 = (f32[2,384]{1,0:T(2,128)}, f32[2,384]{1,0:T(2,128)S(1)}, u32[]{:S(2)}, u32[]{:S(2)}) collective-permute-start(f32[2,384]{1,0:T(2,128)} %wave_in.1), channel_id=1, source_target_pairs={{0,1},{1,0},{2,3},{3,2},{4,5},{5,4},{6,7},{7,6},{8,9},{9,8},{10,11... | collective-permute-start | bytes 9224 | tf_op jit(solution)/shard_map/ppermute | solution.py:143
  3.1 1.5 %copy-start.2 = (s32[128,2]{0,1:T(2,128)S(1)}, s32[128,2]{0,1:T(2,128)}, u32[]{:S(2)}) copy-start(s32[128,2]{0,1:T(2,128)} %param.9) | copy-start | bytes 3076
  4.2 0.7 %copy-start = (f32[2,384]{1,0:T(2,128)S(1)}, f32[2,384]{1,0:T(2,128)}, u32[]{:S(2)}) copy-start(f32[2,384]{1,0:T(2,128)} %wave_in.1) | copy-start | bytes 9220
  4.2 1.3 %collective-permute-start.2 = (f32[2,384]{1,0:T(2,128)S(1)}, f32[2,384]{1,0:T(2,128)S(1)}, u32[]{:S(2)}, u32[]{:S(2)}) collective-permute-start(f32[2,384]{1,0:T(2,128)S(1)} %collective-permute-done.refs_3_), channel_id=1, source_target_pairs={{0,1},{1,0},{2,3},{3,2},{4,5},{5,4},{6,7},{7,6},{8,9},{9,8},{10,11... | collective-permute-start | bytes 9224 | tf_op jit(solution)/shard_map/ppermute | solution.py:143
  4.5 0.7 %copy-start.1 = (s32[128,2]{0,1:T(2,128)S(1)}, s32[128,2]{0,1:T(2,128)}, u32[]{:S(2)}) copy-start(s32[128,2]{0,1:T(2,128)} %param.8) | copy-start | bytes 3076
  4.5 0.7 %copy-start.3 = (f32[64]{0:T(128)S(1)}, f32[64]{0:T(128)}, u32[]{:S(2)}) copy-start(f32[64]{0:T(128)} %param.6) | copy-start | bytes 772
  6.5 4.2 %collective-permute-start.3 = (bf16[4,16,384]{2,1,0:T(8,128)(2,1)S(1)}, bf16[4,16,384]{2,1,0:T(8,128)(2,1)S(1)}, u32[]{:S(2)}, u32[]{:S(2)}) collective-permute-start(bf16[4,16,384]{2,1,0:T(8,128)(2,1)S(1)} %get-tuple-element.22), channel_id=1, source_target_pairs={{0,4},{4,0},{8,12},{12,8},{16,20},{20,16},{24,28},{28,24},{1,5},{5... | collective-permute-start | bytes 147464 | tf_op jit(solution)/shard_map/ppermute | solution.py:143
  10.7 3.9 %collective-permute-start.4 = (bf16[2,16,384]{2,1,0:T(8,128)(2,1)S(1)}, bf16[2,16,384]{2,1,0:T(8,128)(2,1)S(1)}, u32[]{:S(2)}, u32[]{:S(2)}) collective-permute-start(bf16[2,16,384]{2,1,0:T(8,128)(2,1)S(1)} %fusion), channel_id=1, source_target_pairs={{0,8},{4,12},{8,0},{12,4},{16,24},{20,28},{24,16},{28,20},{1,9},{5... | collective-permute-start | bytes 73736 | tf_op jit(solution)/shard_map/ppermute | solution.py:143
  14.6 4.7 %collective-permute-start.5 = (bf16[1,16,384]{2,1,0:T(8,128)(2,1)S(1)}, bf16[1,16,384]{2,1,0:T(8,128)(2,1)S(1)}, u32[]{:S(2)}, u32[]{:S(2)}) collective-permute-start(bf16[1,16,384]{2,1,0:T(8,128)(2,1)S(1)} %dynamic-slice_convert_fusion), channel_id=1, source_target_pairs={{0,16},{4,20},{8,24},{12,28},{16,0},{20,4},{24,8},{28,12},{1,17},{... | collective-permute-start | bytes 36872 | tf_op jit(solution)/shard_map/ppermute | solution.py:143

commit v4 on v3

--- a/solution.py
+++ b/solution.py
@@ -22,8 +22,8 @@
 
 
 def columns_kernel(owners, wave_in, taps_in, presence_ref, moveout_ref, wave_ref, toeplitz_ref, used_ref, shift_ref, row_ref):
-    stations, _, half_rows, _ = used_ref.shape
-    owned = half_rows * 2 // owners
+    stations, parts, part_rows, _ = used_ref.shape
+    owned = part_rows * parts // owners
     taps = taps_in.shape[1]
     wave_ref[...] = wave_in[...]
     row_ref[...] = jnp.zeros_like(row_ref)
@@ -33,9 +33,9 @@
     tap = PAIR - 1 - lane - sample
     picked = lane_gather(jnp.broadcast_to(row_ref[0:1, :], (PAIR, LANES)), tap & (LANES - 1))
     toeplitz_ref[...] = jnp.where((tap >= 0) & (tap < taps), picked, 0.0)
-    place = lax.broadcasted_iota(jnp.int32, (LANES, half_rows * 2), 1)
-    half, rest = place // half_rows, place % half_rows
-    old = (rest // owned * 2 + half) * owned + rest % owned
+    place = lax.broadcasted_iota(jnp.int32, (LANES, part_rows * parts), 1)
+    part, rest = place // part_rows, place % part_rows
+    old = (rest // owned * parts + part) * owned + rest % owned
     for s in range(stations):
         shift = lane_gather(jnp.broadcast_to(moveout_ref[s : s + 1, :], old.shape), old)
         shift_ref[s] = shift.T.reshape(shift_ref.shape[1:])
@@ -43,15 +43,16 @@
         used_ref[s] = used.astype(jnp.float32).T.reshape(used_ref.shape[1:])
 
 
-def stack_half(half, rows_ref, used_ref, shift_ref, hankel_ref, inverse_ref, out_ref):
+def stack_parts(parts, rows_ref, used_ref, shift_ref, hankel_ref, inverse_ref, out_refs):
     stations, groups, _, owned, templ_len = rows_ref.shape
-    half_rows = groups * owned
+    part_rows = groups * owned
+    all_rows = len(parts) * part_rows
     corr_len = inverse_ref.shape[1]
-    out_len = out_ref.shape[2]
+    out_len = out_refs[0].shape[2]
     lag_pairs, time_pairs = templ_len // PAIR, corr_len // PAIR
     total = None
     for s in range(stations):
-        rows = rows_ref[s, :, half].reshape(half_rows, templ_len)
+        rows = jnp.concatenate([rows_ref[s, :, p].reshape(part_rows, templ_len) for p in parts], axis=0)
         raw = [None] * time_pairs
         for offset in range(1, lag_pairs + time_pairs):
             uses = [(j, offset - lag_pairs + j) for j in range(lag_pairs) if 0 <= offset - lag_pairs + j < time_pairs]
@@ -62,26 +63,28 @@
             left = jnp.concatenate([rows[:, j * PAIR : (j + 1) * PAIR] for j, _ in uses], axis=0)
             product = jnp.dot(left, window, preferred_element_type=jnp.float32)
             for k, (_, t) in enumerate(uses):
-                part = product[k * half_rows : (k + 1) * half_rows]
+                part = product[k * all_rows : (k + 1) * all_rows]
                 raw[t] = part if raw[t] is None else raw[t] + part
         correlation = jnp.concatenate(raw, axis=1) * inverse_ref[s : s + 1, :]
         wide = rows.astype(jnp.float32)
         norm = lax.rsqrt(jnp.sum(wide * wide, axis=1, keepdims=True) + epsilon)
-        shift = shift_ref[s, half]
+        shift = jnp.concatenate([shift_ref[s, p] for p in parts], axis=0)
         place = PAIR - 1 - lax.broadcasted_iota(jnp.int32, shift.shape, 1) - shift
         index, later = place & (LANES - 1), place >= LANES
         moved = [lane_gather(correlation[:, at : at + LANES], index) for at in range(0, corr_len, LANES)]
         last = corr_len // LANES - 1
-        scale = norm * used_ref[s, half]
+        scale = norm * jnp.concatenate([used_ref[s, p] for p in parts], axis=0)
         aligned = [scale * jnp.where(later, moved[last - c], moved[last - 1 - c]) for c in range(out_len // LANES)]
         total = aligned if total is None else [a + b for a, b in zip(total, aligned)]
-    for c, part in enumerate(total):
-        out_ref[:, :, c * LANES : (c + 1) * LANES] = part.astype(out_ref.dtype).reshape(groups, owned, LANES)
-
-
-def send_kernel(*refs):
-    *segment_refs, toeplitz_ref, rows_ref, used_ref, shift_ref = refs[:-7]
-    send_ref, hankel_ref, inverse_ref, wave_ref, series_ref, sums_of_ref, sums_ref = refs[-7:]
+    for k, out_ref in enumerate(out_refs):
+        for c, part in enumerate(total):
+            piece = part[k * part_rows : (k + 1) * part_rows].astype(out_ref.dtype)
+            out_ref[:, :, c * LANES : (c + 1) * LANES] = piece.reshape(groups, owned, LANES)
+
+
+def send_kernel(segments, *refs):
+    segment_refs, (toeplitz_ref, rows_ref, used_ref, shift_ref, *send_refs) = refs[:segments], refs[segments:-6]
+    hankel_ref, inverse_ref, wave_ref, series_ref, sums_of_ref, sums_ref = refs[-6:]
     stations, templ_len = rows_ref.shape[0], rows_ref.shape[-1]
     corr_len = inverse_ref.shape[1]
     seg_len = segment_refs[0].shape[1]
@@ -132,11 +135,14 @@
         )
         for c in range(1, blocks):
             hankel_ref[s, :, c * LANES : (c + 1) * LANES] = ahead[:, c * LANES : (c + 1) * LANES].astype(jnp.bfloat16)
-    stack_half(1 - (lax.axis_index("sta") & 1), rows_ref, used_ref, shift_ref, hankel_ref, inverse_ref, send_ref)
+    me = lax.axis_index("sta") & len(send_refs)
+    parts = [me ^ distance for distance in range(1, len(send_refs) + 1)]
+    stack_parts(parts, rows_ref, used_ref, shift_ref, hankel_ref, inverse_ref, send_refs)
 
 
 def keep_kernel(rows_ref, used_ref, shift_ref, hankel_ref, inverse_ref, keep_ref):
-    stack_half(lax.axis_index("sta") & 1, rows_ref, used_ref, shift_ref, hankel_ref, inverse_ref, keep_ref)
+    me = lax.axis_index("sta") & (rows_ref.shape[2] - 1)
+    stack_parts([me], rows_ref, used_ref, shift_ref, hankel_ref, inverse_ref, [keep_ref])
 
 
 def flip(value, axis, mask):
@@ -151,20 +157,21 @@
     corr_len = samples - templ_len
     out_len = corr_len - SHIFT_MOST
     owned = block_rows // owners
-    half_rows = block_rows // 2
+    parts = min(owners, 4)
+    part_rows = block_rows // parts
     vmem = pl.BlockSpec(memory_space=pltpu.VMEM)
     options = dict(
         compiler_params=pltpu.CompilerParams(vmem_limit_bytes=16 * 1024 * 1024),
         cost_estimate=pl.CostEstimate(flops=1 << 20, bytes_accessed=1 << 20, transcendentals=0),
     )
-    rows = templates.transpose(1, 0, 2).reshape(stations, owners // 2, 2, owned, templ_len)
+    rows = templates.transpose(1, 0, 2).reshape(stations, owners // parts, parts, owned, templ_len)
     own, toeplitz, used, shift = pl.pallas_call(
         functools.partial(columns_kernel, owners),
         out_shape=(
             jax.ShapeDtypeStruct(waveform.shape, jnp.float32),
             jax.ShapeDtypeStruct((PAIR, LANES), jnp.float32),
-            jax.ShapeDtypeStruct((stations, 2, half_rows, LANES), jnp.float32),
-            jax.ShapeDtypeStruct((stations, 2, half_rows, LANES), jnp.int32),
+            jax.ShapeDtypeStruct((stations, parts, part_rows, LANES), jnp.float32),
+            jax.ShapeDtypeStruct((stations, parts, part_rows, LANES), jnp.int32),
         ),
         in_specs=[vmem] * 4,
         out_specs=(vmem,) * 4,
@@ -182,42 +189,42 @@
             sent[mask], rows = lax.optimization_barrier((sent[mask], rows))
         bit //= 2
     sent[0] = own
-    send, hankel, inverse = pl.pallas_call(
-        send_kernel,
+    *send, hankel, inverse = pl.pallas_call(
+        functools.partial(send_kernel, segments),
         out_shape=(
-            jax.ShapeDtypeStruct((owners // 2, owned, out_len), jnp.bfloat16),
+            *[jax.ShapeDtypeStruct((owners // parts, owned, out_len), jnp.bfloat16)] * (parts - 1),
             jax.ShapeDtypeStruct((stations, LANES, samples), jnp.bfloat16),
             jax.ShapeDtypeStruct((stations, corr_len), jnp.float32),
         ),
         in_specs=[vmem] * (segments + 4),
-        out_specs=(vmem,) * 3,
+        out_specs=(vmem,) * (parts + 1),
         scratch_shapes=[
             pltpu.VMEM((segments,) + waveform.shape, jnp.float32),
             pltpu.VMEM((samples // LANES * stations, LANES), jnp.float32),
             pltpu.VMEM((LANES, 3 * LANES), jnp.bfloat16),
             pltpu.VMEM((samples // LANES * stations, 3 * LANES), jnp.float32),
         ],
-        name="send_half",
+        name="send_parts",
         **options,
     )(*[sent[d] for d in range(segments)], toeplitz, rows, used, shift)
     stack = pl.pallas_call(
         keep_kernel,
-        out_shape=jax.ShapeDtypeStruct((owners // 2, owned, out_len), jnp.float32),
+        out_shape=jax.ShapeDtypeStruct((owners // parts, owned, out_len), jnp.float32),
         in_specs=[vmem] * 5,
         out_specs=vmem,
-        name="keep_half",
+        name="keep_part",
         **options,
     )(rows, used, shift, hankel, inverse)
-    bit = 1
-    while True:
-        stack = stack + flip(send, "sta", bit).astype(jnp.float32)
-        bit *= 2
-        if bit >= owners:
-            break
+    for distance in range(1, parts):
+        stack = stack + flip(send[distance - 1], "sta", distance).astype(jnp.float32)
+    bit = parts
+    while bit < owners:
         pairs = stack.reshape(stack.shape[0] // 2, 2, owned, out_len)
         side = (sta // bit) % 2
         stack = lax.dynamic_index_in_dim(pairs, side, 1, keepdims=False)
-        send = lax.dynamic_index_in_dim(pairs, 1 - side, 1, keepdims=False).astype(jnp.bfloat16)
+        other = lax.dynamic_index_in_dim(pairs, 1 - side, 1, keepdims=False).astype(jnp.bfloat16)
+        stack = stack + flip(other, "sta", bit).astype(jnp.float32)
+        bit *= 2
     return stack
 
 

time: 20.1 us -> 19.3 us (0.960)
  starting transfers between devices: 10.2 us -> 9.57 us
    ppermute x6 -> x7, starting transfers between devices: 10.2 us -> 9.57 us  [flip(): lax.ppermute(value, axis, [(i, i ^ mask) for i in range(lax.axis_size(axi...]
    ppermute x6 -> x7, waiting for transfers between devices: 5.26 us -> 5.17 us  [flip(): lax.ppermute(value, axis, [(i, i ^ mask) for i in range(lax.axis_size(axi...]
    add x3 -> x2, other arithmetic: 0.63 us -> 0.63 us  [the longest x1 0.61 us: shards(): stack = stack + flip(other, 'sta', bit).astype(jnp.float32)]
  transfers between devices with their start and end apart: 6 -> 7, of which waited for: 3 -> 4; matrix products, arithmetic and copies ran while one was open for 6% -> 6% of each run, Pallas kernels for 4% -> 4%
where the time goes in v4:
time: 19.3 us; the launch traced here: 19.2 us
  starting transfers between devices  9.57 us (50%)
  waiting for transfers between devices  5.17 us (27%)
  local copies, waits for them, and re-layouts  1.86 us (10%)
  Pallas kernels  1.86 us (10%)
  other arithmetic  0.63 us (3%)
    ppermute x7, starting transfers between devices, flip(): lax.ppermute(value, axis, [(i, i ^ mask) for i in range(lax.axis_size(axi...  9.57 us
    ppermute x7, waiting for transfers between devices, flip(): lax.ppermute(value, axis, [(i, i ^ mask) for i in range(lax.axis_size(axi...  5.17 us
    transpose x1, local copies, waits for them, and re-layouts, shards(): templates.transpose(1, 0, 2)  1.16 us
    pallas_call x1, Pallas kernels, shards(): pl.pallas_call(functools.partial(send_kernel, segments), out_shape=(*[jax...  1.12 us
    unnamed x8, local copies, waits for them, and re-layouts  0.68 us
    add x1, other arithmetic, shards(): stack = stack + flip(other, 'sta', bit).astype(jnp.float32)  0.61 us
    pallas_call x1, Pallas kernels, shards(): pl.pallas_call(keep_kernel, out_shape=jax.ShapeDtypeStruct((owners // par...  0.47 us
  transfers between devices with their start and end apart: 7, of which 4 were waited for; matrix products, arithmetic and copies ran while one was open for 6% of the time, Pallas kernels for 4%

profile of v4, /device:TPU:0, one launch (start us, length us, event | category | flops | bytes accessed | tf_op | source)
XLA Modules:
  0.0 19.2 jit_solution(3539612105597340990)
XLA Ops:
  0.0 2.4 %collective-permute-start = (f32[2,384]{1,0:T(2,128)}, f32[2,384]{1,0:T(2,128)S(1)}, u32[]{:S(2)}, u32[]{:S(2)}) collective-permute-start(f32[2,384]{1,0:T(2,128)} %wave_in.1), channel_id=1, source_target_pairs={{0,3},{1,2},{2,1},{3,0},{4,7},{5,6},{6,5},{7,4},{8,11},{9,10},{10,... | collective-permute-start | bytes 9224 | tf_op jit(solution)/shard_map/ppermute | solution.py:149
  2.4 0.7 %collective-permute-start.1 = (f32[2,384]{1,0:T(2,128)}, f32[2,384]{1,0:T(2,128)S(1)}, u32[]{:S(2)}, u32[]{:S(2)}) collective-permute-start(f32[2,384]{1,0:T(2,128)} %wave_in.1), channel_id=1, source_target_pairs={{0,1},{1,0},{2,3},{3,2},{4,5},{5,4},{6,7},{7,6},{8,9},{9,8},{10,11... | collective-permute-start | bytes 9224 | tf_op jit(solution)/shard_map/ppermute | solution.py:149
  3.1 1.2 %copy.6 = bf16[2,128,1024]{2,1,0:T(8,128)(2,1)S(1)} copy(bf16[2,128,1024]{2,0,1:T(2,128)(2,1)} %bitcast.10) | data formatting | bytes 1048576 | tf_op jit(solution)/shard_map/transpose | solution.py:167
  4.2 0.0 collective-permute-done.refs_3_
  4.2 0.0 copy-start
  4.2 0.3 %collective-permute-start.2 = (f32[2,384]{1,0:T(2,128)S(1)}, f32[2,384]{1,0:T(2,128)S(1)}, u32[]{:S(2)}, u32[]{:S(2)}) collective-permute-start(f32[2,384]{1,0:T(2,128)S(1)} %collective-permute-done.refs_3_), channel_id=1, source_target_pairs={{0,1},{1,0},{2,3},{3,2},{4,5},{5,4},{6,7},{7,6},{8,9},{9,8},{10,11... | collective-permute-start | bytes 9224 | tf_op jit(solution)/shard_map/ppermute | solution.py:149
  4.6 0.0 copy-done.2
  4.6 0.4 %copy-done = f32[2,384]{1,0:T(2,128)S(1)} copy-done((f32[2,384]{1,0:T(2,128)S(1)}, f32[2,384]{1,0:T(2,128)}, u32[]{:S(2)}) %copy-start) | copy-done | bytes 3096
  4.9 0.3 %copy-done.1 = s32[128,2]{0,1:T(2,128)S(1)} copy-done((s32[128,2]{0,1:T(2,128)S(1)}, s32[128,2]{0,1:T(2,128)}, u32[]{:S(2)}) %copy-start.1) | copy-done | bytes 1048
  5.2 0.0 copy-done.3
  5.2 0.3 %columns.1 = (f32[2,384]{1,0:T(2,128)S(1)}, f32[256,128]{1,0:T(8,128)S(1)}, f32[2,4,32,128]{3,2,1,0:T(8,128)S(1)}, s32[2,4,32,128]{3,2,1,0:T(8,128)S(1)}) custom-call(f32[2,384]{1,0:T(2,128)S(1)} %copy-done, f32[1,64]{1,0:T(1,128)S(1)} %bitcast.9, s32[2,128]{1,0:T(2,128)S(1)} %bitcast.7, s32[2,128]{1,0:T(2,128)S(1)} %bitcast.8), custom_call_target="tpu_custom_call" | custom-call | flops 1048576 | bytes 1048576 | tf_op jit(solution)/shard_map/columns/pallas_call | solution.py:168
  5.5 0.0 collective-permute-done.1.refs_1_
  5.5 0.0 collective-permute-done.2.refs_2_
  5.5 1.1 %send_parts.1 = (bf16[2,16,384]{2,1,0:T(8,128)(2,1)S(1)}, bf16[2,16,384]{2,1,0:T(8,128)(2,1)S(1)}, bf16[2,16,384]{2,1,0:T(8,128)(2,1)S(1)}, bf16[2,128,1536]{2,1,0:T(8,128)(2,1)S(1)}, f32[2,512]{1,0:T(2,128)S(1)}) custom-call(f32[2,384]{1,0:T(2,128)S(1)} %get-tuple-element.19.refs_0_, f32[2,384]{1,0:T(2,128)S(1)} %collective-permute-done.1.refs_1_, ...), custom_call_target="tpu_custom_call" | custom-call | flops 1048576 | bytes 1048576 | tf_op jit(solution)/shard_map/send_parts/pallas_call | solution.py:192
  6.6 2.9 %collective-permute-start.5 = (bf16[2,16,384]{2,1,0:T(8,128)(2,1)S(1)}, bf16[2,16,384]{2,1,0:T(8,128)(2,1)S(1)}, u32[]{:S(2)}, u32[]{:S(2)}) collective-permute-start(bf16[2,16,384]{2,1,0:T(8,128)(2,1)S(1)} %get-tuple-element.26), channel_id=1, source_target_pairs={{0,12},{4,8},{8,4},{12,0},{16,28},{20,24},{24,20},{28,16},{1,13},{... | collective-permute-start | bytes 73736 | tf_op jit(solution)/shard_map/ppermute | solution.py:149
  9.6 0.4 %collective-permute-start.4 = (bf16[2,16,384]{2,1,0:T(8,128)(2,1)S(1)}, bf16[2,16,384]{2,1,0:T(8,128)(2,1)S(1)}, u32[]{:S(2)}, u32[]{:S(2)}) collective-permute-start(bf16[2,16,384]{2,1,0:T(8,128)(2,1)S(1)} %get-tuple-element.25), channel_id=1, source_target_pairs={{0,8},{4,12},{8,0},{12,4},{16,24},{20,28},{24,16},{28,20},{1,9},{5... | collective-permute-start | bytes 73736 | tf_op jit(solution)/shard_map/ppermute | solution.py:149
  10.0 0.2 %collective-permute-start.3 = (bf16[2,16,384]{2,1,0:T(8,128)(2,1)S(1)}, bf16[2,16,384]{2,1,0:T(8,128)(2,1)S(1)}, u32[]{:S(2)}, u32[]{:S(2)}) collective-permute-start(bf16[2,16,384]{2,1,0:T(8,128)(2,1)S(1)} %get-tuple-element.24), channel_id=1, source_target_pairs={{0,4},{4,0},{8,12},{12,8},{16,20},{20,16},{24,28},{28,24},{1,5},{5... | collective-permute-start | bytes 73736 | tf_op jit(solution)/shard_map/ppermute | solution.py:149
  10.2 0.5 %keep_part.1 = f32[2,16,384]{2,1,0:T(8,128)S(1)} custom-call(bf16[2,2,4,16,1024]{4,3,2,1,0:T(8,128)(2,1)S(1)} %bitcast.6, f32[2,4,32,128]{3,2,1,0:T(8,128)S(1)} %get-tuple-element.17.refs_6_.used_ref, s32[2,4,32,128]{3,2,1,0:T(8,128)S(1)} %get-tuple-element.18.refs_7_.shift_ref, bf16[2,128,1536]{2,1,0:T(8,128)(2,1)S(1)} %get-tuple-element.22.hankel_ref, ...), custom_call_target="tpu_custom_call" | custom-call | flops 1048576 | bytes 1048576 | tf_op jit(solution)/shard_map/keep_part/pallas_call | solution.py:210
  10.7 0.7 %collective-permute-done.5 = bf16[2,16,384]{2,1,0:T(8,128)(2,1)S(1)} collective-permute-done((bf16[2,16,384]{2,1,0:T(8,128)(2,1)S(1)}, bf16[2,16,384]{2,1,0:T(8,128)(2,1)S(1)}, u32[]{:S(2)}, u32[]{:S(2)}) %collective-permute-start.5) | collective-permute-done | bytes 24608 | tf_op jit(solution)/shard_map/ppermute | solution.py:149
  11.4 2.0 %collective-permute-done.4 = bf16[2,16,384]{2,1,0:T(8,128)(2,1)S(1)} collective-permute-done((bf16[2,16,384]{2,1,0:T(8,128)(2,1)S(1)}, bf16[2,16,384]{2,1,0:T(8,128)(2,1)S(1)}, u32[]{:S(2)}, u32[]{:S(2)}) %collective-permute-start.4) | collective-permute-done | bytes 24608 | tf_op jit(solution)/shard_map/ppermute | solution.py:149
  13.4 0.4 %collective-permute-done.3 = bf16[2,16,384]{2,1,0:T(8,128)(2,1)S(1)} collective-permute-done((bf16[2,16,384]{2,1,0:T(8,128)(2,1)S(1)}, bf16[2,16,384]{2,1,0:T(8,128)(2,1)S(1)}, u32[]{:S(2)}, u32[]{:S(2)}) %collective-permute-start.3) | collective-permute-done | bytes 24608 | tf_op jit(solution)/shard_map/ppermute | solution.py:149
  13.9 2.7 %collective-permute-start.6 = (bf16[1,16,384]{2,1,0:T(8,128)(2,1)S(1)}, bf16[1,16,384]{2,1,0:T(8,128)(2,1)S(1)}, u32[]{:S(2)}, u32[]{:S(2)}) collective-permute-start(bf16[1,16,384]{2,1,0:T(8,128)(2,1)S(1)} %dynamic-slice_convert_fusion), channel_id=1, source_target_pairs={{0,16},{4,20},{8,24},{12,28},{16,0},{20,4},{24,8},{28,12},{1,17},{... | collective-permute-start | bytes 36872 | tf_op jit(solution)/shard_map/ppermute | solution.py:149
  16.5 2.0 %collective-permute-done.6 = bf16[1,16,384]{2,1,0:T(8,128)(2,1)S(1)} collective-permute-done((bf16[1,16,384]{2,1,0:T(8,128)(2,1)S(1)}, bf16[1,16,384]{2,1,0:T(8,128)(2,1)S(1)}, u32[]{:S(2)}, u32[]{:S(2)}) %collective-permute-start.6) | collective-permute-done | bytes 12320 | tf_op jit(solution)/shard_map/ppermute | solution.py:149
  18.5 0.6 %convert_add_fusion.1 = f32[1,16,384]{2,1,0:T(8,128)} fusion(bf16[1,16,384]{2,1,0:T(8,128)(2,1)S(1)} %collective-permute-done.6, f32[2,16,384]{2,1,0:T(8,128)S(1)} %convert_add_fusion, s32[]{:T(128)S(6)} %select_n.20), kind=kLoop, calls=%fused_computation.1 | loop fusion | flops 12288 | bytes 61444 | tf_op jit(solution)/shard_map/add | solution.py:226
  (5 shorter events, 0.0 us)
Async XLA Ops:
  0.0 4.2 %collective-permute-start = (f32[2,384]{1,0:T(2,128)}, f32[2,384]{1,0:T(2,128)S(1)}, u32[]{:S(2)}, u32[]{:S(2)}) collective-permute-start(f32[2,384]{1,0:T(2,128)} %wave_in.1), channel_id=1, source_target_pairs={{0,3},{1,2},{2,1},{3,0},{4,7},{5,6},{6,5},{7,4},{8,11},{9,10},{10,... | collective-permute-start | bytes 9224 | tf_op jit(solution)/shard_map/ppermute | solution.py:149
  2.4 3.1 %collective-permute-start.1 = (f32[2,384]{1,0:T(2,128)}, f32[2,384]{1,0:T(2,128)S(1)}, u32[]{:S(2)}, u32[]{:S(2)}) collective-permute-start(f32[2,384]{1,0:T(2,128)} %wave_in.1), channel_id=1, source_target_pairs={{0,1},{1,0},{2,3},{3,2},{4,5},{5,4},{6,7},{7,6},{8,9},{9,8},{10,11... | collective-permute-start | bytes 9224 | tf_op jit(solution)/shard_map/ppermute | solution.py:149
  3.1 1.5 %copy-start.2 = (s32[128,2]{0,1:T(2,128)S(1)}, s32[128,2]{0,1:T(2,128)}, u32[]{:S(2)}) copy-start(s32[128,2]{0,1:T(2,128)} %param.9) | copy-start | bytes 3076
  4.2 0.7 %copy-start = (f32[2,384]{1,0:T(2,128)S(1)}, f32[2,384]{1,0:T(2,128)}, u32[]{:S(2)}) copy-start(f32[2,384]{1,0:T(2,128)} %wave_in.1) | copy-start | bytes 9220
  4.2 1.3 %collective-permute-start.2 = (f32[2,384]{1,0:T(2,128)S(1)}, f32[2,384]{1,0:T(2,128)S(1)}, u32[]{:S(2)}, u32[]{:S(2)}) collective-permute-start(f32[2,384]{1,0:T(2,128)S(1)} %collective-permute-done.refs_3_), channel_id=1, source_target_pairs={{0,1},{1,0},{2,3},{3,2},{4,5},{5,4},{6,7},{7,6},{8,9},{9,8},{10,11... | collective-permute-start | bytes 9224 | tf_op jit(solution)/shard_map/ppermute | solution.py:149
  4.5 0.7 %copy-start.1 = (s32[128,2]{0,1:T(2,128)S(1)}, s32[128,2]{0,1:T(2,128)}, u32[]{:S(2)}) copy-start(s32[128,2]{0,1:T(2,128)} %param.8) | copy-start | bytes 3076
  4.5 0.7 %copy-start.3 = (f32[64]{0:T(128)S(1)}, f32[64]{0:T(128)}, u32[]{:S(2)}) copy-start(f32[64]{0:T(128)} %param.6) | copy-start | bytes 772
  6.6 4.8 %collective-permute-start.5 = (bf16[2,16,384]{2,1,0:T(8,128)(2,1)S(1)}, bf16[2,16,384]{2,1,0:T(8,128)(2,1)S(1)}, u32[]{:S(2)}, u32[]{:S(2)}) collective-permute-start(bf16[2,16,384]{2,1,0:T(8,128)(2,1)S(1)} %get-tuple-element.26), channel_id=1, source_target_pairs={{0,12},{4,8},{8,4},{12,0},{16,28},{20,24},{24,20},{28,16},{1,13},{... | collective-permute-start | bytes 73736 | tf_op jit(solution)/shard_map/ppermute | solution.py:149
  9.6 3.8 %collective-permute-start.4 = (bf16[2,16,384]{2,1,0:T(8,128)(2,1)S(1)}, bf16[2,16,384]{2,1,0:T(8,128)(2,1)S(1)}, u32[]{:S(2)}, u32[]{:S(2)}) collective-permute-start(bf16[2,16,384]{2,1,0:T(8,128)(2,1)S(1)} %get-tuple-element.25), channel_id=1, source_target_pairs={{0,8},{4,12},{8,0},{12,4},{16,24},{20,28},{24,16},{28,20},{1,9},{5... | collective-permute-start | bytes 73736 | tf_op jit(solution)/shard_map/ppermute | solution.py:149
  10.0 3.8 %collective-permute-start.3 = (bf16[2,16,384]{2,1,0:T(8,128)(2,1)S(1)}, bf16[2,16,384]{2,1,0:T(8,128)(2,1)S(1)}, u32[]{:S(2)}, u32[]{:S(2)}) collective-permute-start(bf16[2,16,384]{2,1,0:T(8,128)(2,1)S(1)} %get-tuple-element.24), channel_id=1, source_target_pairs={{0,4},{4,0},{8,12},{12,8},{16,20},{20,16},{24,28},{28,24},{1,5},{5... | collective-permute-start | bytes 73736 | tf_op jit(solution)/shard_map/ppermute | solution.py:149
  13.9 4.7 %collective-permute-start.6 = (bf16[1,16,384]{2,1,0:T(8,128)(2,1)S(1)}, bf16[1,16,384]{2,1,0:T(8,128)(2,1)S(1)}, u32[]{:S(2)}, u32[]{:S(2)}) collective-permute-start(bf16[1,16,384]{2,1,0:T(8,128)(2,1)S(1)} %dynamic-slice_convert_fusion), channel_id=1, source_target_pairs={{0,16},{4,20},{8,24},{12,28},{16,0},{20,4},{24,8},{28,12},{1,17},{... | collective-permute-start | bytes 36872 | tf_op jit(solution)/shard_map/ppermute | solution.py:149

commit v5 on v4

--- a/solution.py
+++ b/solution.py
@@ -69,12 +69,16 @@
         wide = rows.astype(jnp.float32)
         norm = lax.rsqrt(jnp.sum(wide * wide, axis=1, keepdims=True) + epsilon)
         shift = jnp.concatenate([shift_ref[s, p] for p in parts], axis=0)
-        place = PAIR - 1 - lax.broadcasted_iota(jnp.int32, shift.shape, 1) - shift
-        index, later = place & (LANES - 1), place >= LANES
-        moved = [lane_gather(correlation[:, at : at + LANES], index) for at in range(0, corr_len, LANES)]
+        lane = lax.broadcasted_iota(jnp.int32, shift.shape, 1)
+        index = (PAIR - 1 - lane - shift) & (LANES - 1)
+        later = lane + shift < LANES
+        columns = [correlation[:, at : at + LANES] for at in range(0, corr_len, LANES)]
         last = corr_len // LANES - 1
         scale = norm * jnp.concatenate([used_ref[s, p] for p in parts], axis=0)
-        aligned = [scale * jnp.where(later, moved[last - c], moved[last - 1 - c]) for c in range(out_len // LANES)]
+        aligned = [
+            scale * lane_gather(jnp.where(later, columns[last - c], columns[last - 1 - c]), index)
+            for c in range(out_len // LANES)
+        ]
         total = aligned if total is None else [a + b for a, b in zip(total, aligned)]
     for k, out_ref in enumerate(out_refs):
         for c, part in enumerate(total):

time: 19.3 us -> 19.2 us (level)
  no operation moved by 1% of the time
where the time goes in v5:
time: 19.2 us; the launch traced here: 19.1 us
  starting transfers between devices  9.57 us (50%)
  waiting for transfers between devices  5.2 us (27%)
  local copies, waits for them, and re-layouts  1.86 us (10%)
  Pallas kernels  1.74 us (9%)
  other arithmetic  0.63 us (3%)
    ppermute x7, starting transfers between devices, flip(): lax.ppermute(value, axis, [(i, i ^ mask) for i in range(lax.axis_size(axi...  9.57 us
    ppermute x7, waiting for transfers between devices, flip(): lax.ppermute(value, axis, [(i, i ^ mask) for i in range(lax.axis_size(axi...  5.2 us
    transpose x1, local copies, waits for them, and re-layouts, shards(): templates.transpose(1, 0, 2)  1.16 us
    pallas_call x1, Pallas kernels, shards(): pl.pallas_call(functools.partial(send_kernel, segments), out_shape=(*[jax...  1.04 us
    unnamed x8, local copies, waits for them, and re-layouts  0.68 us
    add x1, other arithmetic, shards(): stack = stack + flip(other, 'sta', bit).astype(jnp.float32)  0.61 us
    pallas_call x1, Pallas kernels, shards(): pl.pallas_call(keep_kernel, out_shape=jax.ShapeDtypeStruct((owners // par...  0.44 us
  transfers between devices with their start and end apart: 7, of which 4 were waited for; matrix products, arithmetic and copies ran while one was open for 6% of the time, Pallas kernels for 4%

profile of v5, /device:TPU:0, one launch (start us, length us, event | category | flops | bytes accessed | tf_op | source)
XLA Modules:
  0.0 19.1 jit_solution(1726361375830453549)
XLA Ops:
  0.0 2.4 %collective-permute-start = (f32[2,384]{1,0:T(2,128)}, f32[2,384]{1,0:T(2,128)S(1)}, u32[]{:S(2)}, u32[]{:S(2)}) collective-permute-start(f32[2,384]{1,0:T(2,128)} %wave_in.1), channel_id=1, source_target_pairs={{0,3},{1,2},{2,1},{3,0},{4,7},{5,6},{6,5},{7,4},{8,11},{9,10},{10,... | collective-permute-start | bytes 9224 | tf_op jit(solution)/shard_map/ppermute | solution.py:153
  2.4 0.7 %collective-permute-start.1 = (f32[2,384]{1,0:T(2,128)}, f32[2,384]{1,0:T(2,128)S(1)}, u32[]{:S(2)}, u32[]{:S(2)}) collective-permute-start(f32[2,384]{1,0:T(2,128)} %wave_in.1), channel_id=1, source_target_pairs={{0,1},{1,0},{2,3},{3,2},{4,5},{5,4},{6,7},{7,6},{8,9},{9,8},{10,11... | collective-permute-start | bytes 9224 | tf_op jit(solution)/shard_map/ppermute | solution.py:153
  3.1 1.2 %copy.6 = bf16[2,128,1024]{2,1,0:T(8,128)(2,1)S(1)} copy(bf16[2,128,1024]{2,0,1:T(2,128)(2,1)} %bitcast.10) | data formatting | bytes 1048576 | tf_op jit(solution)/shard_map/transpose | solution.py:171
  4.2 0.0 collective-permute-done.refs_3_
  4.2 0.0 copy-start
  4.2 0.3 %collective-permute-start.2 = (f32[2,384]{1,0:T(2,128)S(1)}, f32[2,384]{1,0:T(2,128)S(1)}, u32[]{:S(2)}, u32[]{:S(2)}) collective-permute-start(f32[2,384]{1,0:T(2,128)S(1)} %collective-permute-done.refs_3_), channel_id=1, source_target_pairs={{0,1},{1,0},{2,3},{3,2},{4,5},{5,4},{6,7},{7,6},{8,9},{9,8},{10,11... | collective-permute-start | bytes 9224 | tf_op jit(solution)/shard_map/ppermute | solution.py:153
  4.6 0.0 copy-done.2
  4.6 0.4 %copy-done = f32[2,384]{1,0:T(2,128)S(1)} copy-done((f32[2,384]{1,0:T(2,128)S(1)}, f32[2,384]{1,0:T(2,128)}, u32[]{:S(2)}) %copy-start) | copy-done | bytes 3096
  4.9 0.3 %copy-done.1 = s32[128,2]{0,1:T(2,128)S(1)} copy-done((s32[128,2]{0,1:T(2,128)S(1)}, s32[128,2]{0,1:T(2,128)}, u32[]{:S(2)}) %copy-start.1) | copy-done | bytes 1048
  5.2 0.0 copy-done.3
  5.2 0.3 %columns.1 = (f32[2,384]{1,0:T(2,128)S(1)}, f32[256,128]{1,0:T(8,128)S(1)}, f32[2,4,32,128]{3,2,1,0:T(8,128)S(1)}, s32[2,4,32,128]{3,2,1,0:T(8,128)S(1)}) custom-call(f32[2,384]{1,0:T(2,128)S(1)} %copy-done, f32[1,64]{1,0:T(1,128)S(1)} %bitcast.9, s32[2,128]{1,0:T(2,128)S(1)} %bitcast.7, s32[2,128]{1,0:T(2,128)S(1)} %bitcast.8), custom_call_target="tpu_custom_call" | custom-call | flops 1048576 | bytes 1048576 | tf_op jit(solution)/shard_map/columns/pallas_call | solution.py:172
  5.5 0.0 collective-permute-done.1.refs_1_
  5.5 0.0 collective-permute-done.2.refs_2_
  5.5 1.0 %send_parts.1 = (bf16[2,16,384]{2,1,0:T(8,128)(2,1)S(1)}, bf16[2,16,384]{2,1,0:T(8,128)(2,1)S(1)}, bf16[2,16,384]{2,1,0:T(8,128)(2,1)S(1)}, bf16[2,128,1536]{2,1,0:T(8,128)(2,1)S(1)}, f32[2,512]{1,0:T(2,128)S(1)}) custom-call(f32[2,384]{1,0:T(2,128)S(1)} %get-tuple-element.19.refs_0_, f32[2,384]{1,0:T(2,128)S(1)} %collective-permute-done.1.refs_1_, ...), custom_call_target="tpu_custom_call" | custom-call | flops 1048576 | bytes 1048576 | tf_op jit(solution)/shard_map/send_parts/pallas_call | solution.py:196
  6.6 2.9 %collective-permute-start.5 = (bf16[2,16,384]{2,1,0:T(8,128)(2,1)S(1)}, bf16[2,16,384]{2,1,0:T(8,128)(2,1)S(1)}, u32[]{:S(2)}, u32[]{:S(2)}) collective-permute-start(bf16[2,16,384]{2,1,0:T(8,128)(2,1)S(1)} %get-tuple-element.26), channel_id=1, source_target_pairs={{0,12},{4,8},{8,4},{12,0},{16,28},{20,24},{24,20},{28,16},{1,13},{... | collective-permute-start | bytes 73736 | tf_op jit(solution)/shard_map/ppermute | solution.py:153
  9.5 0.4 %collective-permute-start.4 = (bf16[2,16,384]{2,1,0:T(8,128)(2,1)S(1)}, bf16[2,16,384]{2,1,0:T(8,128)(2,1)S(1)}, u32[]{:S(2)}, u32[]{:S(2)}) collective-permute-start(bf16[2,16,384]{2,1,0:T(8,128)(2,1)S(1)} %get-tuple-element.25), channel_id=1, source_target_pairs={{0,8},{4,12},{8,0},{12,4},{16,24},{20,28},{24,16},{28,20},{1,9},{5... | collective-permute-start | bytes 73736 | tf_op jit(solution)/shard_map/ppermute | solution.py:153
  9.9 0.2 %collective-permute-start.3 = (bf16[2,16,384]{2,1,0:T(8,128)(2,1)S(1)}, bf16[2,16,384]{2,1,0:T(8,128)(2,1)S(1)}, u32[]{:S(2)}, u32[]{:S(2)}) collective-permute-start(bf16[2,16,384]{2,1,0:T(8,128)(2,1)S(1)} %get-tuple-element.24), channel_id=1, source_target_pairs={{0,4},{4,0},{8,12},{12,8},{16,20},{20,16},{24,28},{28,24},{1,5},{5... | collective-permute-start | bytes 73736 | tf_op jit(solution)/shard_map/ppermute | solution.py:153
  10.1 0.4 %keep_part.1 = f32[2,16,384]{2,1,0:T(8,128)S(1)} custom-call(bf16[2,2,4,16,1024]{4,3,2,1,0:T(8,128)(2,1)S(1)} %bitcast.6, f32[2,4,32,128]{3,2,1,0:T(8,128)S(1)} %get-tuple-element.17.refs_6_.used_ref, s32[2,4,32,128]{3,2,1,0:T(8,128)S(1)} %get-tuple-element.18.refs_7_.shift_ref, bf16[2,128,1536]{2,1,0:T(8,128)(2,1)S(1)} %get-tuple-element.22.hankel_ref, ...), custom_call_target="tpu_custom_call" | custom-call | flops 1048576 | bytes 1048576 | tf_op jit(solution)/shard_map/keep_part/pallas_call | solution.py:214
  10.6 0.8 %collective-permute-done.5 = bf16[2,16,384]{2,1,0:T(8,128)(2,1)S(1)} collective-permute-done((bf16[2,16,384]{2,1,0:T(8,128)(2,1)S(1)}, bf16[2,16,384]{2,1,0:T(8,128)(2,1)S(1)}, u32[]{:S(2)}, u32[]{:S(2)}) %collective-permute-start.5) | collective-permute-done | bytes 24608 | tf_op jit(solution)/shard_map/ppermute | solution.py:153
  11.3 2.0 %collective-permute-done.4 = bf16[2,16,384]{2,1,0:T(8,128)(2,1)S(1)} collective-permute-done((bf16[2,16,384]{2,1,0:T(8,128)(2,1)S(1)}, bf16[2,16,384]{2,1,0:T(8,128)(2,1)S(1)}, u32[]{:S(2)}, u32[]{:S(2)}) %collective-permute-start.4) | collective-permute-done | bytes 24608 | tf_op jit(solution)/shard_map/ppermute | solution.py:153
  13.3 0.4 %collective-permute-done.3 = bf16[2,16,384]{2,1,0:T(8,128)(2,1)S(1)} collective-permute-done((bf16[2,16,384]{2,1,0:T(8,128)(2,1)S(1)}, bf16[2,16,384]{2,1,0:T(8,128)(2,1)S(1)}, u32[]{:S(2)}, u32[]{:S(2)}) %collective-permute-start.3) | collective-permute-done | bytes 24608 | tf_op jit(solution)/shard_map/ppermute | solution.py:153
  13.8 2.7 %collective-permute-start.6 = (bf16[1,16,384]{2,1,0:T(8,128)(2,1)S(1)}, bf16[1,16,384]{2,1,0:T(8,128)(2,1)S(1)}, u32[]{:S(2)}, u32[]{:S(2)}) collective-permute-start(bf16[1,16,384]{2,1,0:T(8,128)(2,1)S(1)} %dynamic-slice_convert_fusion), channel_id=1, source_target_pairs={{0,16},{4,20},{8,24},{12,28},{16,0},{20,4},{24,8},{28,12},{1,17},{... | collective-permute-start | bytes 36872 | tf_op jit(solution)/shard_map/ppermute | solution.py:153
  16.4 2.0 %collective-permute-done.6 = bf16[1,16,384]{2,1,0:T(8,128)(2,1)S(1)} collective-permute-done((bf16[1,16,384]{2,1,0:T(8,128)(2,1)S(1)}, bf16[1,16,384]{2,1,0:T(8,128)(2,1)S(1)}, u32[]{:S(2)}, u32[]{:S(2)}) %collective-permute-start.6) | collective-permute-done | bytes 12320 | tf_op jit(solution)/shard_map/ppermute | solution.py:153
  18.4 0.6 %convert_add_fusion.1 = f32[1,16,384]{2,1,0:T(8,128)} fusion(bf16[1,16,384]{2,1,0:T(8,128)(2,1)S(1)} %collective-permute-done.6, f32[2,16,384]{2,1,0:T(8,128)S(1)} %convert_add_fusion, s32[]{:T(128)S(6)} %select_n.20), kind=kLoop, calls=%fused_computation.1 | loop fusion | flops 12288 | bytes 61444 | tf_op jit(solution)/shard_map/add | solution.py:230
  (5 shorter events, 0.0 us)
Async XLA Ops:
  0.0 4.2 %collective-permute-start = (f32[2,384]{1,0:T(2,128)}, f32[2,384]{1,0:T(2,128)S(1)}, u32[]{:S(2)}, u32[]{:S(2)}) collective-permute-start(f32[2,384]{1,0:T(2,128)} %wave_in.1), channel_id=1, source_target_pairs={{0,3},{1,2},{2,1},{3,0},{4,7},{5,6},{6,5},{7,4},{8,11},{9,10},{10,... | collective-permute-start | bytes 9224 | tf_op jit(solution)/shard_map/ppermute | solution.py:153
  2.4 3.1 %collective-permute-start.1 = (f32[2,384]{1,0:T(2,128)}, f32[2,384]{1,0:T(2,128)S(1)}, u32[]{:S(2)}, u32[]{:S(2)}) collective-permute-start(f32[2,384]{1,0:T(2,128)} %wave_in.1), channel_id=1, source_target_pairs={{0,1},{1,0},{2,3},{3,2},{4,5},{5,4},{6,7},{7,6},{8,9},{9,8},{10,11... | collective-permute-start | bytes 9224 | tf_op jit(solution)/shard_map/ppermute | solution.py:153
  3.1 1.5 %copy-start.2 = (s32[128,2]{0,1:T(2,128)S(1)}, s32[128,2]{0,1:T(2,128)}, u32[]{:S(2)}) copy-start(s32[128,2]{0,1:T(2,128)} %param.9) | copy-start | bytes 3076
  4.2 0.7 %copy-start = (f32[2,384]{1,0:T(2,128)S(1)}, f32[2,384]{1,0:T(2,128)}, u32[]{:S(2)}) copy-start(f32[2,384]{1,0:T(2,128)} %wave_in.1) | copy-start | bytes 9220
  4.2 1.3 %collective-permute-start.2 = (f32[2,384]{1,0:T(2,128)S(1)}, f32[2,384]{1,0:T(2,128)S(1)}, u32[]{:S(2)}, u32[]{:S(2)}) collective-permute-start(f32[2,384]{1,0:T(2,128)S(1)} %collective-permute-done.refs_3_), channel_id=1, source_target_pairs={{0,1},{1,0},{2,3},{3,2},{4,5},{5,4},{6,7},{7,6},{8,9},{9,8},{10,11... | collective-permute-start | bytes 9224 | tf_op jit(solution)/shard_map/ppermute | solution.py:153
  4.5 0.7 %copy-start.1 = (s32[128,2]{0,1:T(2,128)S(1)}, s32[128,2]{0,1:T(2,128)}, u32[]{:S(2)}) copy-start(s32[128,2]{0,1:T(2,128)} %param.8) | copy-start | bytes 3076
  4.5 0.7 %copy-start.3 = (f32[64]{0:T(128)S(1)}, f32[64]{0:T(128)}, u32[]{:S(2)}) copy-start(f32[64]{0:T(128)} %param.6) | copy-start | bytes 772
  6.6 4.8 %collective-permute-start.5 = (bf16[2,16,384]{2,1,0:T(8,128)(2,1)S(1)}, bf16[2,16,384]{2,1,0:T(8,128)(2,1)S(1)}, u32[]{:S(2)}, u32[]{:S(2)}) collective-permute-start(bf16[2,16,384]{2,1,0:T(8,128)(2,1)S(1)} %get-tuple-element.26), channel_id=1, source_target_pairs={{0,12},{4,8},{8,4},{12,0},{16,28},{20,24},{24,20},{28,16},{1,13},{... | collective-permute-start | bytes 73736 | tf_op jit(solution)/shard_map/ppermute | solution.py:153
  9.5 3.8 %collective-permute-start.4 = (bf16[2,16,384]{2,1,0:T(8,128)(2,1)S(1)}, bf16[2,16,384]{2,1,0:T(8,128)(2,1)S(1)}, u32[]{:S(2)}, u32[]{:S(2)}) collective-permute-start(bf16[2,16,384]{2,1,0:T(8,128)(2,1)S(1)} %get-tuple-element.25), channel_id=1, source_target_pairs={{0,8},{4,12},{8,0},{12,4},{16,24},{20,28},{24,16},{28,20},{1,9},{5... | collective-permute-start | bytes 73736 | tf_op jit(solution)/shard_map/ppermute | solution.py:153
  9.9 3.8 %collective-permute-start.3 = (bf16[2,16,384]{2,1,0:T(8,128)(2,1)S(1)}, bf16[2,16,384]{2,1,0:T(8,128)(2,1)S(1)}, u32[]{:S(2)}, u32[]{:S(2)}) collective-permute-start(bf16[2,16,384]{2,1,0:T(8,128)(2,1)S(1)} %get-tuple-element.24), channel_id=1, source_target_pairs={{0,4},{4,0},{8,12},{12,8},{16,20},{20,16},{24,28},{28,24},{1,5},{5... | collective-permute-start | bytes 73736 | tf_op jit(solution)/shard_map/ppermute | solution.py:153
  13.8 4.7 %collective-permute-start.6 = (bf16[1,16,384]{2,1,0:T(8,128)(2,1)S(1)}, bf16[1,16,384]{2,1,0:T(8,128)(2,1)S(1)}, u32[]{:S(2)}, u32[]{:S(2)}) collective-permute-start(bf16[1,16,384]{2,1,0:T(8,128)(2,1)S(1)} %dynamic-slice_convert_fusion), channel_id=1, source_target_pairs={{0,16},{4,20},{8,24},{12,28},{16,0},{20,4},{24,8},{28,12},{1,17},{... | collective-permute-start | bytes 36872 | tf_op jit(solution)/shard_map/ppermute | solution.py:153

commit v6 on v5

--- a/solution.py
+++ b/solution.py
@@ -149,8 +149,11 @@
     stack_parts([me], rows_ref, used_ref, shift_ref, hankel_ref, inverse_ref, [keep_ref])
 
 
-def flip(value, axis, mask):
-    return lax.ppermute(value, axis, [(i, i ^ mask) for i in range(lax.axis_size(axis))])
+def flip(value, sta_mask, tpl_mask):
+    across = lax.axis_size("tpl")
+    mask = sta_mask * across + tpl_mask
+    pairs = [(i, i ^ mask) for i in range(lax.axis_size("sta") * across)]
+    return lax.ppermute(value, ("sta", "tpl"), pairs)
 
 
 def shards(waveform, fir_taps, templates, presence, moveout):
@@ -188,7 +191,7 @@
     while bit >= 1:
         mask = bit | 1
         for d, piece in list(sent.items()):
-            sent[d ^ mask] = flip(piece, "tpl", mask)
+            sent[d ^ mask] = flip(piece, 0, mask)
         if bit == segments // 2:
             sent[mask], rows = lax.optimization_barrier((sent[mask], rows))
         bit //= 2
@@ -219,16 +222,28 @@
         name="keep_part",
         **options,
     )(rows, used, shift, hankel, inverse)
-    for distance in range(1, parts):
-        stack = stack + flip(send[distance - 1], "sta", distance).astype(jnp.float32)
-    bit = parts
-    while bit < owners:
-        pairs = stack.reshape(stack.shape[0] // 2, 2, owned, out_len)
-        side = (sta // bit) % 2
-        stack = lax.dynamic_index_in_dim(pairs, side, 1, keepdims=False)
-        other = lax.dynamic_index_in_dim(pairs, 1 - side, 1, keepdims=False).astype(jnp.bfloat16)
-        stack = stack + flip(other, "sta", bit).astype(jnp.float32)
-        bit *= 2
+    rounds = [parts]
+    while rounds[-1] < owners:
+        rounds.append(rounds[-1] * 2)
+    turns = len(rounds) // 2 * 2 if segments > 1 else 0
+    for number, reach in enumerate(rounds):
+        turn = 1 if number < turns else 0
+        if number == 0:
+            moved = [(distance, send[distance - 1]) for distance in range(1, parts)]
+        else:
+            bit = reach // 2
+            pairs = stack.reshape(stack.shape[0] // 2, 2, owned, out_len)
+            side = (sta // bit) % 2
+            stack = lax.dynamic_index_in_dim(pairs, side, 1, keepdims=False)
+            moved = [(bit, lax.dynamic_index_in_dim(pairs, 1 - side, 1, keepdims=False).astype(jnp.bfloat16))]
+        arrived = [flip(piece, distance, turn) for distance, piece in moved]
+        if turn:
+            if number == 0:
+                stack, _ = lax.optimization_barrier((stack, arrived[-1]))
+            pieces = [stack[:, :, at : at + LANES] for at in range(0, out_len, LANES)]
+            stack = jnp.concatenate([flip(piece, 0, turn) for piece in pieces], axis=2)
+        for piece in arrived:
+            stack = stack + piece.astype(jnp.float32)
     return stack
 
 

time: 19.2 us -> 18 us (0.938)
  waiting for transfers between devices: 5.2 us -> 2.9 us
  starting transfers between devices: 9.57 us -> 10.6 us
    ppermute x7 -> x13, waiting for transfers between devices: 5.2 us -> 2.9 us  [flip(): return lax.ppermute(value, ('sta', 'tpl'), pairs)]
    ppermute x7 -> x13, starting transfers between devices: 9.57 us -> 10.6 us  [flip(): return lax.ppermute(value, ('sta', 'tpl'), pairs)]
  transfers between devices with their start and end apart: 7 -> 13, of which waited for: 4 -> 6; matrix products, arithmetic and copies ran while one was open for 6% -> 7% of each run, Pallas kernels for 4% -> 4%
where the time goes in v6:
time: 18 us; the launch traced here: 17.9 us
  starting transfers between devices  10.6 us (59%)
  waiting for transfers between devices  2.9 us (16%)
  local copies, waits for them, and re-layouts  1.87 us (10%)
  Pallas kernels  1.76 us (10%)
  other arithmetic  0.63 us (4%)
    ppermute x13, starting transfers between devices, flip(): return lax.ppermute(value, ('sta', 'tpl'), pairs)  10.6 us
    ppermute x13, waiting for transfers between devices, flip(): return lax.ppermute(value, ('sta', 'tpl'), pairs)  2.9 us
    transpose x1, local copies, waits for them, and re-layouts, shards(): templates.transpose(1, 0, 2)  1.16 us
    pallas_call x1, Pallas kernels, shards(): pl.pallas_call(functools.partial(send_kernel, segments), out_shape=(*[jax...  1.05 us
    unnamed x8, local copies, waits for them, and re-layouts  0.68 us
    add x2, other arithmetic, shards(): stack = stack + piece.astype(jnp.float32)  0.63 us
    pallas_call x1, Pallas kernels, shards(): pl.pallas_call(keep_kernel, out_shape=jax.ShapeDtypeStruct((owners // par...  0.44 us
  transfers between devices with their start and end apart: 13, of which 6 were waited for; matrix products, arithmetic and copies ran while one was open for 7% of the time, Pallas kernels for 4%

profile of v6, /device:TPU:0, one launch (start us, length us, event | category | flops | bytes accessed | tf_op | source)
XLA Modules:
  0.0 17.9 jit_solution(501177486372979817)
XLA Ops:
  0.0 2.4 %collective-permute-start = (f32[2,384]{1,0:T(2,128)}, f32[2,384]{1,0:T(2,128)S(1)}, u32[]{:S(2)}, u32[]{:S(2)}) collective-permute-start(f32[2,384]{1,0:T(2,128)} %wave_in.1), channel_id=1, source_target_pairs={{0,3},{1,2},{2,1},{3,0},{4,7},{5,6},{6,5},{7,4},{8,11},{9,10},{10,... | collective-permute-start | bytes 9224 | tf_op jit(solution)/shard_map/ppermute | solution.py:156
  2.4 0.7 %collective-permute-start.1 = (f32[2,384]{1,0:T(2,128)}, f32[2,384]{1,0:T(2,128)S(1)}, u32[]{:S(2)}, u32[]{:S(2)}) collective-permute-start(f32[2,384]{1,0:T(2,128)} %wave_in.1), channel_id=1, source_target_pairs={{0,1},{1,0},{2,3},{3,2},{4,5},{5,4},{6,7},{7,6},{8,9},{9,8},{10,11... | collective-permute-start | bytes 9224 | tf_op jit(solution)/shard_map/ppermute | solution.py:156
  3.1 1.2 %copy.6 = bf16[2,128,1024]{2,1,0:T(8,128)(2,1)S(1)} copy(bf16[2,128,1024]{2,0,1:T(2,128)(2,1)} %bitcast.10) | data formatting | bytes 1048576 | tf_op jit(solution)/shard_map/transpose | solution.py:174
  4.3 0.3 %collective-permute-start.2 = (f32[2,384]{1,0:T(2,128)S(1)}, f32[2,384]{1,0:T(2,128)S(1)}, u32[]{:S(2)}, u32[]{:S(2)}) collective-permute-start(f32[2,384]{1,0:T(2,128)S(1)} %collective-permute-done.refs_3_), channel_id=1, source_target_pairs={{0,1},{1,0},{2,3},{3,2},{4,5},{5,4},{6,7},{7,6},{8,9},{9,8},{10,11... | collective-permute-start | bytes 9224 | tf_op jit(solution)/shard_map/ppermute | solution.py:156
  4.6 0.4 %copy-done = f32[2,384]{1,0:T(2,128)S(1)} copy-done((f32[2,384]{1,0:T(2,128)S(1)}, f32[2,384]{1,0:T(2,128)}, u32[]{:S(2)}) %copy-start) | copy-done | bytes 3096
  4.9 0.3 %copy-done.1 = s32[128,2]{0,1:T(2,128)S(1)} copy-done((s32[128,2]{0,1:T(2,128)S(1)}, s32[128,2]{0,1:T(2,128)}, u32[]{:S(2)}) %copy-start.1) | copy-done | bytes 1048
  5.2 0.3 %columns.1 = (f32[2,384]{1,0:T(2,128)S(1)}, f32[256,128]{1,0:T(8,128)S(1)}, f32[2,4,32,128]{3,2,1,0:T(8,128)S(1)}, s32[2,4,32,128]{3,2,1,0:T(8,128)S(1)}) custom-call(f32[2,384]{1,0:T(2,128)S(1)} %copy-done, f32[1,64]{1,0:T(1,128)S(1)} %bitcast.9, s32[2,128]{1,0:T(2,128)S(1)} %bitcast.7, s32[2,128]{1,0:T(2,128)S(1)} %bitcast.8), custom_call_target="tpu_custom_call" | custom-call | flops 1048576 | bytes 1048576 | tf_op jit(solution)/shard_map/columns/pallas_call | solution.py:175
  5.5 1.1 %send_parts.1 = (bf16[2,16,384]{2,1,0:T(8,128)(2,1)S(1)}, bf16[2,16,384]{2,1,0:T(8,128)(2,1)S(1)}, bf16[2,16,384]{2,1,0:T(8,128)(2,1)S(1)}, bf16[2,128,1536]{2,1,0:T(8,128)(2,1)S(1)}, f32[2,512]{1,0:T(2,128)S(1)}) custom-call(f32[2,384]{1,0:T(2,128)S(1)} %get-tuple-element.20.refs_0_, f32[2,384]{1,0:T(2,128)S(1)} %collective-permute-done.1.refs_1_, ...), custom_call_target="tpu_custom_call" | custom-call | flops 1048576 | bytes 1048576 | tf_op jit(solution)/shard_map/send_parts/pallas_call | solution.py:199
  6.6 2.8 %collective-permute-start.3 = (bf16[2,16,384]{2,1,0:T(8,128)(2,1)S(1)}, bf16[2,16,384]{2,1,0:T(8,128)(2,1)S(1)}, u32[]{:S(2)}, u32[]{:S(2)}) collective-permute-start(bf16[2,16,384]{2,1,0:T(8,128)(2,1)S(1)} %get-tuple-element.25), channel_id=1, source_target_pairs={{0,13},{1,12},{2,15},{3,14},{4,9},{5,8},{6,11},{7,10},{8,5},{9,4},... | collective-permute-start | bytes 73736 | tf_op jit(solution)/shard_map/ppermute | solution.py:156
  9.4 0.2 %collective-permute-start.8 = (bf16[2,16,384]{2,1,0:T(8,128)(2,1)S(1)}, bf16[2,16,384]{2,1,0:T(8,128)(2,1)S(1)}, u32[]{:S(2)}, u32[]{:S(2)}) collective-permute-start(bf16[2,16,384]{2,1,0:T(8,128)(2,1)S(1)} %get-tuple-element.28), channel_id=1, source_target_pairs={{0,9},{1,8},{2,11},{3,10},{4,13},{5,12},{6,15},{7,14},{8,1},{9,0},... | collective-permute-start | bytes 73736 | tf_op jit(solution)/shard_map/ppermute | solution.py:156
  9.7 0.2 %collective-permute-start.7 = (bf16[2,16,384]{2,1,0:T(8,128)(2,1)S(1)}, bf16[2,16,384]{2,1,0:T(8,128)(2,1)S(1)}, u32[]{:S(2)}, u32[]{:S(2)}) collective-permute-start(bf16[2,16,384]{2,1,0:T(8,128)(2,1)S(1)} %get-tuple-element.27), channel_id=1, source_target_pairs={{0,5},{1,4},{2,7},{3,6},{4,1},{5,0},{6,3},{7,2},{8,13},{9,12},{10,... | collective-permute-start | bytes 73736 | tf_op jit(solution)/shard_map/ppermute | solution.py:156
  9.9 0.4 %keep_part.1 = f32[2,16,384]{2,1,0:T(8,128)S(1)} custom-call(bf16[2,2,4,16,1024]{4,3,2,1,0:T(8,128)(2,1)S(1)} %bitcast.6, f32[2,4,32,128]{3,2,1,0:T(8,128)S(1)} %get-tuple-element.18.refs_6_.used_ref, s32[2,4,32,128]{3,2,1,0:T(8,128)S(1)} %get-tuple-element.19.refs_7_.shift_ref, bf16[2,128,1536]{2,1,0:T(8,128)(2,1)S(1)} %get-tuple-element.23.hankel_ref, ...), custom_call_target="tpu_custom_call" | custom-call | flops 1048576 | bytes 1048576 | tf_op jit(solution)/shard_map/keep_part/pallas_call | solution.py:217
  10.3 0.6 %collective-permute-done.3 = bf16[2,16,384]{2,1,0:T(8,128)(2,1)S(1)} collective-permute-done((bf16[2,16,384]{2,1,0:T(8,128)(2,1)S(1)}, bf16[2,16,384]{2,1,0:T(8,128)(2,1)S(1)}, u32[]{:S(2)}, u32[]{:S(2)}) %collective-permute-start.3) | collective-permute-done | bytes 24608 | tf_op jit(solution)/shard_map/ppermute | solution.py:156
  11.1 0.3 %collective-permute-start.5 = (f32[2,16,128]{2,1,0:T(8,128)S(1)}, f32[2,16,128]{2,1,0:T(8,128)S(1)}, u32[]{:S(2)}, u32[]{:S(2)}) collective-permute-start(f32[2,16,128]{2,1,0:T(8,128)S(1)} %get-tuple-element.34), channel_id=1, source_target_pairs={{0,1},{1,0},{2,3},{3,2},{4,5},{5,4},{6,7},{7,6},{8,9},{9,8},{10,11... | collective-permute-start | bytes 49160 | tf_op jit(solution)/shard_map/ppermute | solution.py:156
  11.6 1.0 %collective-permute-done.8 = bf16[2,16,384]{2,1,0:T(8,128)(2,1)S(1)} collective-permute-done((bf16[2,16,384]{2,1,0:T(8,128)(2,1)S(1)}, bf16[2,16,384]{2,1,0:T(8,128)(2,1)S(1)}, u32[]{:S(2)}, u32[]{:S(2)}) %collective-permute-start.8) | collective-permute-done | bytes 24608 | tf_op jit(solution)/shard_map/ppermute | solution.py:156
  12.7 0.2 %collective-permute-done.7 = bf16[2,16,384]{2,1,0:T(8,128)(2,1)S(1)} collective-permute-done((bf16[2,16,384]{2,1,0:T(8,128)(2,1)S(1)}, bf16[2,16,384]{2,1,0:T(8,128)(2,1)S(1)}, u32[]{:S(2)}, u32[]{:S(2)}) %collective-permute-start.7) | collective-permute-done | bytes 24608 | tf_op jit(solution)/shard_map/ppermute | solution.py:156
  13.0 2.6 %collective-permute-start.12 = (bf16[1,16,384]{2,1,0:T(8,128)(2,1)S(1)}, bf16[1,16,384]{2,1,0:T(8,128)(2,1)S(1)}, u32[]{:S(2)}, u32[]{:S(2)}) collective-permute-start(bf16[1,16,384]{2,1,0:T(8,128)(2,1)S(1)} %dynamic-slice_convert_fusion), channel_id=1, source_target_pairs={{0,17},{1,16},{2,19},{3,18},{4,21},{5,20},{6,23},{7,22},{8,25},{9,... | collective-permute-start | bytes 36872 | tf_op jit(solution)/shard_map/ppermute | solution.py:156
  15.6 0.2 %collective-permute-start.11 = (f32[1,16,128]{2,1,0:T(8,128)S(1)}, f32[1,16,128]{2,1,0:T(8,128)S(1)}, u32[]{:S(2)}, u32[]{:S(2)}) collective-permute-start(f32[1,16,128]{2,1,0:T(8,128)S(1)} %get-tuple-element.31), channel_id=1, source_target_pairs={{0,1},{1,0},{2,3},{3,2},{4,5},{5,4},{6,7},{7,6},{8,9},{9,8},{10,11... | collective-permute-start | bytes 24584 | tf_op jit(solution)/shard_map/ppermute | solution.py:156
  15.8 0.3 %collective-permute-start.10 = (f32[1,16,128]{2,1,0:T(8,128)S(1)}, f32[1,16,128]{2,1,0:T(8,128)S(1)}, u32[]{:S(2)}, u32[]{:S(2)}) collective-permute-start(f32[1,16,128]{2,1,0:T(8,128)S(1)} %get-tuple-element.30), channel_id=1, source_target_pairs={{0,1},{1,0},{2,3},{3,2},{4,5},{5,4},{6,7},{7,6},{8,9},{9,8},{10,11... | collective-permute-start | bytes 24584 | tf_op jit(solution)/shard_map/ppermute | solution.py:156
  16.1 0.2 %collective-permute-start.9 = (f32[1,16,128]{2,1,0:T(8,128)S(1)}, f32[1,16,128]{2,1,0:T(8,128)S(1)}, u32[]{:S(2)}, u32[]{:S(2)}) collective-permute-start(f32[1,16,128]{2,1,0:T(8,128)S(1)} %get-tuple-element.29), channel_id=1, source_target_pairs={{0,1},{1,0},{2,3},{3,2},{4,5},{5,4},{6,7},{7,6},{8,9},{9,8},{10,11... | collective-permute-start | bytes 24584 | tf_op jit(solution)/shard_map/ppermute | solution.py:156
  16.3 0.5 %collective-permute-done.11 = f32[1,16,128]{2,1,0:T(8,128)S(1)} collective-permute-done((f32[1,16,128]{2,1,0:T(8,128)S(1)}, f32[1,16,128]{2,1,0:T(8,128)S(1)}, u32[]{:S(2)}, u32[]{:S(2)}) %collective-permute-start.11) | collective-permute-done | bytes 8224 | tf_op jit(solution)/shard_map/ppermute | solution.py:156
  16.7 0.2 %collective-permute-done.10 = f32[1,16,128]{2,1,0:T(8,128)S(1)} collective-permute-done((f32[1,16,128]{2,1,0:T(8,128)S(1)}, f32[1,16,128]{2,1,0:T(8,128)S(1)}, u32[]{:S(2)}, u32[]{:S(2)}) %collective-permute-start.10) | collective-permute-done | bytes 8224 | tf_op jit(solution)/shard_map/ppermute | solution.py:156
  16.9 0.3 %collective-permute-done.9 = f32[1,16,128]{2,1,0:T(8,128)S(1)} collective-permute-done((f32[1,16,128]{2,1,0:T(8,128)S(1)}, f32[1,16,128]{2,1,0:T(8,128)S(1)}, u32[]{:S(2)}, u32[]{:S(2)}) %collective-permute-start.9) | collective-permute-done | bytes 8224 | tf_op jit(solution)/shard_map/ppermute | solution.py:156
  17.2 0.6 %maximum_add_fusion.1 = f32[1,16,384]{2,1,0:T(8,128)} fusion(f32[1,16,128]{2,1,0:T(8,128)S(1)} %collective-permute-done.11, f32[1,16,128]{2,1,0:T(8,128)S(1)} %collective-permute-done.10, f32[1,16,128]{2,1,0:T(8,128)S(1)} %collective-permute-done.9, bf16[1,16,384]{2,1,0:T(8,128)(2,1)S(1)} %collective-permute-done.12), kind=kLoop, calls=%fused_computation.3 | loop fusion | flops 24576 | bytes 61440 | tf_op jit(solution)/shard_map/add | solution.py:246
  (19 shorter events, 0.4 us)
Async XLA Ops:
  0.0 4.2 %collective-permute-start = (f32[2,384]{1,0:T(2,128)}, f32[2,384]{1,0:T(2,128)S(1)}, u32[]{:S(2)}, u32[]{:S(2)}) collective-permute-start(f32[2,384]{1,0:T(2,128)} %wave_in.1), channel_id=1, source_target_pairs={{0,3},{1,2},{2,1},{3,0},{4,7},{5,6},{6,5},{7,4},{8,11},{9,10},{10,... | collective-permute-start | bytes 9224 | tf_op jit(solution)/shard_map/ppermute | solution.py:156
  2.4 3.1 %collective-permute-start.1 = (f32[2,384]{1,0:T(2,128)}, f32[2,384]{1,0:T(2,128)S(1)}, u32[]{:S(2)}, u32[]{:S(2)}) collective-permute-start(f32[2,384]{1,0:T(2,128)} %wave_in.1), channel_id=1, source_target_pairs={{0,1},{1,0},{2,3},{3,2},{4,5},{5,4},{6,7},{7,6},{8,9},{9,8},{10,11... | collective-permute-start | bytes 9224 | tf_op jit(solution)/shard_map/ppermute | solution.py:156
  3.1 1.5 %copy-start.2 = (s32[128,2]{0,1:T(2,128)S(1)}, s32[128,2]{0,1:T(2,128)}, u32[]{:S(2)}) copy-start(s32[128,2]{0,1:T(2,128)} %param.9) | copy-start | bytes 3076
  4.2 0.7 %copy-start = (f32[2,384]{1,0:T(2,128)S(1)}, f32[2,384]{1,0:T(2,128)}, u32[]{:S(2)}) copy-start(f32[2,384]{1,0:T(2,128)} %wave_in.1) | copy-start | bytes 9220
  4.3 1.3 %collective-permute-start.2 = (f32[2,384]{1,0:T(2,128)S(1)}, f32[2,384]{1,0:T(2,128)S(1)}, u32[]{:S(2)}, u32[]{:S(2)}) collective-permute-start(f32[2,384]{1,0:T(2,128)S(1)} %collective-permute-done.refs_3_), channel_id=1, source_target_pairs={{0,1},{1,0},{2,3},{3,2},{4,5},{5,4},{6,7},{7,6},{8,9},{9,8},{10,11... | collective-permute-start | bytes 9224 | tf_op jit(solution)/shard_map/ppermute | solution.py:156
  4.5 0.7 %copy-start.1 = (s32[128,2]{0,1:T(2,128)S(1)}, s32[128,2]{0,1:T(2,128)}, u32[]{:S(2)}) copy-start(s32[128,2]{0,1:T(2,128)} %param.8) | copy-start | bytes 3076
  4.5 0.7 %copy-start.3 = (f32[64]{0:T(128)S(1)}, f32[64]{0:T(128)}, u32[]{:S(2)}) copy-start(f32[64]{0:T(128)} %param.6) | copy-start | bytes 772
  6.6 4.4 %collective-permute-start.3 = (bf16[2,16,384]{2,1,0:T(8,128)(2,1)S(1)}, bf16[2,16,384]{2,1,0:T(8,128)(2,1)S(1)}, u32[]{:S(2)}, u32[]{:S(2)}) collective-permute-start(bf16[2,16,384]{2,1,0:T(8,128)(2,1)S(1)} %get-tuple-element.25), channel_id=1, source_target_pairs={{0,13},{1,12},{2,15},{3,14},{4,9},{5,8},{6,11},{7,10},{8,5},{9,4},... | collective-permute-start | bytes 73736 | tf_op jit(solution)/shard_map/ppermute | solution.py:156
  9.4 3.3 %collective-permute-start.8 = (bf16[2,16,384]{2,1,0:T(8,128)(2,1)S(1)}, bf16[2,16,384]{2,1,0:T(8,128)(2,1)S(1)}, u32[]{:S(2)}, u32[]{:S(2)}) collective-permute-start(bf16[2,16,384]{2,1,0:T(8,128)(2,1)S(1)} %get-tuple-element.28), channel_id=1, source_target_pairs={{0,9},{1,8},{2,11},{3,10},{4,13},{5,12},{6,15},{7,14},{8,1},{9,0},... | collective-permute-start | bytes 73736 | tf_op jit(solution)/shard_map/ppermute | solution.py:156
  9.7 3.3 %collective-permute-start.7 = (bf16[2,16,384]{2,1,0:T(8,128)(2,1)S(1)}, bf16[2,16,384]{2,1,0:T(8,128)(2,1)S(1)}, u32[]{:S(2)}, u32[]{:S(2)}) collective-permute-start(bf16[2,16,384]{2,1,0:T(8,128)(2,1)S(1)} %get-tuple-element.27), channel_id=1, source_target_pairs={{0,5},{1,4},{2,7},{3,6},{4,1},{5,0},{6,3},{7,2},{8,13},{9,12},{10,... | collective-permute-start | bytes 73736 | tf_op jit(solution)/shard_map/ppermute | solution.py:156
  10.9 2.0 %collective-permute-start.6 = (f32[2,16,128]{2,1,0:T(8,128)S(1)}, f32[2,16,128]{2,1,0:T(8,128)S(1)}, u32[]{:S(2)}, u32[]{:S(2)}) collective-permute-start(f32[2,16,128]{2,1,0:T(8,128)S(1)} %get-tuple-element.33), channel_id=1, source_target_pairs={{0,1},{1,0},{2,3},{3,2},{4,5},{5,4},{6,7},{7,6},{8,9},{9,8},{10,11... | collective-permute-start | bytes 49160 | tf_op jit(solution)/shard_map/ppermute | solution.py:156
  11.1 1.8 %collective-permute-start.5 = (f32[2,16,128]{2,1,0:T(8,128)S(1)}, f32[2,16,128]{2,1,0:T(8,128)S(1)}, u32[]{:S(2)}, u32[]{:S(2)}) collective-permute-start(f32[2,16,128]{2,1,0:T(8,128)S(1)} %get-tuple-element.34), channel_id=1, source_target_pairs={{0,1},{1,0},{2,3},{3,2},{4,5},{5,4},{6,7},{7,6},{8,9},{9,8},{10,11... | collective-permute-start | bytes 49160 | tf_op jit(solution)/shard_map/ppermute | solution.py:156
  11.5 1.5 %collective-permute-start.4 = (f32[2,16,128]{2,1,0:T(8,128)S(1)}, f32[2,16,128]{2,1,0:T(8,128)S(1)}, u32[]{:S(2)}, u32[]{:S(2)}) collective-permute-start(f32[2,16,128]{2,1,0:T(8,128)S(1)} %get-tuple-element.32), channel_id=1, source_target_pairs={{0,1},{1,0},{2,3},{3,2},{4,5},{5,4},{6,7},{7,6},{8,9},{9,8},{10,11... | collective-permute-start | bytes 49160 | tf_op jit(solution)/shard_map/ppermute | solution.py:156
  13.0 4.3 %collective-permute-start.12 = (bf16[1,16,384]{2,1,0:T(8,128)(2,1)S(1)}, bf16[1,16,384]{2,1,0:T(8,128)(2,1)S(1)}, u32[]{:S(2)}, u32[]{:S(2)}) collective-permute-start(bf16[1,16,384]{2,1,0:T(8,128)(2,1)S(1)} %dynamic-slice_convert_fusion), channel_id=1, source_target_pairs={{0,17},{1,16},{2,19},{3,18},{4,21},{5,20},{6,23},{7,22},{8,25},{9,... | collective-permute-start | bytes 36872 | tf_op jit(solution)/shard_map/ppermute | solution.py:156
  15.6 1.2 %collective-permute-start.11 = (f32[1,16,128]{2,1,0:T(8,128)S(1)}, f32[1,16,128]{2,1,0:T(8,128)S(1)}, u32[]{:S(2)}, u32[]{:S(2)}) collective-permute-start(f32[1,16,128]{2,1,0:T(8,128)S(1)} %get-tuple-element.31), channel_id=1, source_target_pairs={{0,1},{1,0},{2,3},{3,2},{4,5},{5,4},{6,7},{7,6},{8,9},{9,8},{10,11... | collective-permute-start | bytes 24584 | tf_op jit(solution)/shard_map/ppermute | solution.py:156
  15.8 1.2 %collective-permute-start.10 = (f32[1,16,128]{2,1,0:T(8,128)S(1)}, f32[1,16,128]{2,1,0:T(8,128)S(1)}, u32[]{:S(2)}, u32[]{:S(2)}) collective-permute-start(f32[1,16,128]{2,1,0:T(8,128)S(1)} %get-tuple-element.30), channel_id=1, source_target_pairs={{0,1},{1,0},{2,3},{3,2},{4,5},{5,4},{6,7},{7,6},{8,9},{9,8},{10,11... | collective-permute-start | bytes 24584 | tf_op jit(solution)/shard_map/ppermute | solution.py:156
  16.1 1.2 %collective-permute-start.9 = (f32[1,16,128]{2,1,0:T(8,128)S(1)}, f32[1,16,128]{2,1,0:T(8,128)S(1)}, u32[]{:S(2)}, u32[]{:S(2)}) collective-permute-start(f32[1,16,128]{2,1,0:T(8,128)S(1)} %get-tuple-element.29), channel_id=1, source_target_pairs={{0,1},{1,0},{2,3},{3,2},{4,5},{5,4},{6,7},{7,6},{8,9},{9,8},{10,11... | collective-permute-start | bytes 24584 | tf_op jit(solution)/shard_map/ppermute | solution.py:156

commit v7 on v6

--- a/solution.py
+++ b/solution.py
@@ -235,13 +235,17 @@
             pairs = stack.reshape(stack.shape[0] // 2, 2, owned, out_len)
             side = (sta // bit) % 2
             stack = lax.dynamic_index_in_dim(pairs, side, 1, keepdims=False)
-            moved = [(bit, lax.dynamic_index_in_dim(pairs, 1 - side, 1, keepdims=False).astype(jnp.bfloat16))]
+            moved = [(bit, lax.dynamic_index_in_dim(pairs, 1 - side, 1, keepdims=False))]
         arrived = [flip(piece, distance, turn) for distance, piece in moved]
         if turn:
             if number == 0:
                 stack, _ = lax.optimization_barrier((stack, arrived[-1]))
-            pieces = [stack[:, :, at : at + LANES] for at in range(0, out_len, LANES)]
-            stack = jnp.concatenate([flip(piece, 0, turn) for piece in pieces], axis=2)
+            if number == 0:
+                pieces = [stack[:, :, at : at + LANES] for at in range(0, out_len, LANES)]
+                stack = jnp.concatenate([flip(piece, 0, turn) for piece in pieces], axis=2)
+            else:
+                pieces = [stack[:, : owned // 2], stack[:, owned // 2 :]]
+                stack = jnp.concatenate([flip(piece, 0, turn) for piece in pieces], axis=1)
         for piece in arrived:
             stack = stack + piece.astype(jnp.float32)
     return stack

time: 18 us -> 18 us (level)
  starting transfers between devices: 10.6 us -> 10.4 us
    ppermute x13 -> x12, starting transfers between devices: 10.6 us -> 10.4 us  [flip(): return lax.ppermute(value, ('sta', 'tpl'), pairs)]
    ppermute x13 -> x12, waiting for transfers between devices: 2.9 us -> 3.04 us  [flip(): return lax.ppermute(value, ('sta', 'tpl'), pairs)]
  transfers between devices with their start and end apart: 13 -> 12, of which waited for: 6 -> 6; matrix products, arithmetic and copies ran while one was open for 7% -> 7% of each run, Pallas kernels for 4% -> 4%
where the time goes in v7:
time: 18 us; the launch traced here: 17.8 us
  starting transfers between devices  10.4 us (58%)
  waiting for transfers between devices  3.04 us (17%)
  local copies, waits for them, and re-layouts  1.87 us (10%)
  Pallas kernels  1.76 us (10%)
  other arithmetic  0.63 us (4%)
    ppermute x12, starting transfers between devices, flip(): return lax.ppermute(value, ('sta', 'tpl'), pairs)  10.4 us
    ppermute x12, waiting for transfers between devices, flip(): return lax.ppermute(value, ('sta', 'tpl'), pairs)  3.04 us
    transpose x1, local copies, waits for them, and re-layouts, shards(): templates.transpose(1, 0, 2)  1.16 us
    pallas_call x1, Pallas kernels, shards(): pl.pallas_call(functools.partial(send_kernel, segments), out_shape=(*[jax...  1.05 us
    unnamed x8, local copies, waits for them, and re-layouts  0.68 us
    add x2, other arithmetic, shards(): stack = stack + piece.astype(jnp.float32)  0.63 us
    pallas_call x1, Pallas kernels, shards(): pl.pallas_call(keep_kernel, out_shape=jax.ShapeDtypeStruct((owners // par...  0.44 us
  transfers between devices with their start and end apart: 12, of which 6 were waited for; matrix products, arithmetic and copies ran while one was open for 7% of the time, Pallas kernels for 4%

profile of v7, /device:TPU:0, one launch (start us, length us, event | category | flops | bytes accessed | tf_op | source)
XLA Modules:
  0.0 17.8 jit_solution(11268389505600990588)
XLA Ops:
  0.0 2.4 %collective-permute-start = (f32[2,384]{1,0:T(2,128)}, f32[2,384]{1,0:T(2,128)S(1)}, u32[]{:S(2)}, u32[]{:S(2)}) collective-permute-start(f32[2,384]{1,0:T(2,128)} %wave_in.1), channel_id=1, source_target_pairs={{0,3},{1,2},{2,1},{3,0},{4,7},{5,6},{6,5},{7,4},{8,11},{9,10},{10,... | collective-permute-start | bytes 9224 | tf_op jit(solution)/shard_map/ppermute | solution.py:156
  2.4 0.7 %collective-permute-start.1 = (f32[2,384]{1,0:T(2,128)}, f32[2,384]{1,0:T(2,128)S(1)}, u32[]{:S(2)}, u32[]{:S(2)}) collective-permute-start(f32[2,384]{1,0:T(2,128)} %wave_in.1), channel_id=1, source_target_pairs={{0,1},{1,0},{2,3},{3,2},{4,5},{5,4},{6,7},{7,6},{8,9},{9,8},{10,11... | collective-permute-start | bytes 9224 | tf_op jit(solution)/shard_map/ppermute | solution.py:156
  3.1 1.2 %copy.6 = bf16[2,128,1024]{2,1,0:T(8,128)(2,1)S(1)} copy(bf16[2,128,1024]{2,0,1:T(2,128)(2,1)} %bitcast.10) | data formatting | bytes 1048576 | tf_op jit(solution)/shard_map/transpose | solution.py:174
  4.3 0.3 %collective-permute-start.2 = (f32[2,384]{1,0:T(2,128)S(1)}, f32[2,384]{1,0:T(2,128)S(1)}, u32[]{:S(2)}, u32[]{:S(2)}) collective-permute-start(f32[2,384]{1,0:T(2,128)S(1)} %collective-permute-done.refs_3_), channel_id=1, source_target_pairs={{0,1},{1,0},{2,3},{3,2},{4,5},{5,4},{6,7},{7,6},{8,9},{9,8},{10,11... | collective-permute-start | bytes 9224 | tf_op jit(solution)/shard_map/ppermute | solution.py:156
  4.6 0.4 %copy-done = f32[2,384]{1,0:T(2,128)S(1)} copy-done((f32[2,384]{1,0:T(2,128)S(1)}, f32[2,384]{1,0:T(2,128)}, u32[]{:S(2)}) %copy-start) | copy-done | bytes 3096
  4.9 0.3 %copy-done.1 = s32[128,2]{0,1:T(2,128)S(1)} copy-done((s32[128,2]{0,1:T(2,128)S(1)}, s32[128,2]{0,1:T(2,128)}, u32[]{:S(2)}) %copy-start.1) | copy-done | bytes 1048
  5.2 0.3 %columns.1 = (f32[2,384]{1,0:T(2,128)S(1)}, f32[256,128]{1,0:T(8,128)S(1)}, f32[2,4,32,128]{3,2,1,0:T(8,128)S(1)}, s32[2,4,32,128]{3,2,1,0:T(8,128)S(1)}) custom-call(f32[2,384]{1,0:T(2,128)S(1)} %copy-done, f32[1,64]{1,0:T(1,128)S(1)} %bitcast.9, s32[2,128]{1,0:T(2,128)S(1)} %bitcast.7, s32[2,128]{1,0:T(2,128)S(1)} %bitcast.8), custom_call_target="tpu_custom_call" | custom-call | flops 1048576 | bytes 1048576 | tf_op jit(solution)/shard_map/columns/pallas_call | solution.py:175
  5.5 1.1 %send_parts.1 = (bf16[2,16,384]{2,1,0:T(8,128)(2,1)S(1)}, bf16[2,16,384]{2,1,0:T(8,128)(2,1)S(1)}, bf16[2,16,384]{2,1,0:T(8,128)(2,1)S(1)}, bf16[2,128,1536]{2,1,0:T(8,128)(2,1)S(1)}, f32[2,512]{1,0:T(2,128)S(1)}) custom-call(f32[2,384]{1,0:T(2,128)S(1)} %get-tuple-element.20.refs_0_, f32[2,384]{1,0:T(2,128)S(1)} %collective-permute-done.1.refs_1_, ...), custom_call_target="tpu_custom_call" | custom-call | flops 1048576 | bytes 1048576 | tf_op jit(solution)/shard_map/send_parts/pallas_call | solution.py:199
  6.6 2.8 %collective-permute-start.3 = (bf16[2,16,384]{2,1,0:T(8,128)(2,1)S(1)}, bf16[2,16,384]{2,1,0:T(8,128)(2,1)S(1)}, u32[]{:S(2)}, u32[]{:S(2)}) collective-permute-start(bf16[2,16,384]{2,1,0:T(8,128)(2,1)S(1)} %get-tuple-element.25), channel_id=1, source_target_pairs={{0,13},{1,12},{2,15},{3,14},{4,9},{5,8},{6,11},{7,10},{8,5},{9,4},... | collective-permute-start | bytes 73736 | tf_op jit(solution)/shard_map/ppermute | solution.py:156
  9.4 0.2 %collective-permute-start.8 = (bf16[2,16,384]{2,1,0:T(8,128)(2,1)S(1)}, bf16[2,16,384]{2,1,0:T(8,128)(2,1)S(1)}, u32[]{:S(2)}, u32[]{:S(2)}) collective-permute-start(bf16[2,16,384]{2,1,0:T(8,128)(2,1)S(1)} %get-tuple-element.28), channel_id=1, source_target_pairs={{0,9},{1,8},{2,11},{3,10},{4,13},{5,12},{6,15},{7,14},{8,1},{9,0},... | collective-permute-start | bytes 73736 | tf_op jit(solution)/shard_map/ppermute | solution.py:156
  9.7 0.2 %collective-permute-start.7 = (bf16[2,16,384]{2,1,0:T(8,128)(2,1)S(1)}, bf16[2,16,384]{2,1,0:T(8,128)(2,1)S(1)}, u32[]{:S(2)}, u32[]{:S(2)}) collective-permute-start(bf16[2,16,384]{2,1,0:T(8,128)(2,1)S(1)} %get-tuple-element.27), channel_id=1, source_target_pairs={{0,5},{1,4},{2,7},{3,6},{4,1},{5,0},{6,3},{7,2},{8,13},{9,12},{10,... | collective-permute-start | bytes 73736 | tf_op jit(solution)/shard_map/ppermute | solution.py:156
  9.9 0.4 %keep_part.1 = f32[2,16,384]{2,1,0:T(8,128)S(1)} custom-call(bf16[2,2,4,16,1024]{4,3,2,1,0:T(8,128)(2,1)S(1)} %bitcast.6, f32[2,4,32,128]{3,2,1,0:T(8,128)S(1)} %get-tuple-element.18.refs_6_.used_ref, s32[2,4,32,128]{3,2,1,0:T(8,128)S(1)} %get-tuple-element.19.refs_7_.shift_ref, bf16[2,128,1536]{2,1,0:T(8,128)(2,1)S(1)} %get-tuple-element.23.hankel_ref, ...), custom_call_target="tpu_custom_call" | custom-call | flops 1048576 | bytes 1048576 | tf_op jit(solution)/shard_map/keep_part/pallas_call | solution.py:217
  10.3 0.6 %collective-permute-done.3 = bf16[2,16,384]{2,1,0:T(8,128)(2,1)S(1)} collective-permute-done((bf16[2,16,384]{2,1,0:T(8,128)(2,1)S(1)}, bf16[2,16,384]{2,1,0:T(8,128)(2,1)S(1)}, u32[]{:S(2)}, u32[]{:S(2)}) %collective-permute-start.3) | collective-permute-done | bytes 24608 | tf_op jit(solution)/shard_map/ppermute | solution.py:156
  11.1 0.3 %collective-permute-start.5 = (f32[2,16,128]{2,1,0:T(8,128)S(1)}, f32[2,16,128]{2,1,0:T(8,128)S(1)}, u32[]{:S(2)}, u32[]{:S(2)}) collective-permute-start(f32[2,16,128]{2,1,0:T(8,128)S(1)} %get-tuple-element.33), channel_id=1, source_target_pairs={{0,1},{1,0},{2,3},{3,2},{4,5},{5,4},{6,7},{7,6},{8,9},{9,8},{10,11... | collective-permute-start | bytes 49160 | tf_op jit(solution)/shard_map/ppermute | solution.py:156
  11.5 0.2 %collective-permute-start.4 = (f32[2,16,128]{2,1,0:T(8,128)S(1)}, f32[2,16,128]{2,1,0:T(8,128)S(1)}, u32[]{:S(2)}, u32[]{:S(2)}) collective-permute-start(f32[2,16,128]{2,1,0:T(8,128)S(1)} %get-tuple-element.31), channel_id=1, source_target_pairs={{0,1},{1,0},{2,3},{3,2},{4,5},{5,4},{6,7},{7,6},{8,9},{9,8},{10,11... | collective-permute-start | bytes 49160 | tf_op jit(solution)/shard_map/ppermute | solution.py:156
  11.6 1.0 %collective-permute-done.8 = bf16[2,16,384]{2,1,0:T(8,128)(2,1)S(1)} collective-permute-done((bf16[2,16,384]{2,1,0:T(8,128)(2,1)S(1)}, bf16[2,16,384]{2,1,0:T(8,128)(2,1)S(1)}, u32[]{:S(2)}, u32[]{:S(2)}) %collective-permute-start.8) | collective-permute-done | bytes 24608 | tf_op jit(solution)/shard_map/ppermute | solution.py:156
  12.7 0.2 %collective-permute-done.7 = bf16[2,16,384]{2,1,0:T(8,128)(2,1)S(1)} collective-permute-done((bf16[2,16,384]{2,1,0:T(8,128)(2,1)S(1)}, bf16[2,16,384]{2,1,0:T(8,128)(2,1)S(1)}, u32[]{:S(2)}, u32[]{:S(2)}) %collective-permute-start.7) | collective-permute-done | bytes 24608 | tf_op jit(solution)/shard_map/ppermute | solution.py:156
  13.0 2.6 %collective-permute-start.11 = (f32[1,16,384]{2,1,0:T(8,128)S(1)}, f32[1,16,384]{2,1,0:T(8,128)S(1)}, u32[]{:S(2)}, u32[]{:S(2)}) collective-permute-start(f32[1,16,384]{2,1,0:T(8,128)S(1)} %constant_dynamic-slice_fusion.1), channel_id=1, source_target_pairs={{0,17},{1,16},{2,19},{3,18},{4,21},{5,20},{6,23},{7,22},{8,25},{9,... | collective-permute-start | bytes 73736 | tf_op jit(solution)/shard_map/ppermute | solution.py:156
  15.6 0.2 %collective-permute-start.10 = (f32[1,8,384]{2,1,0:T(8,128)S(1)}, f32[1,8,384]{2,1,0:T(8,128)S(1)}, u32[]{:S(2)}, u32[]{:S(2)}) collective-permute-start(f32[1,8,384]{2,1,0:T(8,128)S(1)} %get-tuple-element.30), channel_id=1, source_target_pairs={{0,1},{1,0},{2,3},{3,2},{4,5},{5,4},{6,7},{7,6},{8,9},{9,8},{10,11... | collective-permute-start | bytes 36872 | tf_op jit(solution)/shard_map/ppermute | solution.py:156
  15.8 0.3 %collective-permute-start.9 = (f32[1,8,384]{2,1,0:T(8,128)S(1)}, f32[1,8,384]{2,1,0:T(8,128)S(1)}, u32[]{:S(2)}, u32[]{:S(2)}) collective-permute-start(f32[1,8,384]{2,1,0:T(8,128)S(1)} %get-tuple-element.29), channel_id=1, source_target_pairs={{0,1},{1,0},{2,3},{3,2},{4,5},{5,4},{6,7},{7,6},{8,9},{9,8},{10,11... | collective-permute-start | bytes 36872 | tf_op jit(solution)/shard_map/ppermute | solution.py:156
  16.1 0.7 %collective-permute-done.10 = f32[1,8,384]{2,1,0:T(8,128)S(1)} collective-permute-done((f32[1,8,384]{2,1,0:T(8,128)S(1)}, f32[1,8,384]{2,1,0:T(8,128)S(1)}, u32[]{:S(2)}, u32[]{:S(2)}) %collective-permute-start.10) | collective-permute-done | bytes 12320 | tf_op jit(solution)/shard_map/ppermute | solution.py:156
  16.7 0.2 %collective-permute-done.9 = f32[1,8,384]{2,1,0:T(8,128)S(1)} collective-permute-done((f32[1,8,384]{2,1,0:T(8,128)S(1)}, f32[1,8,384]{2,1,0:T(8,128)S(1)}, u32[]{:S(2)}, u32[]{:S(2)}) %collective-permute-start.9) | collective-permute-done | bytes 12320 | tf_op jit(solution)/shard_map/ppermute | solution.py:156
  16.9 0.3 %collective-permute-done.11 = f32[1,16,384]{2,1,0:T(8,128)S(1)} collective-permute-done((f32[1,16,384]{2,1,0:T(8,128)S(1)}, f32[1,16,384]{2,1,0:T(8,128)S(1)}, u32[]{:S(2)}, u32[]{:S(2)}) %collective-permute-start.11) | collective-permute-done | bytes 24608 | tf_op jit(solution)/shard_map/ppermute | solution.py:156
  17.2 0.6 %maximum_add_fusion.1 = f32[1,16,384]{2,1,0:T(8,128)} fusion(f32[1,16,384]{2,1,0:T(8,128)S(1)} %collective-permute-done.11, f32[1,8,384]{2,1,0:T(8,128)S(1)} %collective-permute-done.10, f32[1,8,384]{2,1,0:T(8,128)S(1)} %collective-permute-done.9), kind=kLoop, calls=%fused_computation.3 | loop fusion | flops 12288 | bytes 73728 | tf_op jit(solution)/shard_map/add | solution.py:250
  (17 shorter events, 0.2 us)
Async XLA Ops:
  0.0 4.2 %collective-permute-start = (f32[2,384]{1,0:T(2,128)}, f32[2,384]{1,0:T(2,128)S(1)}, u32[]{:S(2)}, u32[]{:S(2)}) collective-permute-start(f32[2,384]{1,0:T(2,128)} %wave_in.1), channel_id=1, source_target_pairs={{0,3},{1,2},{2,1},{3,0},{4,7},{5,6},{6,5},{7,4},{8,11},{9,10},{10,... | collective-permute-start | bytes 9224 | tf_op jit(solution)/shard_map/ppermute | solution.py:156
  2.4 3.1 %collective-permute-start.1 = (f32[2,384]{1,0:T(2,128)}, f32[2,384]{1,0:T(2,128)S(1)}, u32[]{:S(2)}, u32[]{:S(2)}) collective-permute-start(f32[2,384]{1,0:T(2,128)} %wave_in.1), channel_id=1, source_target_pairs={{0,1},{1,0},{2,3},{3,2},{4,5},{5,4},{6,7},{7,6},{8,9},{9,8},{10,11... | collective-permute-start | bytes 9224 | tf_op jit(solution)/shard_map/ppermute | solution.py:156
  3.1 1.5 %copy-start.2 = (s32[128,2]{0,1:T(2,128)S(1)}, s32[128,2]{0,1:T(2,128)}, u32[]{:S(2)}) copy-start(s32[128,2]{0,1:T(2,128)} %param.9) | copy-start | bytes 3076
  4.2 0.7 %copy-start = (f32[2,384]{1,0:T(2,128)S(1)}, f32[2,384]{1,0:T(2,128)}, u32[]{:S(2)}) copy-start(f32[2,384]{1,0:T(2,128)} %wave_in.1) | copy-start | bytes 9220
  4.3 1.3 %collective-permute-start.2 = (f32[2,384]{1,0:T(2,128)S(1)}, f32[2,384]{1,0:T(2,128)S(1)}, u32[]{:S(2)}, u32[]{:S(2)}) collective-permute-start(f32[2,384]{1,0:T(2,128)S(1)} %collective-permute-done.refs_3_), channel_id=1, source_target_pairs={{0,1},{1,0},{2,3},{3,2},{4,5},{5,4},{6,7},{7,6},{8,9},{9,8},{10,11... | collective-permute-start | bytes 9224 | tf_op jit(solution)/shard_map/ppermute | solution.py:156
  4.5 0.7 %copy-start.1 = (s32[128,2]{0,1:T(2,128)S(1)}, s32[128,2]{0,1:T(2,128)}, u32[]{:S(2)}) copy-start(s32[128,2]{0,1:T(2,128)} %param.8) | copy-start | bytes 3076
  4.5 0.7 %copy-start.3 = (f32[64]{0:T(128)S(1)}, f32[64]{0:T(128)}, u32[]{:S(2)}) copy-start(f32[64]{0:T(128)} %param.6) | copy-start | bytes 772
  6.6 4.4 %collective-permute-start.3 = (bf16[2,16,384]{2,1,0:T(8,128)(2,1)S(1)}, bf16[2,16,384]{2,1,0:T(8,128)(2,1)S(1)}, u32[]{:S(2)}, u32[]{:S(2)}) collective-permute-start(bf16[2,16,384]{2,1,0:T(8,128)(2,1)S(1)} %get-tuple-element.25), channel_id=1, source_target_pairs={{0,13},{1,12},{2,15},{3,14},{4,9},{5,8},{6,11},{7,10},{8,5},{9,4},... | collective-permute-start | bytes 73736 | tf_op jit(solution)/shard_map/ppermute | solution.py:156
  9.4 3.3 %collective-permute-start.8 = (bf16[2,16,384]{2,1,0:T(8,128)(2,1)S(1)}, bf16[2,16,384]{2,1,0:T(8,128)(2,1)S(1)}, u32[]{:S(2)}, u32[]{:S(2)}) collective-permute-start(bf16[2,16,384]{2,1,0:T(8,128)(2,1)S(1)} %get-tuple-element.28), channel_id=1, source_target_pairs={{0,9},{1,8},{2,11},{3,10},{4,13},{5,12},{6,15},{7,14},{8,1},{9,0},... | collective-permute-start | bytes 73736 | tf_op jit(solution)/shard_map/ppermute | solution.py:156
  9.7 3.3 %collective-permute-start.7 = (bf16[2,16,384]{2,1,0:T(8,128)(2,1)S(1)}, bf16[2,16,384]{2,1,0:T(8,128)(2,1)S(1)}, u32[]{:S(2)}, u32[]{:S(2)}) collective-permute-start(bf16[2,16,384]{2,1,0:T(8,128)(2,1)S(1)} %get-tuple-element.27), channel_id=1, source_target_pairs={{0,5},{1,4},{2,7},{3,6},{4,1},{5,0},{6,3},{7,2},{8,13},{9,12},{10,... | collective-permute-start | bytes 73736 | tf_op jit(solution)/shard_map/ppermute | solution.py:156
  10.9 2.0 %collective-permute-start.6 = (f32[2,16,128]{2,1,0:T(8,128)S(1)}, f32[2,16,128]{2,1,0:T(8,128)S(1)}, u32[]{:S(2)}, u32[]{:S(2)}) collective-permute-start(f32[2,16,128]{2,1,0:T(8,128)S(1)} %get-tuple-element.32), channel_id=1, source_target_pairs={{0,1},{1,0},{2,3},{3,2},{4,5},{5,4},{6,7},{7,6},{8,9},{9,8},{10,11... | collective-permute-start | bytes 49160 | tf_op jit(solution)/shard_map/ppermute | solution.py:156
  11.1 1.8 %collective-permute-start.5 = (f32[2,16,128]{2,1,0:T(8,128)S(1)}, f32[2,16,128]{2,1,0:T(8,128)S(1)}, u32[]{:S(2)}, u32[]{:S(2)}) collective-permute-start(f32[2,16,128]{2,1,0:T(8,128)S(1)} %get-tuple-element.33), channel_id=1, source_target_pairs={{0,1},{1,0},{2,3},{3,2},{4,5},{5,4},{6,7},{7,6},{8,9},{9,8},{10,11... | collective-permute-start | bytes 49160 | tf_op jit(solution)/shard_map/ppermute | solution.py:156
  11.5 1.5 %collective-permute-start.4 = (f32[2,16,128]{2,1,0:T(8,128)S(1)}, f32[2,16,128]{2,1,0:T(8,128)S(1)}, u32[]{:S(2)}, u32[]{:S(2)}) collective-permute-start(f32[2,16,128]{2,1,0:T(8,128)S(1)} %get-tuple-element.31), channel_id=1, source_target_pairs={{0,1},{1,0},{2,3},{3,2},{4,5},{5,4},{6,7},{7,6},{8,9},{9,8},{10,11... | collective-permute-start | bytes 49160 | tf_op jit(solution)/shard_map/ppermute | solution.py:156
  13.0 4.2 %collective-permute-start.11 = (f32[1,16,384]{2,1,0:T(8,128)S(1)}, f32[1,16,384]{2,1,0:T(8,128)S(1)}, u32[]{:S(2)}, u32[]{:S(2)}) collective-permute-start(f32[1,16,384]{2,1,0:T(8,128)S(1)} %constant_dynamic-slice_fusion.1), channel_id=1, source_target_pairs={{0,17},{1,16},{2,19},{3,18},{4,21},{5,20},{6,23},{7,22},{8,25},{9,... | collective-permute-start | bytes 73736 | tf_op jit(solution)/shard_map/ppermute | solution.py:156
  15.6 1.2 %collective-permute-start.10 = (f32[1,8,384]{2,1,0:T(8,128)S(1)}, f32[1,8,384]{2,1,0:T(8,128)S(1)}, u32[]{:S(2)}, u32[]{:S(2)}) collective-permute-start(f32[1,8,384]{2,1,0:T(8,128)S(1)} %get-tuple-element.30), channel_id=1, source_target_pairs={{0,1},{1,0},{2,3},{3,2},{4,5},{5,4},{6,7},{7,6},{8,9},{9,8},{10,11... | collective-permute-start | bytes 36872 | tf_op jit(solution)/shard_map/ppermute | solution.py:156
  15.8 1.2 %collective-permute-start.9 = (f32[1,8,384]{2,1,0:T(8,128)S(1)}, f32[1,8,384]{2,1,0:T(8,128)S(1)}, u32[]{:S(2)}, u32[]{:S(2)}) collective-permute-start(f32[1,8,384]{2,1,0:T(8,128)S(1)} %get-tuple-element.29), channel_id=1, source_target_pairs={{0,1},{1,0},{2,3},{3,2},{4,5},{5,4},{6,7},{7,6},{8,9},{9,8},{10,11... | collective-permute-start | bytes 36872 | tf_op jit(solution)/shard_map/ppermute | solution.py:156

commit v8 on v7

--- a/solution.py
+++ b/solution.py
@@ -54,7 +54,7 @@
     for s in range(stations):
         rows = jnp.concatenate([rows_ref[s, :, p].reshape(part_rows, templ_len) for p in parts], axis=0)
         raw = [None] * time_pairs
-        for offset in range(1, lag_pairs + time_pairs):
+        for offset in reversed(range(1, lag_pairs + time_pairs)):
             uses = [(j, offset - lag_pairs + j) for j in range(lag_pairs) if 0 <= offset - lag_pairs + j < time_pairs]
             at = offset * PAIR
             window = jnp.concatenate(

time: 18 us -> 17.9 us (level)
  no operation moved by 1% of the time
where the time goes in v8:
time: 17.9 us; the launch traced here: 17.8 us
  starting transfers between devices  10.4 us (58%)
  waiting for transfers between devices  3.06 us (17%)
  local copies, waits for them, and re-layouts  1.87 us (10%)
  Pallas kernels  1.72 us (10%)
  other arithmetic  0.63 us (4%)
    ppermute x12, starting transfers between devices, flip(): return lax.ppermute(value, ('sta', 'tpl'), pairs)  10.4 us
    ppermute x12, waiting for transfers between devices, flip(): return lax.ppermute(value, ('sta', 'tpl'), pairs)  3.06 us
    transpose x1, local copies, waits for them, and re-layouts, shards(): templates.transpose(1, 0, 2)  1.16 us
    pallas_call x1, Pallas kernels, shards(): pl.pallas_call(functools.partial(send_kernel, segments), out_shape=(*[jax...  1.03 us
    unnamed x8, local copies, waits for them, and re-layouts  0.68 us
    add x2, other arithmetic, shards(): stack = stack + piece.astype(jnp.float32)  0.63 us
    pallas_call x1, Pallas kernels, shards(): pl.pallas_call(keep_kernel, out_shape=jax.ShapeDtypeStruct((owners // par...  0.43 us
  transfers between devices with their start and end apart: 12, of which 6 were waited for; matrix products, arithmetic and copies ran while one was open for 7% of the time, Pallas kernels for 4%

profile of v8, /device:TPU:0, one launch (start us, length us, event | category | flops | bytes accessed | tf_op | source)
XLA Modules:
  0.0 17.8 jit_solution(7765947485130962246)
XLA Ops:
  0.0 2.4 %collective-permute-start = (f32[2,384]{1,0:T(2,128)}, f32[2,384]{1,0:T(2,128)S(1)}, u32[]{:S(2)}, u32[]{:S(2)}) collective-permute-start(f32[2,384]{1,0:T(2,128)} %wave_in.1), channel_id=1, source_target_pairs={{0,3},{1,2},{2,1},{3,0},{4,7},{5,6},{6,5},{7,4},{8,11},{9,10},{10,... | collective-permute-start | bytes 9224 | tf_op jit(solution)/shard_map/ppermute | solution.py:156
  2.4 0.7 %collective-permute-start.1 = (f32[2,384]{1,0:T(2,128)}, f32[2,384]{1,0:T(2,128)S(1)}, u32[]{:S(2)}, u32[]{:S(2)}) collective-permute-start(f32[2,384]{1,0:T(2,128)} %wave_in.1), channel_id=1, source_target_pairs={{0,1},{1,0},{2,3},{3,2},{4,5},{5,4},{6,7},{7,6},{8,9},{9,8},{10,11... | collective-permute-start | bytes 9224 | tf_op jit(solution)/shard_map/ppermute | solution.py:156
  3.1 1.2 %copy.6 = bf16[2,128,1024]{2,1,0:T(8,128)(2,1)S(1)} copy(bf16[2,128,1024]{2,0,1:T(2,128)(2,1)} %bitcast.10) | data formatting | bytes 1048576 | tf_op jit(solution)/shard_map/transpose | solution.py:174
  4.3 0.3 %collective-permute-start.2 = (f32[2,384]{1,0:T(2,128)S(1)}, f32[2,384]{1,0:T(2,128)S(1)}, u32[]{:S(2)}, u32[]{:S(2)}) collective-permute-start(f32[2,384]{1,0:T(2,128)S(1)} %collective-permute-done.refs_3_), channel_id=1, source_target_pairs={{0,1},{1,0},{2,3},{3,2},{4,5},{5,4},{6,7},{7,6},{8,9},{9,8},{10,11... | collective-permute-start | bytes 9224 | tf_op jit(solution)/shard_map/ppermute | solution.py:156
  4.6 0.4 %copy-done = f32[2,384]{1,0:T(2,128)S(1)} copy-done((f32[2,384]{1,0:T(2,128)S(1)}, f32[2,384]{1,0:T(2,128)}, u32[]{:S(2)}) %copy-start) | copy-done | bytes 3096
  4.9 0.3 %copy-done.1 = s32[128,2]{0,1:T(2,128)S(1)} copy-done((s32[128,2]{0,1:T(2,128)S(1)}, s32[128,2]{0,1:T(2,128)}, u32[]{:S(2)}) %copy-start.1) | copy-done | bytes 1048
  5.2 0.3 %columns.1 = (f32[2,384]{1,0:T(2,128)S(1)}, f32[256,128]{1,0:T(8,128)S(1)}, f32[2,4,32,128]{3,2,1,0:T(8,128)S(1)}, s32[2,4,32,128]{3,2,1,0:T(8,128)S(1)}) custom-call(f32[2,384]{1,0:T(2,128)S(1)} %copy-done, f32[1,64]{1,0:T(1,128)S(1)} %bitcast.9, s32[2,128]{1,0:T(2,128)S(1)} %bitcast.7, s32[2,128]{1,0:T(2,128)S(1)} %bitcast.8), custom_call_target="tpu_custom_call" | custom-call | flops 1048576 | bytes 1048576 | tf_op jit(solution)/shard_map/columns/pallas_call | solution.py:175
  5.5 1.0 %send_parts.1 = (bf16[2,16,384]{2,1,0:T(8,128)(2,1)S(1)}, bf16[2,16,384]{2,1,0:T(8,128)(2,1)S(1)}, bf16[2,16,384]{2,1,0:T(8,128)(2,1)S(1)}, bf16[2,128,1536]{2,1,0:T(8,128)(2,1)S(1)}, f32[2,512]{1,0:T(2,128)S(1)}) custom-call(f32[2,384]{1,0:T(2,128)S(1)} %get-tuple-element.20.refs_0_, f32[2,384]{1,0:T(2,128)S(1)} %collective-permute-done.1.refs_1_, ...), custom_call_target="tpu_custom_call" | custom-call | flops 1048576 | bytes 1048576 | tf_op jit(solution)/shard_map/send_parts/pallas_call | solution.py:199
  6.5 2.8 %collective-permute-start.3 = (bf16[2,16,384]{2,1,0:T(8,128)(2,1)S(1)}, bf16[2,16,384]{2,1,0:T(8,128)(2,1)S(1)}, u32[]{:S(2)}, u32[]{:S(2)}) collective-permute-start(bf16[2,16,384]{2,1,0:T(8,128)(2,1)S(1)} %get-tuple-element.25), channel_id=1, source_target_pairs={{0,13},{1,12},{2,15},{3,14},{4,9},{5,8},{6,11},{7,10},{8,5},{9,4},... | collective-permute-start | bytes 73736 | tf_op jit(solution)/shard_map/ppermute | solution.py:156
  9.4 0.2 %collective-permute-start.8 = (bf16[2,16,384]{2,1,0:T(8,128)(2,1)S(1)}, bf16[2,16,384]{2,1,0:T(8,128)(2,1)S(1)}, u32[]{:S(2)}, u32[]{:S(2)}) collective-permute-start(bf16[2,16,384]{2,1,0:T(8,128)(2,1)S(1)} %get-tuple-element.28), channel_id=1, source_target_pairs={{0,9},{1,8},{2,11},{3,10},{4,13},{5,12},{6,15},{7,14},{8,1},{9,0},... | collective-permute-start | bytes 73736 | tf_op jit(solution)/shard_map/ppermute | solution.py:156
  9.6 0.2 %collective-permute-start.7 = (bf16[2,16,384]{2,1,0:T(8,128)(2,1)S(1)}, bf16[2,16,384]{2,1,0:T(8,128)(2,1)S(1)}, u32[]{:S(2)}, u32[]{:S(2)}) collective-permute-start(bf16[2,16,384]{2,1,0:T(8,128)(2,1)S(1)} %get-tuple-element.27), channel_id=1, source_target_pairs={{0,5},{1,4},{2,7},{3,6},{4,1},{5,0},{6,3},{7,2},{8,13},{9,12},{10,... | collective-permute-start | bytes 73736 | tf_op jit(solution)/shard_map/ppermute | solution.py:156
  9.8 0.4 %keep_part.1 = f32[2,16,384]{2,1,0:T(8,128)S(1)} custom-call(bf16[2,2,4,16,1024]{4,3,2,1,0:T(8,128)(2,1)S(1)} %bitcast.6, f32[2,4,32,128]{3,2,1,0:T(8,128)S(1)} %get-tuple-element.18.refs_6_.used_ref, s32[2,4,32,128]{3,2,1,0:T(8,128)S(1)} %get-tuple-element.19.refs_7_.shift_ref, bf16[2,128,1536]{2,1,0:T(8,128)(2,1)S(1)} %get-tuple-element.23.hankel_ref, ...), custom_call_target="tpu_custom_call" | custom-call | flops 1048576 | bytes 1048576 | tf_op jit(solution)/shard_map/keep_part/pallas_call | solution.py:217
  10.2 0.7 %collective-permute-done.3 = bf16[2,16,384]{2,1,0:T(8,128)(2,1)S(1)} collective-permute-done((bf16[2,16,384]{2,1,0:T(8,128)(2,1)S(1)}, bf16[2,16,384]{2,1,0:T(8,128)(2,1)S(1)}, u32[]{:S(2)}, u32[]{:S(2)}) %collective-permute-start.3) | collective-permute-done | bytes 24608 | tf_op jit(solution)/shard_map/ppermute | solution.py:156
  10.9 0.2 %collective-permute-start.6 = (f32[2,16,128]{2,1,0:T(8,128)S(1)}, f32[2,16,128]{2,1,0:T(8,128)S(1)}, u32[]{:S(2)}, u32[]{:S(2)}) collective-permute-start(f32[2,16,128]{2,1,0:T(8,128)S(1)} %get-tuple-element.32), channel_id=1, source_target_pairs={{0,1},{1,0},{2,3},{3,2},{4,5},{5,4},{6,7},{7,6},{8,9},{9,8},{10,11... | collective-permute-start | bytes 49160 | tf_op jit(solution)/shard_map/ppermute | solution.py:156
  11.1 0.3 %collective-permute-start.5 = (f32[2,16,128]{2,1,0:T(8,128)S(1)}, f32[2,16,128]{2,1,0:T(8,128)S(1)}, u32[]{:S(2)}, u32[]{:S(2)}) collective-permute-start(f32[2,16,128]{2,1,0:T(8,128)S(1)} %get-tuple-element.33), channel_id=1, source_target_pairs={{0,1},{1,0},{2,3},{3,2},{4,5},{5,4},{6,7},{7,6},{8,9},{9,8},{10,11... | collective-permute-start | bytes 49160 | tf_op jit(solution)/shard_map/ppermute | solution.py:156
  11.6 1.0 %collective-permute-done.8 = bf16[2,16,384]{2,1,0:T(8,128)(2,1)S(1)} collective-permute-done((bf16[2,16,384]{2,1,0:T(8,128)(2,1)S(1)}, bf16[2,16,384]{2,1,0:T(8,128)(2,1)S(1)}, u32[]{:S(2)}, u32[]{:S(2)}) %collective-permute-start.8) | collective-permute-done | bytes 24608 | tf_op jit(solution)/shard_map/ppermute | solution.py:156
  12.6 0.2 %collective-permute-done.7 = bf16[2,16,384]{2,1,0:T(8,128)(2,1)S(1)} collective-permute-done((bf16[2,16,384]{2,1,0:T(8,128)(2,1)S(1)}, bf16[2,16,384]{2,1,0:T(8,128)(2,1)S(1)}, u32[]{:S(2)}, u32[]{:S(2)}) %collective-permute-start.7) | collective-permute-done | bytes 24608 | tf_op jit(solution)/shard_map/ppermute | solution.py:156
  12.9 2.6 %collective-permute-start.11 = (f32[1,16,384]{2,1,0:T(8,128)S(1)}, f32[1,16,384]{2,1,0:T(8,128)S(1)}, u32[]{:S(2)}, u32[]{:S(2)}) collective-permute-start(f32[1,16,384]{2,1,0:T(8,128)S(1)} %constant_dynamic-slice_fusion.1), channel_id=1, source_target_pairs={{0,17},{1,16},{2,19},{3,18},{4,21},{5,20},{6,23},{7,22},{8,25},{9,... | collective-permute-start | bytes 73736 | tf_op jit(solution)/shard_map/ppermute | solution.py:156
  15.5 0.2 %collective-permute-start.10 = (f32[1,8,384]{2,1,0:T(8,128)S(1)}, f32[1,8,384]{2,1,0:T(8,128)S(1)}, u32[]{:S(2)}, u32[]{:S(2)}) collective-permute-start(f32[1,8,384]{2,1,0:T(8,128)S(1)} %get-tuple-element.30), channel_id=1, source_target_pairs={{0,1},{1,0},{2,3},{3,2},{4,5},{5,4},{6,7},{7,6},{8,9},{9,8},{10,11... | collective-permute-start | bytes 36872 | tf_op jit(solution)/shard_map/ppermute | solution.py:156
  15.7 0.3 %collective-permute-start.9 = (f32[1,8,384]{2,1,0:T(8,128)S(1)}, f32[1,8,384]{2,1,0:T(8,128)S(1)}, u32[]{:S(2)}, u32[]{:S(2)}) collective-permute-start(f32[1,8,384]{2,1,0:T(8,128)S(1)} %get-tuple-element.29), channel_id=1, source_target_pairs={{0,1},{1,0},{2,3},{3,2},{4,5},{5,4},{6,7},{7,6},{8,9},{9,8},{10,11... | collective-permute-start | bytes 36872 | tf_op jit(solution)/shard_map/ppermute | solution.py:156
  16.0 0.7 %collective-permute-done.10 = f32[1,8,384]{2,1,0:T(8,128)S(1)} collective-permute-done((f32[1,8,384]{2,1,0:T(8,128)S(1)}, f32[1,8,384]{2,1,0:T(8,128)S(1)}, u32[]{:S(2)}, u32[]{:S(2)}) %collective-permute-start.10) | collective-permute-done | bytes 12320 | tf_op jit(solution)/shard_map/ppermute | solution.py:156
  16.7 0.2 %collective-permute-done.9 = f32[1,8,384]{2,1,0:T(8,128)S(1)} collective-permute-done((f32[1,8,384]{2,1,0:T(8,128)S(1)}, f32[1,8,384]{2,1,0:T(8,128)S(1)}, u32[]{:S(2)}, u32[]{:S(2)}) %collective-permute-start.9) | collective-permute-done | bytes 12320 | tf_op jit(solution)/shard_map/ppermute | solution.py:156
  16.9 0.3 %collective-permute-done.11 = f32[1,16,384]{2,1,0:T(8,128)S(1)} collective-permute-done((f32[1,16,384]{2,1,0:T(8,128)S(1)}, f32[1,16,384]{2,1,0:T(8,128)S(1)}, u32[]{:S(2)}, u32[]{:S(2)}) %collective-permute-start.11) | collective-permute-done | bytes 24608 | tf_op jit(solution)/shard_map/ppermute | solution.py:156
  17.1 0.6 %maximum_add_fusion.1 = f32[1,16,384]{2,1,0:T(8,128)} fusion(f32[1,16,384]{2,1,0:T(8,128)S(1)} %collective-permute-done.11, f32[1,8,384]{2,1,0:T(8,128)S(1)} %collective-permute-done.10, f32[1,8,384]{2,1,0:T(8,128)S(1)} %collective-permute-done.9), kind=kLoop, calls=%fused_computation.3 | loop fusion | flops 12288 | bytes 73728 | tf_op jit(solution)/shard_map/add | solution.py:250
  (17 shorter events, 0.2 us)
Async XLA Ops:
  0.0 4.2 %collective-permute-start = (f32[2,384]{1,0:T(2,128)}, f32[2,384]{1,0:T(2,128)S(1)}, u32[]{:S(2)}, u32[]{:S(2)}) collective-permute-start(f32[2,384]{1,0:T(2,128)} %wave_in.1), channel_id=1, source_target_pairs={{0,3},{1,2},{2,1},{3,0},{4,7},{5,6},{6,5},{7,4},{8,11},{9,10},{10,... | collective-permute-start | bytes 9224 | tf_op jit(solution)/shard_map/ppermute | solution.py:156
  2.4 3.1 %collective-permute-start.1 = (f32[2,384]{1,0:T(2,128)}, f32[2,384]{1,0:T(2,128)S(1)}, u32[]{:S(2)}, u32[]{:S(2)}) collective-permute-start(f32[2,384]{1,0:T(2,128)} %wave_in.1), channel_id=1, source_target_pairs={{0,1},{1,0},{2,3},{3,2},{4,5},{5,4},{6,7},{7,6},{8,9},{9,8},{10,11... | collective-permute-start | bytes 9224 | tf_op jit(solution)/shard_map/ppermute | solution.py:156
  3.1 1.5 %copy-start.2 = (s32[128,2]{0,1:T(2,128)S(1)}, s32[128,2]{0,1:T(2,128)}, u32[]{:S(2)}) copy-start(s32[128,2]{0,1:T(2,128)} %param.9) | copy-start | bytes 3076
  4.2 0.7 %copy-start = (f32[2,384]{1,0:T(2,128)S(1)}, f32[2,384]{1,0:T(2,128)}, u32[]{:S(2)}) copy-start(f32[2,384]{1,0:T(2,128)} %wave_in.1) | copy-start | bytes 9220
  4.3 1.3 %collective-permute-start.2 = (f32[2,384]{1,0:T(2,128)S(1)}, f32[2,384]{1,0:T(2,128)S(1)}, u32[]{:S(2)}, u32[]{:S(2)}) collective-permute-start(f32[2,384]{1,0:T(2,128)S(1)} %collective-permute-done.refs_3_), channel_id=1, source_target_pairs={{0,1},{1,0},{2,3},{3,2},{4,5},{5,4},{6,7},{7,6},{8,9},{9,8},{10,11... | collective-permute-start | bytes 9224 | tf_op jit(solution)/shard_map/ppermute | solution.py:156
  4.5 0.7 %copy-start.1 = (s32[128,2]{0,1:T(2,128)S(1)}, s32[128,2]{0,1:T(2,128)}, u32[]{:S(2)}) copy-start(s32[128,2]{0,1:T(2,128)} %param.8) | copy-start | bytes 3076
  4.5 0.7 %copy-start.3 = (f32[64]{0:T(128)S(1)}, f32[64]{0:T(128)}, u32[]{:S(2)}) copy-start(f32[64]{0:T(128)} %param.6) | copy-start | bytes 772
  6.5 4.4 %collective-permute-start.3 = (bf16[2,16,384]{2,1,0:T(8,128)(2,1)S(1)}, bf16[2,16,384]{2,1,0:T(8,128)(2,1)S(1)}, u32[]{:S(2)}, u32[]{:S(2)}) collective-permute-start(bf16[2,16,384]{2,1,0:T(8,128)(2,1)S(1)} %get-tuple-element.25), channel_id=1, source_target_pairs={{0,13},{1,12},{2,15},{3,14},{4,9},{5,8},{6,11},{7,10},{8,5},{9,4},... | collective-permute-start | bytes 73736 | tf_op jit(solution)/shard_map/ppermute | solution.py:156
  9.4 3.3 %collective-permute-start.8 = (bf16[2,16,384]{2,1,0:T(8,128)(2,1)S(1)}, bf16[2,16,384]{2,1,0:T(8,128)(2,1)S(1)}, u32[]{:S(2)}, u32[]{:S(2)}) collective-permute-start(bf16[2,16,384]{2,1,0:T(8,128)(2,1)S(1)} %get-tuple-element.28), channel_id=1, source_target_pairs={{0,9},{1,8},{2,11},{3,10},{4,13},{5,12},{6,15},{7,14},{8,1},{9,0},... | collective-permute-start | bytes 73736 | tf_op jit(solution)/shard_map/ppermute | solution.py:156
  9.6 3.3 %collective-permute-start.7 = (bf16[2,16,384]{2,1,0:T(8,128)(2,1)S(1)}, bf16[2,16,384]{2,1,0:T(8,128)(2,1)S(1)}, u32[]{:S(2)}, u32[]{:S(2)}) collective-permute-start(bf16[2,16,384]{2,1,0:T(8,128)(2,1)S(1)} %get-tuple-element.27), channel_id=1, source_target_pairs={{0,5},{1,4},{2,7},{3,6},{4,1},{5,0},{6,3},{7,2},{8,13},{9,12},{10,... | collective-permute-start | bytes 73736 | tf_op jit(solution)/shard_map/ppermute | solution.py:156
  10.9 2.0 %collective-permute-start.6 = (f32[2,16,128]{2,1,0:T(8,128)S(1)}, f32[2,16,128]{2,1,0:T(8,128)S(1)}, u32[]{:S(2)}, u32[]{:S(2)}) collective-permute-start(f32[2,16,128]{2,1,0:T(8,128)S(1)} %get-tuple-element.32), channel_id=1, source_target_pairs={{0,1},{1,0},{2,3},{3,2},{4,5},{5,4},{6,7},{7,6},{8,9},{9,8},{10,11... | collective-permute-start | bytes 49160 | tf_op jit(solution)/shard_map/ppermute | solution.py:156
  11.1 1.8 %collective-permute-start.5 = (f32[2,16,128]{2,1,0:T(8,128)S(1)}, f32[2,16,128]{2,1,0:T(8,128)S(1)}, u32[]{:S(2)}, u32[]{:S(2)}) collective-permute-start(f32[2,16,128]{2,1,0:T(8,128)S(1)} %get-tuple-element.33), channel_id=1, source_target_pairs={{0,1},{1,0},{2,3},{3,2},{4,5},{5,4},{6,7},{7,6},{8,9},{9,8},{10,11... | collective-permute-start | bytes 49160 | tf_op jit(solution)/shard_map/ppermute | solution.py:156
  11.4 1.5 %collective-permute-start.4 = (f32[2,16,128]{2,1,0:T(8,128)S(1)}, f32[2,16,128]{2,1,0:T(8,128)S(1)}, u32[]{:S(2)}, u32[]{:S(2)}) collective-permute-start(f32[2,16,128]{2,1,0:T(8,128)S(1)} %get-tuple-element.31), channel_id=1, source_target_pairs={{0,1},{1,0},{2,3},{3,2},{4,5},{5,4},{6,7},{7,6},{8,9},{9,8},{10,11... | collective-permute-start | bytes 49160 | tf_op jit(solution)/shard_map/ppermute | solution.py:156
  12.9 4.2 %collective-permute-start.11 = (f32[1,16,384]{2,1,0:T(8,128)S(1)}, f32[1,16,384]{2,1,0:T(8,128)S(1)}, u32[]{:S(2)}, u32[]{:S(2)}) collective-permute-start(f32[1,16,384]{2,1,0:T(8,128)S(1)} %constant_dynamic-slice_fusion.1), channel_id=1, source_target_pairs={{0,17},{1,16},{2,19},{3,18},{4,21},{5,20},{6,23},{7,22},{8,25},{9,... | collective-permute-start | bytes 73736 | tf_op jit(solution)/shard_map/ppermute | solution.py:156
  15.5 1.2 %collective-permute-start.10 = (f32[1,8,384]{2,1,0:T(8,128)S(1)}, f32[1,8,384]{2,1,0:T(8,128)S(1)}, u32[]{:S(2)}, u32[]{:S(2)}) collective-permute-start(f32[1,8,384]{2,1,0:T(8,128)S(1)} %get-tuple-element.30), channel_id=1, source_target_pairs={{0,1},{1,0},{2,3},{3,2},{4,5},{5,4},{6,7},{7,6},{8,9},{9,8},{10,11... | collective-permute-start | bytes 36872 | tf_op jit(solution)/shard_map/ppermute | solution.py:156
  15.7 1.2 %collective-permute-start.9 = (f32[1,8,384]{2,1,0:T(8,128)S(1)}, f32[1,8,384]{2,1,0:T(8,128)S(1)}, u32[]{:S(2)}, u32[]{:S(2)}) collective-permute-start(f32[1,8,384]{2,1,0:T(8,128)S(1)} %get-tuple-element.29), channel_id=1, source_target_pairs={{0,1},{1,0},{2,3},{3,2},{4,5},{5,4},{6,7},{7,6},{8,9},{9,8},{10,11... | collective-permute-start | bytes 36872 | tf_op jit(solution)/shard_map/ppermute | solution.py:156

commit v9 on v8

--- a/solution.py
+++ b/solution.py
@@ -46,7 +46,6 @@
 def stack_parts(parts, rows_ref, used_ref, shift_ref, hankel_ref, inverse_ref, out_refs):
     stations, groups, _, owned, templ_len = rows_ref.shape
     part_rows = groups * owned
-    all_rows = len(parts) * part_rows
     corr_len = inverse_ref.shape[1]
     out_len = out_refs[0].shape[2]
     lag_pairs, time_pairs = templ_len // PAIR, corr_len // PAIR
@@ -60,25 +59,32 @@
             window = jnp.concatenate(
                 [hankel_ref[s, :, at : at + PAIR], hankel_ref[s, :, at - LANES : at - LANES + PAIR]], axis=0
             )
-            left = jnp.concatenate([rows[:, j * PAIR : (j + 1) * PAIR] for j, _ in uses], axis=0)
-            product = jnp.dot(left, window, preferred_element_type=jnp.float32)
-            for k, (_, t) in enumerate(uses):
-                part = product[k * all_rows : (k + 1) * all_rows]
+            for j, t in uses:
+                part = jnp.dot(rows[:, j * PAIR : (j + 1) * PAIR], window, preferred_element_type=jnp.float32)
                 raw[t] = part if raw[t] is None else raw[t] + part
-        correlation = jnp.concatenate(raw, axis=1) * inverse_ref[s : s + 1, :]
-        wide = rows.astype(jnp.float32)
-        norm = lax.rsqrt(jnp.sum(wide * wide, axis=1, keepdims=True) + epsilon)
-        shift = jnp.concatenate([shift_ref[s, p] for p in parts], axis=0)
-        lane = lax.broadcasted_iota(jnp.int32, shift.shape, 1)
-        index = (PAIR - 1 - lane - shift) & (LANES - 1)
-        later = lane + shift < LANES
-        columns = [correlation[:, at : at + LANES] for at in range(0, corr_len, LANES)]
+        inverse = inverse_ref[s : s + 1, :]
         last = corr_len // LANES - 1
-        scale = norm * jnp.concatenate([used_ref[s, p] for p in parts], axis=0)
-        aligned = [
-            scale * lane_gather(jnp.where(later, columns[last - c], columns[last - 1 - c]), index)
-            for c in range(out_len // LANES)
-        ]
+        done = []
+        for number, p in enumerate(parts):
+            first, end = number * part_rows, (number + 1) * part_rows
+            wide = rows[first:end].astype(jnp.float32)
+            scale = lax.rsqrt(jnp.sum(wide * wide, axis=1, keepdims=True) + epsilon) * used_ref[s, p]
+            shift = shift_ref[s, p]
+            lane = lax.broadcasted_iota(jnp.int32, shift.shape, 1)
+            index = (PAIR - 1 - lane - shift) & (LANES - 1)
+            later = lane + shift < LANES
+            columns = [
+                values[first:end, at : at + LANES] * inverse[:, t * PAIR + at : t * PAIR + at + LANES]
+                for t, values in enumerate(raw)
+                for at in range(0, PAIR, LANES)
+            ]
+            done.append(
+                [
+                    lane_gather(scale * jnp.where(later, columns[last - c], columns[last - 1 - c]), index)
+                    for c in range(out_len // LANES)
+                ]
+            )
+        aligned = [jnp.concatenate([part[c] for part in done], axis=0) for c in range(out_len // LANES)]
         total = aligned if total is None else [a + b for a, b in zip(total, aligned)]
     for k, out_ref in enumerate(out_refs):
         for c, part in enumerate(total):

time: 17.9 us -> 17.9 us (level)
  transfers between devices with their start and end apart: 12 -> 12, of which waited for: 6 -> 6; matrix products, arithmetic and copies ran while one was open for 7% -> 7% of each run, Pallas kernels for 4% -> 5%
where the time goes in v9:
time: 17.9 us; the launch traced here: 17.7 us
  starting transfers between devices  10.4 us (58%)
  waiting for transfers between devices  2.95 us (16%)
  local copies, waits for them, and re-layouts  1.87 us (10%)
  Pallas kernels  1.79 us (10%)
  other arithmetic  0.63 us (4%)
    ppermute x12, starting transfers between devices, flip(): return lax.ppermute(value, ('sta', 'tpl'), pairs)  10.4 us
    ppermute x12, waiting for transfers between devices, flip(): return lax.ppermute(value, ('sta', 'tpl'), pairs)  2.95 us
    transpose x1, local copies, waits for them, and re-layouts, shards(): templates.transpose(1, 0, 2)  1.16 us
    pallas_call x1, Pallas kernels, shards(): pl.pallas_call(functools.partial(send_kernel, segments), out_shape=(*[jax...  0.97 us
    unnamed x8, local copies, waits for them, and re-layouts  0.68 us
    add x2, other arithmetic, shards(): stack = stack + piece.astype(jnp.float32)  0.63 us
    pallas_call x1, Pallas kernels, shards(): pl.pallas_call(keep_kernel, out_shape=jax.ShapeDtypeStruct((owners // par...  0.55 us
  transfers between devices with their start and end apart: 12, of which 6 were waited for; matrix products, arithmetic and copies ran while one was open for 7% of the time, Pallas kernels for 5%

profile of v9, /device:TPU:0, one launch (start us, length us, event | category | flops | bytes accessed | tf_op | source)
XLA Modules:
  0.0 17.7 jit_solution(16370407623550827753)
XLA Ops:
  0.0 2.4 %collective-permute-start = (f32[2,384]{1,0:T(2,128)}, f32[2,384]{1,0:T(2,128)S(1)}, u32[]{:S(2)}, u32[]{:S(2)}) collective-permute-start(f32[2,384]{1,0:T(2,128)} %wave_in.1), channel_id=1, source_target_pairs={{0,3},{1,2},{2,1},{3,0},{4,7},{5,6},{6,5},{7,4},{8,11},{9,10},{10,... | collective-permute-start | bytes 9224 | tf_op jit(solution)/shard_map/ppermute | solution.py:162
  2.4 0.7 %collective-permute-start.1 = (f32[2,384]{1,0:T(2,128)}, f32[2,384]{1,0:T(2,128)S(1)}, u32[]{:S(2)}, u32[]{:S(2)}) collective-permute-start(f32[2,384]{1,0:T(2,128)} %wave_in.1), channel_id=1, source_target_pairs={{0,1},{1,0},{2,3},{3,2},{4,5},{5,4},{6,7},{7,6},{8,9},{9,8},{10,11... | collective-permute-start | bytes 9224 | tf_op jit(solution)/shard_map/ppermute | solution.py:162
  3.1 1.2 %copy.6 = bf16[2,128,1024]{2,1,0:T(8,128)(2,1)S(1)} copy(bf16[2,128,1024]{2,0,1:T(2,128)(2,1)} %bitcast.10) | data formatting | bytes 1048576 | tf_op jit(solution)/shard_map/transpose | solution.py:180
  4.3 0.3 %collective-permute-start.2 = (f32[2,384]{1,0:T(2,128)S(1)}, f32[2,384]{1,0:T(2,128)S(1)}, u32[]{:S(2)}, u32[]{:S(2)}) collective-permute-start(f32[2,384]{1,0:T(2,128)S(1)} %collective-permute-done.refs_3_), channel_id=1, source_target_pairs={{0,1},{1,0},{2,3},{3,2},{4,5},{5,4},{6,7},{7,6},{8,9},{9,8},{10,11... | collective-permute-start | bytes 9224 | tf_op jit(solution)/shard_map/ppermute | solution.py:162
  4.6 0.4 %copy-done = f32[2,384]{1,0:T(2,128)S(1)} copy-done((f32[2,384]{1,0:T(2,128)S(1)}, f32[2,384]{1,0:T(2,128)}, u32[]{:S(2)}) %copy-start) | copy-done | bytes 3096
  4.9 0.3 %copy-done.1 = s32[128,2]{0,1:T(2,128)S(1)} copy-done((s32[128,2]{0,1:T(2,128)S(1)}, s32[128,2]{0,1:T(2,128)}, u32[]{:S(2)}) %copy-start.1) | copy-done | bytes 1048
  5.2 0.3 %columns.1 = (f32[2,384]{1,0:T(2,128)S(1)}, f32[256,128]{1,0:T(8,128)S(1)}, f32[2,4,32,128]{3,2,1,0:T(8,128)S(1)}, s32[2,4,32,128]{3,2,1,0:T(8,128)S(1)}) custom-call(f32[2,384]{1,0:T(2,128)S(1)} %copy-done, f32[1,64]{1,0:T(1,128)S(1)} %bitcast.9, s32[2,128]{1,0:T(2,128)S(1)} %bitcast.7, s32[2,128]{1,0:T(2,128)S(1)} %bitcast.8), custom_call_target="tpu_custom_call" | custom-call | flops 1048576 | bytes 1048576 | tf_op jit(solution)/shard_map/columns/pallas_call | solution.py:181
  5.5 1.0 %send_parts.1 = (bf16[2,16,384]{2,1,0:T(8,128)(2,1)S(1)}, bf16[2,16,384]{2,1,0:T(8,128)(2,1)S(1)}, bf16[2,16,384]{2,1,0:T(8,128)(2,1)S(1)}, bf16[2,128,1536]{2,1,0:T(8,128)(2,1)S(1)}, f32[2,512]{1,0:T(2,128)S(1)}) custom-call(f32[2,384]{1,0:T(2,128)S(1)} %get-tuple-element.20.refs_0_, f32[2,384]{1,0:T(2,128)S(1)} %collective-permute-done.1.refs_1_, ...), custom_call_target="tpu_custom_call" | custom-call | flops 1048576 | bytes 1048576 | tf_op jit(solution)/shard_map/send_parts/pallas_call | solution.py:205
  6.5 2.8 %collective-permute-start.3 = (bf16[2,16,384]{2,1,0:T(8,128)(2,1)S(1)}, bf16[2,16,384]{2,1,0:T(8,128)(2,1)S(1)}, u32[]{:S(2)}, u32[]{:S(2)}) collective-permute-start(bf16[2,16,384]{2,1,0:T(8,128)(2,1)S(1)} %get-tuple-element.25), channel_id=1, source_target_pairs={{0,13},{1,12},{2,15},{3,14},{4,9},{5,8},{6,11},{7,10},{8,5},{9,4},... | collective-permute-start | bytes 73736 | tf_op jit(solution)/shard_map/ppermute | solution.py:162
  9.3 0.2 %collective-permute-start.8 = (bf16[2,16,384]{2,1,0:T(8,128)(2,1)S(1)}, bf16[2,16,384]{2,1,0:T(8,128)(2,1)S(1)}, u32[]{:S(2)}, u32[]{:S(2)}) collective-permute-start(bf16[2,16,384]{2,1,0:T(8,128)(2,1)S(1)} %get-tuple-element.28), channel_id=1, source_target_pairs={{0,9},{1,8},{2,11},{3,10},{4,13},{5,12},{6,15},{7,14},{8,1},{9,0},... | collective-permute-start | bytes 73736 | tf_op jit(solution)/shard_map/ppermute | solution.py:162
  9.6 0.2 %collective-permute-start.7 = (bf16[2,16,384]{2,1,0:T(8,128)(2,1)S(1)}, bf16[2,16,384]{2,1,0:T(8,128)(2,1)S(1)}, u32[]{:S(2)}, u32[]{:S(2)}) collective-permute-start(bf16[2,16,384]{2,1,0:T(8,128)(2,1)S(1)} %get-tuple-element.27), channel_id=1, source_target_pairs={{0,5},{1,4},{2,7},{3,6},{4,1},{5,0},{6,3},{7,2},{8,13},{9,12},{10,... | collective-permute-start | bytes 73736 | tf_op jit(solution)/shard_map/ppermute | solution.py:162
  9.8 0.5 %keep_part.1 = f32[2,16,384]{2,1,0:T(8,128)S(1)} custom-call(bf16[2,2,4,16,1024]{4,3,2,1,0:T(8,128)(2,1)S(1)} %bitcast.6, f32[2,4,32,128]{3,2,1,0:T(8,128)S(1)} %get-tuple-element.18.refs_6_.used_ref, s32[2,4,32,128]{3,2,1,0:T(8,128)S(1)} %get-tuple-element.19.refs_7_.shift_ref, bf16[2,128,1536]{2,1,0:T(8,128)(2,1)S(1)} %get-tuple-element.23.hankel_ref, ...), custom_call_target="tpu_custom_call" | custom-call | flops 1048576 | bytes 1048576 | tf_op jit(solution)/shard_map/keep_part/pallas_call | solution.py:223
  10.3 0.5 %collective-permute-done.3 = bf16[2,16,384]{2,1,0:T(8,128)(2,1)S(1)} collective-permute-done((bf16[2,16,384]{2,1,0:T(8,128)(2,1)S(1)}, bf16[2,16,384]{2,1,0:T(8,128)(2,1)S(1)}, u32[]{:S(2)}, u32[]{:S(2)}) %collective-permute-start.3) | collective-permute-done | bytes 24608 | tf_op jit(solution)/shard_map/ppermute | solution.py:162
  10.9 0.2 %collective-permute-start.6 = (f32[2,16,128]{2,1,0:T(8,128)S(1)}, f32[2,16,128]{2,1,0:T(8,128)S(1)}, u32[]{:S(2)}, u32[]{:S(2)}) collective-permute-start(f32[2,16,128]{2,1,0:T(8,128)S(1)} %get-tuple-element.32), channel_id=1, source_target_pairs={{0,1},{1,0},{2,3},{3,2},{4,5},{5,4},{6,7},{7,6},{8,9},{9,8},{10,11... | collective-permute-start | bytes 49160 | tf_op jit(solution)/shard_map/ppermute | solution.py:162
  11.0 0.3 %collective-permute-start.5 = (f32[2,16,128]{2,1,0:T(8,128)S(1)}, f32[2,16,128]{2,1,0:T(8,128)S(1)}, u32[]{:S(2)}, u32[]{:S(2)}) collective-permute-start(f32[2,16,128]{2,1,0:T(8,128)S(1)} %get-tuple-element.33), channel_id=1, source_target_pairs={{0,1},{1,0},{2,3},{3,2},{4,5},{5,4},{6,7},{7,6},{8,9},{9,8},{10,11... | collective-permute-start | bytes 49160 | tf_op jit(solution)/shard_map/ppermute | solution.py:162
  11.6 1.0 %collective-permute-done.8 = bf16[2,16,384]{2,1,0:T(8,128)(2,1)S(1)} collective-permute-done((bf16[2,16,384]{2,1,0:T(8,128)(2,1)S(1)}, bf16[2,16,384]{2,1,0:T(8,128)(2,1)S(1)}, u32[]{:S(2)}, u32[]{:S(2)}) %collective-permute-start.8) | collective-permute-done | bytes 24608 | tf_op jit(solution)/shard_map/ppermute | solution.py:162
  12.6 0.2 %collective-permute-done.7 = bf16[2,16,384]{2,1,0:T(8,128)(2,1)S(1)} collective-permute-done((bf16[2,16,384]{2,1,0:T(8,128)(2,1)S(1)}, bf16[2,16,384]{2,1,0:T(8,128)(2,1)S(1)}, u32[]{:S(2)}, u32[]{:S(2)}) %collective-permute-start.7) | collective-permute-done | bytes 24608 | tf_op jit(solution)/shard_map/ppermute | solution.py:162
  12.9 2.6 %collective-permute-start.11 = (f32[1,16,384]{2,1,0:T(8,128)S(1)}, f32[1,16,384]{2,1,0:T(8,128)S(1)}, u32[]{:S(2)}, u32[]{:S(2)}) collective-permute-start(f32[1,16,384]{2,1,0:T(8,128)S(1)} %constant_dynamic-slice_fusion.1), channel_id=1, source_target_pairs={{0,17},{1,16},{2,19},{3,18},{4,21},{5,20},{6,23},{7,22},{8,25},{9,... | collective-permute-start | bytes 73736 | tf_op jit(solution)/shard_map/ppermute | solution.py:162
  15.5 0.2 %collective-permute-start.10 = (f32[1,8,384]{2,1,0:T(8,128)S(1)}, f32[1,8,384]{2,1,0:T(8,128)S(1)}, u32[]{:S(2)}, u32[]{:S(2)}) collective-permute-start(f32[1,8,384]{2,1,0:T(8,128)S(1)} %get-tuple-element.30), channel_id=1, source_target_pairs={{0,1},{1,0},{2,3},{3,2},{4,5},{5,4},{6,7},{7,6},{8,9},{9,8},{10,11... | collective-permute-start | bytes 36872 | tf_op jit(solution)/shard_map/ppermute | solution.py:162
  15.7 0.3 %collective-permute-start.9 = (f32[1,8,384]{2,1,0:T(8,128)S(1)}, f32[1,8,384]{2,1,0:T(8,128)S(1)}, u32[]{:S(2)}, u32[]{:S(2)}) collective-permute-start(f32[1,8,384]{2,1,0:T(8,128)S(1)} %get-tuple-element.29), channel_id=1, source_target_pairs={{0,1},{1,0},{2,3},{3,2},{4,5},{5,4},{6,7},{7,6},{8,9},{9,8},{10,11... | collective-permute-start | bytes 36872 | tf_op jit(solution)/shard_map/ppermute | solution.py:162
  16.0 0.7 %collective-permute-done.10 = f32[1,8,384]{2,1,0:T(8,128)S(1)} collective-permute-done((f32[1,8,384]{2,1,0:T(8,128)S(1)}, f32[1,8,384]{2,1,0:T(8,128)S(1)}, u32[]{:S(2)}, u32[]{:S(2)}) %collective-permute-start.10) | collective-permute-done | bytes 12320 | tf_op jit(solution)/shard_map/ppermute | solution.py:162
  16.7 0.2 %collective-permute-done.9 = f32[1,8,384]{2,1,0:T(8,128)S(1)} collective-permute-done((f32[1,8,384]{2,1,0:T(8,128)S(1)}, f32[1,8,384]{2,1,0:T(8,128)S(1)}, u32[]{:S(2)}, u32[]{:S(2)}) %collective-permute-start.9) | collective-permute-done | bytes 12320 | tf_op jit(solution)/shard_map/ppermute | solution.py:162
  16.8 0.3 %collective-permute-done.11 = f32[1,16,384]{2,1,0:T(8,128)S(1)} collective-permute-done((f32[1,16,384]{2,1,0:T(8,128)S(1)}, f32[1,16,384]{2,1,0:T(8,128)S(1)}, u32[]{:S(2)}, u32[]{:S(2)}) %collective-permute-start.11) | collective-permute-done | bytes 24608 | tf_op jit(solution)/shard_map/ppermute | solution.py:162
  17.1 0.6 %maximum_add_fusion.1 = f32[1,16,384]{2,1,0:T(8,128)} fusion(f32[1,16,384]{2,1,0:T(8,128)S(1)} %collective-permute-done.11, f32[1,8,384]{2,1,0:T(8,128)S(1)} %collective-permute-done.10, f32[1,8,384]{2,1,0:T(8,128)S(1)} %collective-permute-done.9), kind=kLoop, calls=%fused_computation.3 | loop fusion | flops 12288 | bytes 73728 | tf_op jit(solution)/shard_map/add | solution.py:256
  (17 shorter events, 0.2 us)
Async XLA Ops:
  0.0 4.2 %collective-permute-start = (f32[2,384]{1,0:T(2,128)}, f32[2,384]{1,0:T(2,128)S(1)}, u32[]{:S(2)}, u32[]{:S(2)}) collective-permute-start(f32[2,384]{1,0:T(2,128)} %wave_in.1), channel_id=1, source_target_pairs={{0,3},{1,2},{2,1},{3,0},{4,7},{5,6},{6,5},{7,4},{8,11},{9,10},{10,... | collective-permute-start | bytes 9224 | tf_op jit(solution)/shard_map/ppermute | solution.py:162
  2.4 3.1 %collective-permute-start.1 = (f32[2,384]{1,0:T(2,128)}, f32[2,384]{1,0:T(2,128)S(1)}, u32[]{:S(2)}, u32[]{:S(2)}) collective-permute-start(f32[2,384]{1,0:T(2,128)} %wave_in.1), channel_id=1, source_target_pairs={{0,1},{1,0},{2,3},{3,2},{4,5},{5,4},{6,7},{7,6},{8,9},{9,8},{10,11... | collective-permute-start | bytes 9224 | tf_op jit(solution)/shard_map/ppermute | solution.py:162
  3.1 1.5 %copy-start.2 = (s32[128,2]{0,1:T(2,128)S(1)}, s32[128,2]{0,1:T(2,128)}, u32[]{:S(2)}) copy-start(s32[128,2]{0,1:T(2,128)} %param.9) | copy-start | bytes 3076
  4.2 0.7 %copy-start = (f32[2,384]{1,0:T(2,128)S(1)}, f32[2,384]{1,0:T(2,128)}, u32[]{:S(2)}) copy-start(f32[2,384]{1,0:T(2,128)} %wave_in.1) | copy-start | bytes 9220
  4.3 1.3 %collective-permute-start.2 = (f32[2,384]{1,0:T(2,128)S(1)}, f32[2,384]{1,0:T(2,128)S(1)}, u32[]{:S(2)}, u32[]{:S(2)}) collective-permute-start(f32[2,384]{1,0:T(2,128)S(1)} %collective-permute-done.refs_3_), channel_id=1, source_target_pairs={{0,1},{1,0},{2,3},{3,2},{4,5},{5,4},{6,7},{7,6},{8,9},{9,8},{10,11... | collective-permute-start | bytes 9224 | tf_op jit(solution)/shard_map/ppermute | solution.py:162
  4.5 0.7 %copy-start.1 = (s32[128,2]{0,1:T(2,128)S(1)}, s32[128,2]{0,1:T(2,128)}, u32[]{:S(2)}) copy-start(s32[128,2]{0,1:T(2,128)} %param.8) | copy-start | bytes 3076
  4.5 0.7 %copy-start.3 = (f32[64]{0:T(128)S(1)}, f32[64]{0:T(128)}, u32[]{:S(2)}) copy-start(f32[64]{0:T(128)} %param.6) | copy-start | bytes 772
  6.5 4.4 %collective-permute-start.3 = (bf16[2,16,384]{2,1,0:T(8,128)(2,1)S(1)}, bf16[2,16,384]{2,1,0:T(8,128)(2,1)S(1)}, u32[]{:S(2)}, u32[]{:S(2)}) collective-permute-start(bf16[2,16,384]{2,1,0:T(8,128)(2,1)S(1)} %get-tuple-element.25), channel_id=1, source_target_pairs={{0,13},{1,12},{2,15},{3,14},{4,9},{5,8},{6,11},{7,10},{8,5},{9,4},... | collective-permute-start | bytes 73736 | tf_op jit(solution)/shard_map/ppermute | solution.py:162
  9.3 3.3 %collective-permute-start.8 = (bf16[2,16,384]{2,1,0:T(8,128)(2,1)S(1)}, bf16[2,16,384]{2,1,0:T(8,128)(2,1)S(1)}, u32[]{:S(2)}, u32[]{:S(2)}) collective-permute-start(bf16[2,16,384]{2,1,0:T(8,128)(2,1)S(1)} %get-tuple-element.28), channel_id=1, source_target_pairs={{0,9},{1,8},{2,11},{3,10},{4,13},{5,12},{6,15},{7,14},{8,1},{9,0},... | collective-permute-start | bytes 73736 | tf_op jit(solution)/shard_map/ppermute | solution.py:162
  9.6 3.3 %collective-permute-start.7 = (bf16[2,16,384]{2,1,0:T(8,128)(2,1)S(1)}, bf16[2,16,384]{2,1,0:T(8,128)(2,1)S(1)}, u32[]{:S(2)}, u32[]{:S(2)}) collective-permute-start(bf16[2,16,384]{2,1,0:T(8,128)(2,1)S(1)} %get-tuple-element.27), channel_id=1, source_target_pairs={{0,5},{1,4},{2,7},{3,6},{4,1},{5,0},{6,3},{7,2},{8,13},{9,12},{10,... | collective-permute-start | bytes 73736 | tf_op jit(solution)/shard_map/ppermute | solution.py:162
  10.9 2.0 %collective-permute-start.6 = (f32[2,16,128]{2,1,0:T(8,128)S(1)}, f32[2,16,128]{2,1,0:T(8,128)S(1)}, u32[]{:S(2)}, u32[]{:S(2)}) collective-permute-start(f32[2,16,128]{2,1,0:T(8,128)S(1)} %get-tuple-element.32), channel_id=1, source_target_pairs={{0,1},{1,0},{2,3},{3,2},{4,5},{5,4},{6,7},{7,6},{8,9},{9,8},{10,11... | collective-permute-start | bytes 49160 | tf_op jit(solution)/shard_map/ppermute | solution.py:162
  11.0 1.8 %collective-permute-start.5 = (f32[2,16,128]{2,1,0:T(8,128)S(1)}, f32[2,16,128]{2,1,0:T(8,128)S(1)}, u32[]{:S(2)}, u32[]{:S(2)}) collective-permute-start(f32[2,16,128]{2,1,0:T(8,128)S(1)} %get-tuple-element.33), channel_id=1, source_target_pairs={{0,1},{1,0},{2,3},{3,2},{4,5},{5,4},{6,7},{7,6},{8,9},{9,8},{10,11... | collective-permute-start | bytes 49160 | tf_op jit(solution)/shard_map/ppermute | solution.py:162
  11.4 1.5 %collective-permute-start.4 = (f32[2,16,128]{2,1,0:T(8,128)S(1)}, f32[2,16,128]{2,1,0:T(8,128)S(1)}, u32[]{:S(2)}, u32[]{:S(2)}) collective-permute-start(f32[2,16,128]{2,1,0:T(8,128)S(1)} %get-tuple-element.31), channel_id=1, source_target_pairs={{0,1},{1,0},{2,3},{3,2},{4,5},{5,4},{6,7},{7,6},{8,9},{9,8},{10,11... | collective-permute-start | bytes 49160 | tf_op jit(solution)/shard_map/ppermute | solution.py:162
  12.9 4.2 %collective-permute-start.11 = (f32[1,16,384]{2,1,0:T(8,128)S(1)}, f32[1,16,384]{2,1,0:T(8,128)S(1)}, u32[]{:S(2)}, u32[]{:S(2)}) collective-permute-start(f32[1,16,384]{2,1,0:T(8,128)S(1)} %constant_dynamic-slice_fusion.1), channel_id=1, source_target_pairs={{0,17},{1,16},{2,19},{3,18},{4,21},{5,20},{6,23},{7,22},{8,25},{9,... | collective-permute-start | bytes 73736 | tf_op jit(solution)/shard_map/ppermute | solution.py:162
  15.5 1.2 %collective-permute-start.10 = (f32[1,8,384]{2,1,0:T(8,128)S(1)}, f32[1,8,384]{2,1,0:T(8,128)S(1)}, u32[]{:S(2)}, u32[]{:S(2)}) collective-permute-start(f32[1,8,384]{2,1,0:T(8,128)S(1)} %get-tuple-element.30), channel_id=1, source_target_pairs={{0,1},{1,0},{2,3},{3,2},{4,5},{5,4},{6,7},{7,6},{8,9},{9,8},{10,11... | collective-permute-start | bytes 36872 | tf_op jit(solution)/shard_map/ppermute | solution.py:162
  15.7 1.2 %collective-permute-start.9 = (f32[1,8,384]{2,1,0:T(8,128)S(1)}, f32[1,8,384]{2,1,0:T(8,128)S(1)}, u32[]{:S(2)}, u32[]{:S(2)}) collective-permute-start(f32[1,8,384]{2,1,0:T(8,128)S(1)} %get-tuple-element.29), channel_id=1, source_target_pairs={{0,1},{1,0},{2,3},{3,2},{4,5},{5,4},{6,7},{7,6},{8,9},{9,8},{10,11... | collective-permute-start | bytes 36872 | tf_op jit(solution)/shard_map/ppermute | solution.py:162

commit v10 on v9

--- a/solution.py
+++ b/solution.py
@@ -59,8 +59,13 @@
             window = jnp.concatenate(
                 [hankel_ref[s, :, at : at + PAIR], hankel_ref[s, :, at - LANES : at - LANES + PAIR]], axis=0
             )
-            for j, t in uses:
-                part = jnp.dot(rows[:, j * PAIR : (j + 1) * PAIR], window, preferred_element_type=jnp.float32)
+            left = [rows[:, j * PAIR : (j + 1) * PAIR] for j, _ in uses]
+            if len(parts) == 1:
+                product = jnp.dot(jnp.concatenate(left, axis=0), window, preferred_element_type=jnp.float32)
+                made = [product[k * part_rows : (k + 1) * part_rows] for k in range(len(uses))]
+            else:
+                made = [jnp.dot(values, window, preferred_element_type=jnp.float32) for values in left]
+            for (_, t), part in zip(uses, made):
                 raw[t] = part if raw[t] is None else raw[t] + part
         inverse = inverse_ref[s : s + 1, :]
         last = corr_len // LANES - 1

time: 17.9 us -> 17.9 us (level)
  transfers between devices with their start and end apart: 12 -> 12, of which waited for: 6 -> 6; matrix products, arithmetic and copies ran while one was open for 7% -> 7% of each run, Pallas kernels for 5% -> 4%
where the time goes in v10:
time: 17.9 us; the launch traced here: 17.7 us
  starting transfers between devices  10.4 us (58%)
  waiting for transfers between devices  3.09 us (17%)
  local copies, waits for them, and re-layouts  1.87 us (10%)
  Pallas kernels  1.65 us (9%)
  other arithmetic  0.63 us (4%)
    ppermute x12, starting transfers between devices, flip(): return lax.ppermute(value, ('sta', 'tpl'), pairs)  10.4 us
    ppermute x12, waiting for transfers between devices, flip(): return lax.ppermute(value, ('sta', 'tpl'), pairs)  3.09 us
    transpose x1, local copies, waits for them, and re-layouts, shards(): templates.transpose(1, 0, 2)  1.16 us
    pallas_call x1, Pallas kernels, shards(): pl.pallas_call(functools.partial(send_kernel, segments), out_shape=(*[jax...  0.97 us
    unnamed x8, local copies, waits for them, and re-layouts  0.68 us
    add x2, other arithmetic, shards(): stack = stack + piece.astype(jnp.float32)  0.63 us
    pallas_call x1, Pallas kernels, shards(): pl.pallas_call(keep_kernel, out_shape=jax.ShapeDtypeStruct((owners // par...  0.41 us
  transfers between devices with their start and end apart: 12, of which 6 were waited for; matrix products, arithmetic and copies ran while one was open for 7% of the time, Pallas kernels for 4%

profile of v10, /device:TPU:0, one launch (start us, length us, event | category | flops | bytes accessed | tf_op | source)
XLA Modules:
  0.0 17.7 jit_solution(670829021144103198)
XLA Ops:
  0.0 2.4 %collective-permute-start = (f32[2,384]{1,0:T(2,128)}, f32[2,384]{1,0:T(2,128)S(1)}, u32[]{:S(2)}, u32[]{:S(2)}) collective-permute-start(f32[2,384]{1,0:T(2,128)} %wave_in.1), channel_id=1, source_target_pairs={{0,3},{1,2},{2,1},{3,0},{4,7},{5,6},{6,5},{7,4},{8,11},{9,10},{10,... | collective-permute-start | bytes 9224 | tf_op jit(solution)/shard_map/ppermute | solution.py:167
  2.4 0.7 %collective-permute-start.1 = (f32[2,384]{1,0:T(2,128)}, f32[2,384]{1,0:T(2,128)S(1)}, u32[]{:S(2)}, u32[]{:S(2)}) collective-permute-start(f32[2,384]{1,0:T(2,128)} %wave_in.1), channel_id=1, source_target_pairs={{0,1},{1,0},{2,3},{3,2},{4,5},{5,4},{6,7},{7,6},{8,9},{9,8},{10,11... | collective-permute-start | bytes 9224 | tf_op jit(solution)/shard_map/ppermute | solution.py:167
  3.1 1.2 %copy.6 = bf16[2,128,1024]{2,1,0:T(8,128)(2,1)S(1)} copy(bf16[2,128,1024]{2,0,1:T(2,128)(2,1)} %bitcast.10) | data formatting | bytes 1048576 | tf_op jit(solution)/shard_map/transpose | solution.py:185
  4.3 0.3 %collective-permute-start.2 = (f32[2,384]{1,0:T(2,128)S(1)}, f32[2,384]{1,0:T(2,128)S(1)}, u32[]{:S(2)}, u32[]{:S(2)}) collective-permute-start(f32[2,384]{1,0:T(2,128)S(1)} %collective-permute-done.refs_3_), channel_id=1, source_target_pairs={{0,1},{1,0},{2,3},{3,2},{4,5},{5,4},{6,7},{7,6},{8,9},{9,8},{10,11... | collective-permute-start | bytes 9224 | tf_op jit(solution)/shard_map/ppermute | solution.py:167
  4.6 0.4 %copy-done = f32[2,384]{1,0:T(2,128)S(1)} copy-done((f32[2,384]{1,0:T(2,128)S(1)}, f32[2,384]{1,0:T(2,128)}, u32[]{:S(2)}) %copy-start) | copy-done | bytes 3096
  4.9 0.3 %copy-done.1 = s32[128,2]{0,1:T(2,128)S(1)} copy-done((s32[128,2]{0,1:T(2,128)S(1)}, s32[128,2]{0,1:T(2,128)}, u32[]{:S(2)}) %copy-start.1) | copy-done | bytes 1048
  5.2 0.3 %columns.1 = (f32[2,384]{1,0:T(2,128)S(1)}, f32[256,128]{1,0:T(8,128)S(1)}, f32[2,4,32,128]{3,2,1,0:T(8,128)S(1)}, s32[2,4,32,128]{3,2,1,0:T(8,128)S(1)}) custom-call(f32[2,384]{1,0:T(2,128)S(1)} %copy-done, f32[1,64]{1,0:T(1,128)S(1)} %bitcast.9, s32[2,128]{1,0:T(2,128)S(1)} %bitcast.7, s32[2,128]{1,0:T(2,128)S(1)} %bitcast.8), custom_call_target="tpu_custom_call" | custom-call | flops 1048576 | bytes 1048576 | tf_op jit(solution)/shard_map/columns/pallas_call | solution.py:186
  5.5 1.0 %send_parts.1 = (bf16[2,16,384]{2,1,0:T(8,128)(2,1)S(1)}, bf16[2,16,384]{2,1,0:T(8,128)(2,1)S(1)}, bf16[2,16,384]{2,1,0:T(8,128)(2,1)S(1)}, bf16[2,128,1536]{2,1,0:T(8,128)(2,1)S(1)}, f32[2,512]{1,0:T(2,128)S(1)}) custom-call(f32[2,384]{1,0:T(2,128)S(1)} %get-tuple-element.20.refs_0_, f32[2,384]{1,0:T(2,128)S(1)} %collective-permute-done.1.refs_1_, ...), custom_call_target="tpu_custom_call" | custom-call | flops 1048576 | bytes 1048576 | tf_op jit(solution)/shard_map/send_parts/pallas_call | solution.py:210
  6.5 2.8 %collective-permute-start.3 = (bf16[2,16,384]{2,1,0:T(8,128)(2,1)S(1)}, bf16[2,16,384]{2,1,0:T(8,128)(2,1)S(1)}, u32[]{:S(2)}, u32[]{:S(2)}) collective-permute-start(bf16[2,16,384]{2,1,0:T(8,128)(2,1)S(1)} %get-tuple-element.25), channel_id=1, source_target_pairs={{0,13},{1,12},{2,15},{3,14},{4,9},{5,8},{6,11},{7,10},{8,5},{9,4},... | collective-permute-start | bytes 73736 | tf_op jit(solution)/shard_map/ppermute | solution.py:167
  9.3 0.2 %collective-permute-start.8 = (bf16[2,16,384]{2,1,0:T(8,128)(2,1)S(1)}, bf16[2,16,384]{2,1,0:T(8,128)(2,1)S(1)}, u32[]{:S(2)}, u32[]{:S(2)}) collective-permute-start(bf16[2,16,384]{2,1,0:T(8,128)(2,1)S(1)} %get-tuple-element.28), channel_id=1, source_target_pairs={{0,9},{1,8},{2,11},{3,10},{4,13},{5,12},{6,15},{7,14},{8,1},{9,0},... | collective-permute-start | bytes 73736 | tf_op jit(solution)/shard_map/ppermute | solution.py:167
  9.6 0.2 %collective-permute-start.7 = (bf16[2,16,384]{2,1,0:T(8,128)(2,1)S(1)}, bf16[2,16,384]{2,1,0:T(8,128)(2,1)S(1)}, u32[]{:S(2)}, u32[]{:S(2)}) collective-permute-start(bf16[2,16,384]{2,1,0:T(8,128)(2,1)S(1)} %get-tuple-element.27), channel_id=1, source_target_pairs={{0,5},{1,4},{2,7},{3,6},{4,1},{5,0},{6,3},{7,2},{8,13},{9,12},{10,... | collective-permute-start | bytes 73736 | tf_op jit(solution)/shard_map/ppermute | solution.py:167
  9.8 0.4 %keep_part.1 = f32[2,16,384]{2,1,0:T(8,128)S(1)} custom-call(bf16[2,2,4,16,1024]{4,3,2,1,0:T(8,128)(2,1)S(1)} %bitcast.6, f32[2,4,32,128]{3,2,1,0:T(8,128)S(1)} %get-tuple-element.18.refs_6_.used_ref, s32[2,4,32,128]{3,2,1,0:T(8,128)S(1)} %get-tuple-element.19.refs_7_.shift_ref, bf16[2,128,1536]{2,1,0:T(8,128)(2,1)S(1)} %get-tuple-element.23.hankel_ref, ...), custom_call_target="tpu_custom_call" | custom-call | flops 1048576 | bytes 1048576 | tf_op jit(solution)/shard_map/keep_part/pallas_call | solution.py:228
  10.2 0.7 %collective-permute-done.3 = bf16[2,16,384]{2,1,0:T(8,128)(2,1)S(1)} collective-permute-done((bf16[2,16,384]{2,1,0:T(8,128)(2,1)S(1)}, bf16[2,16,384]{2,1,0:T(8,128)(2,1)S(1)}, u32[]{:S(2)}, u32[]{:S(2)}) %collective-permute-start.3) | collective-permute-done | bytes 24608 | tf_op jit(solution)/shard_map/ppermute | solution.py:167
  10.9 0.2 %collective-permute-start.6 = (f32[2,16,128]{2,1,0:T(8,128)S(1)}, f32[2,16,128]{2,1,0:T(8,128)S(1)}, u32[]{:S(2)}, u32[]{:S(2)}) collective-permute-start(f32[2,16,128]{2,1,0:T(8,128)S(1)} %get-tuple-element.32), channel_id=1, source_target_pairs={{0,1},{1,0},{2,3},{3,2},{4,5},{5,4},{6,7},{7,6},{8,9},{9,8},{10,11... | collective-permute-start | bytes 49160 | tf_op jit(solution)/shard_map/ppermute | solution.py:167
  11.0 0.3 %collective-permute-start.5 = (f32[2,16,128]{2,1,0:T(8,128)S(1)}, f32[2,16,128]{2,1,0:T(8,128)S(1)}, u32[]{:S(2)}, u32[]{:S(2)}) collective-permute-start(f32[2,16,128]{2,1,0:T(8,128)S(1)} %get-tuple-element.33), channel_id=1, source_target_pairs={{0,1},{1,0},{2,3},{3,2},{4,5},{5,4},{6,7},{7,6},{8,9},{9,8},{10,11... | collective-permute-start | bytes 49160 | tf_op jit(solution)/shard_map/ppermute | solution.py:167
  11.6 1.0 %collective-permute-done.8 = bf16[2,16,384]{2,1,0:T(8,128)(2,1)S(1)} collective-permute-done((bf16[2,16,384]{2,1,0:T(8,128)(2,1)S(1)}, bf16[2,16,384]{2,1,0:T(8,128)(2,1)S(1)}, u32[]{:S(2)}, u32[]{:S(2)}) %collective-permute-start.8) | collective-permute-done | bytes 24608 | tf_op jit(solution)/shard_map/ppermute | solution.py:167
  12.6 0.2 %collective-permute-done.7 = bf16[2,16,384]{2,1,0:T(8,128)(2,1)S(1)} collective-permute-done((bf16[2,16,384]{2,1,0:T(8,128)(2,1)S(1)}, bf16[2,16,384]{2,1,0:T(8,128)(2,1)S(1)}, u32[]{:S(2)}, u32[]{:S(2)}) %collective-permute-start.7) | collective-permute-done | bytes 24608 | tf_op jit(solution)/shard_map/ppermute | solution.py:167
  12.9 2.6 %collective-permute-start.11 = (f32[1,16,384]{2,1,0:T(8,128)S(1)}, f32[1,16,384]{2,1,0:T(8,128)S(1)}, u32[]{:S(2)}, u32[]{:S(2)}) collective-permute-start(f32[1,16,384]{2,1,0:T(8,128)S(1)} %constant_dynamic-slice_fusion.1), channel_id=1, source_target_pairs={{0,17},{1,16},{2,19},{3,18},{4,21},{5,20},{6,23},{7,22},{8,25},{9,... | collective-permute-start | bytes 73736 | tf_op jit(solution)/shard_map/ppermute | solution.py:167
  15.5 0.2 %collective-permute-start.10 = (f32[1,8,384]{2,1,0:T(8,128)S(1)}, f32[1,8,384]{2,1,0:T(8,128)S(1)}, u32[]{:S(2)}, u32[]{:S(2)}) collective-permute-start(f32[1,8,384]{2,1,0:T(8,128)S(1)} %get-tuple-element.30), channel_id=1, source_target_pairs={{0,1},{1,0},{2,3},{3,2},{4,5},{5,4},{6,7},{7,6},{8,9},{9,8},{10,11... | collective-permute-start | bytes 36872 | tf_op jit(solution)/shard_map/ppermute | solution.py:167
  15.7 0.3 %collective-permute-start.9 = (f32[1,8,384]{2,1,0:T(8,128)S(1)}, f32[1,8,384]{2,1,0:T(8,128)S(1)}, u32[]{:S(2)}, u32[]{:S(2)}) collective-permute-start(f32[1,8,384]{2,1,0:T(8,128)S(1)} %get-tuple-element.29), channel_id=1, source_target_pairs={{0,1},{1,0},{2,3},{3,2},{4,5},{5,4},{6,7},{7,6},{8,9},{9,8},{10,11... | collective-permute-start | bytes 36872 | tf_op jit(solution)/shard_map/ppermute | solution.py:167
  16.0 0.7 %collective-permute-done.10 = f32[1,8,384]{2,1,0:T(8,128)S(1)} collective-permute-done((f32[1,8,384]{2,1,0:T(8,128)S(1)}, f32[1,8,384]{2,1,0:T(8,128)S(1)}, u32[]{:S(2)}, u32[]{:S(2)}) %collective-permute-start.10) | collective-permute-done | bytes 12320 | tf_op jit(solution)/shard_map/ppermute | solution.py:167
  16.7 0.2 %collective-permute-done.9 = f32[1,8,384]{2,1,0:T(8,128)S(1)} collective-permute-done((f32[1,8,384]{2,1,0:T(8,128)S(1)}, f32[1,8,384]{2,1,0:T(8,128)S(1)}, u32[]{:S(2)}, u32[]{:S(2)}) %collective-permute-start.9) | collective-permute-done | bytes 12320 | tf_op jit(solution)/shard_map/ppermute | solution.py:167
  16.8 0.3 %collective-permute-done.11 = f32[1,16,384]{2,1,0:T(8,128)S(1)} collective-permute-done((f32[1,16,384]{2,1,0:T(8,128)S(1)}, f32[1,16,384]{2,1,0:T(8,128)S(1)}, u32[]{:S(2)}, u32[]{:S(2)}) %collective-permute-start.11) | collective-permute-done | bytes 24608 | tf_op jit(solution)/shard_map/ppermute | solution.py:167
  17.1 0.6 %maximum_add_fusion.1 = f32[1,16,384]{2,1,0:T(8,128)} fusion(f32[1,16,384]{2,1,0:T(8,128)S(1)} %collective-permute-done.11, f32[1,8,384]{2,1,0:T(8,128)S(1)} %collective-permute-done.10, f32[1,8,384]{2,1,0:T(8,128)S(1)} %collective-permute-done.9), kind=kLoop, calls=%fused_computation.3 | loop fusion | flops 12288 | bytes 73728 | tf_op jit(solution)/shard_map/add | solution.py:261
  (17 shorter events, 0.2 us)
Async XLA Ops:
  0.0 4.2 %collective-permute-start = (f32[2,384]{1,0:T(2,128)}, f32[2,384]{1,0:T(2,128)S(1)}, u32[]{:S(2)}, u32[]{:S(2)}) collective-permute-start(f32[2,384]{1,0:T(2,128)} %wave_in.1), channel_id=1, source_target_pairs={{0,3},{1,2},{2,1},{3,0},{4,7},{5,6},{6,5},{7,4},{8,11},{9,10},{10,... | collective-permute-start | bytes 9224 | tf_op jit(solution)/shard_map/ppermute | solution.py:167
  2.4 3.1 %collective-permute-start.1 = (f32[2,384]{1,0:T(2,128)}, f32[2,384]{1,0:T(2,128)S(1)}, u32[]{:S(2)}, u32[]{:S(2)}) collective-permute-start(f32[2,384]{1,0:T(2,128)} %wave_in.1), channel_id=1, source_target_pairs={{0,1},{1,0},{2,3},{3,2},{4,5},{5,4},{6,7},{7,6},{8,9},{9,8},{10,11... | collective-permute-start | bytes 9224 | tf_op jit(solution)/shard_map/ppermute | solution.py:167
  3.1 1.5 %copy-start.2 = (s32[128,2]{0,1:T(2,128)S(1)}, s32[128,2]{0,1:T(2,128)}, u32[]{:S(2)}) copy-start(s32[128,2]{0,1:T(2,128)} %param.9) | copy-start | bytes 3076
  4.2 0.7 %copy-start = (f32[2,384]{1,0:T(2,128)S(1)}, f32[2,384]{1,0:T(2,128)}, u32[]{:S(2)}) copy-start(f32[2,384]{1,0:T(2,128)} %wave_in.1) | copy-start | bytes 9220
  4.3 1.3 %collective-permute-start.2 = (f32[2,384]{1,0:T(2,128)S(1)}, f32[2,384]{1,0:T(2,128)S(1)}, u32[]{:S(2)}, u32[]{:S(2)}) collective-permute-start(f32[2,384]{1,0:T(2,128)S(1)} %collective-permute-done.refs_3_), channel_id=1, source_target_pairs={{0,1},{1,0},{2,3},{3,2},{4,5},{5,4},{6,7},{7,6},{8,9},{9,8},{10,11... | collective-permute-start | bytes 9224 | tf_op jit(solution)/shard_map/ppermute | solution.py:167
  4.5 0.7 %copy-start.1 = (s32[128,2]{0,1:T(2,128)S(1)}, s32[128,2]{0,1:T(2,128)}, u32[]{:S(2)}) copy-start(s32[128,2]{0,1:T(2,128)} %param.8) | copy-start | bytes 3076
  4.5 0.7 %copy-start.3 = (f32[64]{0:T(128)S(1)}, f32[64]{0:T(128)}, u32[]{:S(2)}) copy-start(f32[64]{0:T(128)} %param.6) | copy-start | bytes 772
  6.5 4.4 %collective-permute-start.3 = (bf16[2,16,384]{2,1,0:T(8,128)(2,1)S(1)}, bf16[2,16,384]{2,1,0:T(8,128)(2,1)S(1)}, u32[]{:S(2)}, u32[]{:S(2)}) collective-permute-start(bf16[2,16,384]{2,1,0:T(8,128)(2,1)S(1)} %get-tuple-element.25), channel_id=1, source_target_pairs={{0,13},{1,12},{2,15},{3,14},{4,9},{5,8},{6,11},{7,10},{8,5},{9,4},... | collective-permute-start | bytes 73736 | tf_op jit(solution)/shard_map/ppermute | solution.py:167
  9.3 3.3 %collective-permute-start.8 = (bf16[2,16,384]{2,1,0:T(8,128)(2,1)S(1)}, bf16[2,16,384]{2,1,0:T(8,128)(2,1)S(1)}, u32[]{:S(2)}, u32[]{:S(2)}) collective-permute-start(bf16[2,16,384]{2,1,0:T(8,128)(2,1)S(1)} %get-tuple-element.28), channel_id=1, source_target_pairs={{0,9},{1,8},{2,11},{3,10},{4,13},{5,12},{6,15},{7,14},{8,1},{9,0},... | collective-permute-start | bytes 73736 | tf_op jit(solution)/shard_map/ppermute | solution.py:167
  9.6 3.3 %collective-permute-start.7 = (bf16[2,16,384]{2,1,0:T(8,128)(2,1)S(1)}, bf16[2,16,384]{2,1,0:T(8,128)(2,1)S(1)}, u32[]{:S(2)}, u32[]{:S(2)}) collective-permute-start(bf16[2,16,384]{2,1,0:T(8,128)(2,1)S(1)} %get-tuple-element.27), channel_id=1, source_target_pairs={{0,5},{1,4},{2,7},{3,6},{4,1},{5,0},{6,3},{7,2},{8,13},{9,12},{10,... | collective-permute-start | bytes 73736 | tf_op jit(solution)/shard_map/ppermute | solution.py:167
  10.9 2.0 %collective-permute-start.6 = (f32[2,16,128]{2,1,0:T(8,128)S(1)}, f32[2,16,128]{2,1,0:T(8,128)S(1)}, u32[]{:S(2)}, u32[]{:S(2)}) collective-permute-start(f32[2,16,128]{2,1,0:T(8,128)S(1)} %get-tuple-element.32), channel_id=1, source_target_pairs={{0,1},{1,0},{2,3},{3,2},{4,5},{5,4},{6,7},{7,6},{8,9},{9,8},{10,11... | collective-permute-start | bytes 49160 | tf_op jit(solution)/shard_map/ppermute | solution.py:167
  11.0 1.8 %collective-permute-start.5 = (f32[2,16,128]{2,1,0:T(8,128)S(1)}, f32[2,16,128]{2,1,0:T(8,128)S(1)}, u32[]{:S(2)}, u32[]{:S(2)}) collective-permute-start(f32[2,16,128]{2,1,0:T(8,128)S(1)} %get-tuple-element.33), channel_id=1, source_target_pairs={{0,1},{1,0},{2,3},{3,2},{4,5},{5,4},{6,7},{7,6},{8,9},{9,8},{10,11... | collective-permute-start | bytes 49160 | tf_op jit(solution)/shard_map/ppermute | solution.py:167
  11.4 1.5 %collective-permute-start.4 = (f32[2,16,128]{2,1,0:T(8,128)S(1)}, f32[2,16,128]{2,1,0:T(8,128)S(1)}, u32[]{:S(2)}, u32[]{:S(2)}) collective-permute-start(f32[2,16,128]{2,1,0:T(8,128)S(1)} %get-tuple-element.31), channel_id=1, source_target_pairs={{0,1},{1,0},{2,3},{3,2},{4,5},{5,4},{6,7},{7,6},{8,9},{9,8},{10,11... | collective-permute-start | bytes 49160 | tf_op jit(solution)/shard_map/ppermute | solution.py:167
  12.9 4.2 %collective-permute-start.11 = (f32[1,16,384]{2,1,0:T(8,128)S(1)}, f32[1,16,384]{2,1,0:T(8,128)S(1)}, u32[]{:S(2)}, u32[]{:S(2)}) collective-permute-start(f32[1,16,384]{2,1,0:T(8,128)S(1)} %constant_dynamic-slice_fusion.1), channel_id=1, source_target_pairs={{0,17},{1,16},{2,19},{3,18},{4,21},{5,20},{6,23},{7,22},{8,25},{9,... | collective-permute-start | bytes 73736 | tf_op jit(solution)/shard_map/ppermute | solution.py:167
  15.5 1.2 %collective-permute-start.10 = (f32[1,8,384]{2,1,0:T(8,128)S(1)}, f32[1,8,384]{2,1,0:T(8,128)S(1)}, u32[]{:S(2)}, u32[]{:S(2)}) collective-permute-start(f32[1,8,384]{2,1,0:T(8,128)S(1)} %get-tuple-element.30), channel_id=1, source_target_pairs={{0,1},{1,0},{2,3},{3,2},{4,5},{5,4},{6,7},{7,6},{8,9},{9,8},{10,11... | collective-permute-start | bytes 36872 | tf_op jit(solution)/shard_map/ppermute | solution.py:167
  15.7 1.2 %collective-permute-start.9 = (f32[1,8,384]{2,1,0:T(8,128)S(1)}, f32[1,8,384]{2,1,0:T(8,128)S(1)}, u32[]{:S(2)}, u32[]{:S(2)}) collective-permute-start(f32[1,8,384]{2,1,0:T(8,128)S(1)} %get-tuple-element.29), channel_id=1, source_target_pairs={{0,1},{1,0},{2,3},{3,2},{4,5},{5,4},{6,7},{7,6},{8,9},{9,8},{10,11... | collective-permute-start | bytes 36872 | tf_op jit(solution)/shard_map/ppermute | solution.py:167

commit v11 on v10

--- a/solution.py
+++ b/solution.py
@@ -148,7 +148,7 @@
         ahead = pltpu.roll(
             jnp.broadcast_to(whole, (LANES, blocks * LANES)), 0, 1, stride=1, stride_axis=0
         )
-        for c in range(1, blocks):
+        for c in reversed(range(1, blocks)):
             hankel_ref[s, :, c * LANES : (c + 1) * LANES] = ahead[:, c * LANES : (c + 1) * LANES].astype(jnp.bfloat16)
     me = lax.axis_index("sta") & len(send_refs)
     parts = [me ^ distance for distance in range(1, len(send_refs) + 1)]

time: 17.9 us -> 17.9 us (level)
  no operation moved by 1% of the time
where the time goes in v11:
time: 17.9 us; the launch traced here: 17.7 us
  starting transfers between devices  10.4 us (58%)
  waiting for transfers between devices  3.09 us (17%)
  local copies, waits for them, and re-layouts  1.87 us (10%)
  Pallas kernels  1.64 us (9%)
  other arithmetic  0.63 us (4%)
    ppermute x12, starting transfers between devices, flip(): return lax.ppermute(value, ('sta', 'tpl'), pairs)  10.4 us
    ppermute x12, waiting for transfers between devices, flip(): return lax.ppermute(value, ('sta', 'tpl'), pairs)  3.09 us
    transpose x1, local copies, waits for them, and re-layouts, shards(): templates.transpose(1, 0, 2)  1.16 us
    pallas_call x1, Pallas kernels, shards(): pl.pallas_call(functools.partial(send_kernel, segments), out_shape=(*[jax...  0.96 us
    unnamed x8, local copies, waits for them, and re-layouts  0.68 us
    add x2, other arithmetic, shards(): stack = stack + piece.astype(jnp.float32)  0.63 us
    pallas_call x1, Pallas kernels, shards(): pl.pallas_call(keep_kernel, out_shape=jax.ShapeDtypeStruct((owners // par...  0.41 us
  transfers between devices with their start and end apart: 12, of which 6 were waited for; matrix products, arithmetic and copies ran while one was open for 7% of the time, Pallas kernels for 4%

profile of v11, /device:TPU:0, one launch (start us, length us, event | category | flops | bytes accessed | tf_op | source)
XLA Modules:
  0.0 17.7 jit_solution(10560247821498333598)
XLA Ops:
  0.0 2.4 %collective-permute-start = (f32[2,384]{1,0:T(2,128)}, f32[2,384]{1,0:T(2,128)S(1)}, u32[]{:S(2)}, u32[]{:S(2)}) collective-permute-start(f32[2,384]{1,0:T(2,128)} %wave_in.1), channel_id=1, source_target_pairs={{0,3},{1,2},{2,1},{3,0},{4,7},{5,6},{6,5},{7,4},{8,11},{9,10},{10,... | collective-permute-start | bytes 9224 | tf_op jit(solution)/shard_map/ppermute | solution.py:167
  2.4 0.7 %collective-permute-start.1 = (f32[2,384]{1,0:T(2,128)}, f32[2,384]{1,0:T(2,128)S(1)}, u32[]{:S(2)}, u32[]{:S(2)}) collective-permute-start(f32[2,384]{1,0:T(2,128)} %wave_in.1), channel_id=1, source_target_pairs={{0,1},{1,0},{2,3},{3,2},{4,5},{5,4},{6,7},{7,6},{8,9},{9,8},{10,11... | collective-permute-start | bytes 9224 | tf_op jit(solution)/shard_map/ppermute | solution.py:167
  3.1 1.2 %copy.6 = bf16[2,128,1024]{2,1,0:T(8,128)(2,1)S(1)} copy(bf16[2,128,1024]{2,0,1:T(2,128)(2,1)} %bitcast.10) | data formatting | bytes 1048576 | tf_op jit(solution)/shard_map/transpose | solution.py:185
  4.3 0.3 %collective-permute-start.2 = (f32[2,384]{1,0:T(2,128)S(1)}, f32[2,384]{1,0:T(2,128)S(1)}, u32[]{:S(2)}, u32[]{:S(2)}) collective-permute-start(f32[2,384]{1,0:T(2,128)S(1)} %collective-permute-done.refs_3_), channel_id=1, source_target_pairs={{0,1},{1,0},{2,3},{3,2},{4,5},{5,4},{6,7},{7,6},{8,9},{9,8},{10,11... | collective-permute-start | bytes 9224 | tf_op jit(solution)/shard_map/ppermute | solution.py:167
  4.6 0.4 %copy-done = f32[2,384]{1,0:T(2,128)S(1)} copy-done((f32[2,384]{1,0:T(2,128)S(1)}, f32[2,384]{1,0:T(2,128)}, u32[]{:S(2)}) %copy-start) | copy-done | bytes 3096
  4.9 0.3 %copy-done.1 = s32[128,2]{0,1:T(2,128)S(1)} copy-done((s32[128,2]{0,1:T(2,128)S(1)}, s32[128,2]{0,1:T(2,128)}, u32[]{:S(2)}) %copy-start.1) | copy-done | bytes 1048
  5.2 0.3 %columns.1 = (f32[2,384]{1,0:T(2,128)S(1)}, f32[256,128]{1,0:T(8,128)S(1)}, f32[2,4,32,128]{3,2,1,0:T(8,128)S(1)}, s32[2,4,32,128]{3,2,1,0:T(8,128)S(1)}) custom-call(f32[2,384]{1,0:T(2,128)S(1)} %copy-done, f32[1,64]{1,0:T(1,128)S(1)} %bitcast.9, s32[2,128]{1,0:T(2,128)S(1)} %bitcast.7, s32[2,128]{1,0:T(2,128)S(1)} %bitcast.8), custom_call_target="tpu_custom_call" | custom-call | flops 1048576 | bytes 1048576 | tf_op jit(solution)/shard_map/columns/pallas_call | solution.py:186
  5.5 1.0 %send_parts.1 = (bf16[2,16,384]{2,1,0:T(8,128)(2,1)S(1)}, bf16[2,16,384]{2,1,0:T(8,128)(2,1)S(1)}, bf16[2,16,384]{2,1,0:T(8,128)(2,1)S(1)}, bf16[2,128,1536]{2,1,0:T(8,128)(2,1)S(1)}, f32[2,512]{1,0:T(2,128)S(1)}) custom-call(f32[2,384]{1,0:T(2,128)S(1)} %get-tuple-element.20.refs_0_, f32[2,384]{1,0:T(2,128)S(1)} %collective-permute-done.1.refs_1_, ...), custom_call_target="tpu_custom_call" | custom-call | flops 1048576 | bytes 1048576 | tf_op jit(solution)/shard_map/send_parts/pallas_call | solution.py:210
  6.5 2.9 %collective-permute-start.3 = (bf16[2,16,384]{2,1,0:T(8,128)(2,1)S(1)}, bf16[2,16,384]{2,1,0:T(8,128)(2,1)S(1)}, u32[]{:S(2)}, u32[]{:S(2)}) collective-permute-start(bf16[2,16,384]{2,1,0:T(8,128)(2,1)S(1)} %get-tuple-element.25), channel_id=1, source_target_pairs={{0,13},{1,12},{2,15},{3,14},{4,9},{5,8},{6,11},{7,10},{8,5},{9,4},... | collective-permute-start | bytes 73736 | tf_op jit(solution)/shard_map/ppermute | solution.py:167
  9.3 0.2 %collective-permute-start.8 = (bf16[2,16,384]{2,1,0:T(8,128)(2,1)S(1)}, bf16[2,16,384]{2,1,0:T(8,128)(2,1)S(1)}, u32[]{:S(2)}, u32[]{:S(2)}) collective-permute-start(bf16[2,16,384]{2,1,0:T(8,128)(2,1)S(1)} %get-tuple-element.28), channel_id=1, source_target_pairs={{0,9},{1,8},{2,11},{3,10},{4,13},{5,12},{6,15},{7,14},{8,1},{9,0},... | collective-permute-start | bytes 73736 | tf_op jit(solution)/shard_map/ppermute | solution.py:167
  9.6 0.2 %collective-permute-start.7 = (bf16[2,16,384]{2,1,0:T(8,128)(2,1)S(1)}, bf16[2,16,384]{2,1,0:T(8,128)(2,1)S(1)}, u32[]{:S(2)}, u32[]{:S(2)}) collective-permute-start(bf16[2,16,384]{2,1,0:T(8,128)(2,1)S(1)} %get-tuple-element.27), channel_id=1, source_target_pairs={{0,5},{1,4},{2,7},{3,6},{4,1},{5,0},{6,3},{7,2},{8,13},{9,12},{10,... | collective-permute-start | bytes 73736 | tf_op jit(solution)/shard_map/ppermute | solution.py:167
  9.8 0.4 %keep_part.1 = f32[2,16,384]{2,1,0:T(8,128)S(1)} custom-call(bf16[2,2,4,16,1024]{4,3,2,1,0:T(8,128)(2,1)S(1)} %bitcast.6, f32[2,4,32,128]{3,2,1,0:T(8,128)S(1)} %get-tuple-element.18.refs_6_.used_ref, s32[2,4,32,128]{3,2,1,0:T(8,128)S(1)} %get-tuple-element.19.refs_7_.shift_ref, bf16[2,128,1536]{2,1,0:T(8,128)(2,1)S(1)} %get-tuple-element.23.hankel_ref, ...), custom_call_target="tpu_custom_call" | custom-call | flops 1048576 | bytes 1048576 | tf_op jit(solution)/shard_map/keep_part/pallas_call | solution.py:228
  10.2 0.7 %collective-permute-done.3 = bf16[2,16,384]{2,1,0:T(8,128)(2,1)S(1)} collective-permute-done((bf16[2,16,384]{2,1,0:T(8,128)(2,1)S(1)}, bf16[2,16,384]{2,1,0:T(8,128)(2,1)S(1)}, u32[]{:S(2)}, u32[]{:S(2)}) %collective-permute-start.3) | collective-permute-done | bytes 24608 | tf_op jit(solution)/shard_map/ppermute | solution.py:167
  10.9 0.2 %collective-permute-start.6 = (f32[2,16,128]{2,1,0:T(8,128)S(1)}, f32[2,16,128]{2,1,0:T(8,128)S(1)}, u32[]{:S(2)}, u32[]{:S(2)}) collective-permute-start(f32[2,16,128]{2,1,0:T(8,128)S(1)} %get-tuple-element.32), channel_id=1, source_target_pairs={{0,1},{1,0},{2,3},{3,2},{4,5},{5,4},{6,7},{7,6},{8,9},{9,8},{10,11... | collective-permute-start | bytes 49160 | tf_op jit(solution)/shard_map/ppermute | solution.py:167
  11.0 0.3 %collective-permute-start.5 = (f32[2,16,128]{2,1,0:T(8,128)S(1)}, f32[2,16,128]{2,1,0:T(8,128)S(1)}, u32[]{:S(2)}, u32[]{:S(2)}) collective-permute-start(f32[2,16,128]{2,1,0:T(8,128)S(1)} %get-tuple-element.33), channel_id=1, source_target_pairs={{0,1},{1,0},{2,3},{3,2},{4,5},{5,4},{6,7},{7,6},{8,9},{9,8},{10,11... | collective-permute-start | bytes 49160 | tf_op jit(solution)/shard_map/ppermute | solution.py:167
  11.5 1.0 %collective-permute-done.8 = bf16[2,16,384]{2,1,0:T(8,128)(2,1)S(1)} collective-permute-done((bf16[2,16,384]{2,1,0:T(8,128)(2,1)S(1)}, bf16[2,16,384]{2,1,0:T(8,128)(2,1)S(1)}, u32[]{:S(2)}, u32[]{:S(2)}) %collective-permute-start.8) | collective-permute-done | bytes 24608 | tf_op jit(solution)/shard_map/ppermute | solution.py:167
  12.6 0.2 %collective-permute-done.7 = bf16[2,16,384]{2,1,0:T(8,128)(2,1)S(1)} collective-permute-done((bf16[2,16,384]{2,1,0:T(8,128)(2,1)S(1)}, bf16[2,16,384]{2,1,0:T(8,128)(2,1)S(1)}, u32[]{:S(2)}, u32[]{:S(2)}) %collective-permute-start.7) | collective-permute-done | bytes 24608 | tf_op jit(solution)/shard_map/ppermute | solution.py:167
  12.9 2.6 %collective-permute-start.11 = (f32[1,16,384]{2,1,0:T(8,128)S(1)}, f32[1,16,384]{2,1,0:T(8,128)S(1)}, u32[]{:S(2)}, u32[]{:S(2)}) collective-permute-start(f32[1,16,384]{2,1,0:T(8,128)S(1)} %constant_dynamic-slice_fusion.1), channel_id=1, source_target_pairs={{0,17},{1,16},{2,19},{3,18},{4,21},{5,20},{6,23},{7,22},{8,25},{9,... | collective-permute-start | bytes 73736 | tf_op jit(solution)/shard_map/ppermute | solution.py:167
  15.5 0.2 %collective-permute-start.10 = (f32[1,8,384]{2,1,0:T(8,128)S(1)}, f32[1,8,384]{2,1,0:T(8,128)S(1)}, u32[]{:S(2)}, u32[]{:S(2)}) collective-permute-start(f32[1,8,384]{2,1,0:T(8,128)S(1)} %get-tuple-element.30), channel_id=1, source_target_pairs={{0,1},{1,0},{2,3},{3,2},{4,5},{5,4},{6,7},{7,6},{8,9},{9,8},{10,11... | collective-permute-start | bytes 36872 | tf_op jit(solution)/shard_map/ppermute | solution.py:167
  15.7 0.3 %collective-permute-start.9 = (f32[1,8,384]{2,1,0:T(8,128)S(1)}, f32[1,8,384]{2,1,0:T(8,128)S(1)}, u32[]{:S(2)}, u32[]{:S(2)}) collective-permute-start(f32[1,8,384]{2,1,0:T(8,128)S(1)} %get-tuple-element.29), channel_id=1, source_target_pairs={{0,1},{1,0},{2,3},{3,2},{4,5},{5,4},{6,7},{7,6},{8,9},{9,8},{10,11... | collective-permute-start | bytes 36872 | tf_op jit(solution)/shard_map/ppermute | solution.py:167
  16.0 0.7 %collective-permute-done.10 = f32[1,8,384]{2,1,0:T(8,128)S(1)} collective-permute-done((f32[1,8,384]{2,1,0:T(8,128)S(1)}, f32[1,8,384]{2,1,0:T(8,128)S(1)}, u32[]{:S(2)}, u32[]{:S(2)}) %collective-permute-start.10) | collective-permute-done | bytes 12320 | tf_op jit(solution)/shard_map/ppermute | solution.py:167
  16.6 0.2 %collective-permute-done.9 = f32[1,8,384]{2,1,0:T(8,128)S(1)} collective-permute-done((f32[1,8,384]{2,1,0:T(8,128)S(1)}, f32[1,8,384]{2,1,0:T(8,128)S(1)}, u32[]{:S(2)}, u32[]{:S(2)}) %collective-permute-start.9) | collective-permute-done | bytes 12320 | tf_op jit(solution)/shard_map/ppermute | solution.py:167
  16.8 0.3 %collective-permute-done.11 = f32[1,16,384]{2,1,0:T(8,128)S(1)} collective-permute-done((f32[1,16,384]{2,1,0:T(8,128)S(1)}, f32[1,16,384]{2,1,0:T(8,128)S(1)}, u32[]{:S(2)}, u32[]{:S(2)}) %collective-permute-start.11) | collective-permute-done | bytes 24608 | tf_op jit(solution)/shard_map/ppermute | solution.py:167
  17.1 0.6 %maximum_add_fusion.1 = f32[1,16,384]{2,1,0:T(8,128)} fusion(f32[1,16,384]{2,1,0:T(8,128)S(1)} %collective-permute-done.11, f32[1,8,384]{2,1,0:T(8,128)S(1)} %collective-permute-done.10, f32[1,8,384]{2,1,0:T(8,128)S(1)} %collective-permute-done.9), kind=kLoop, calls=%fused_computation.3 | loop fusion | flops 12288 | bytes 73728 | tf_op jit(solution)/shard_map/add | solution.py:261
  (17 shorter events, 0.2 us)
Async XLA Ops:
  0.0 4.2 %collective-permute-start = (f32[2,384]{1,0:T(2,128)}, f32[2,384]{1,0:T(2,128)S(1)}, u32[]{:S(2)}, u32[]{:S(2)}) collective-permute-start(f32[2,384]{1,0:T(2,128)} %wave_in.1), channel_id=1, source_target_pairs={{0,3},{1,2},{2,1},{3,0},{4,7},{5,6},{6,5},{7,4},{8,11},{9,10},{10,... | collective-permute-start | bytes 9224 | tf_op jit(solution)/shard_map/ppermute | solution.py:167
  2.4 3.1 %collective-permute-start.1 = (f32[2,384]{1,0:T(2,128)}, f32[2,384]{1,0:T(2,128)S(1)}, u32[]{:S(2)}, u32[]{:S(2)}) collective-permute-start(f32[2,384]{1,0:T(2,128)} %wave_in.1), channel_id=1, source_target_pairs={{0,1},{1,0},{2,3},{3,2},{4,5},{5,4},{6,7},{7,6},{8,9},{9,8},{10,11... | collective-permute-start | bytes 9224 | tf_op jit(solution)/shard_map/ppermute | solution.py:167
  3.1 1.5 %copy-start.2 = (s32[128,2]{0,1:T(2,128)S(1)}, s32[128,2]{0,1:T(2,128)}, u32[]{:S(2)}) copy-start(s32[128,2]{0,1:T(2,128)} %param.9) | copy-start | bytes 3076
  4.2 0.7 %copy-start = (f32[2,384]{1,0:T(2,128)S(1)}, f32[2,384]{1,0:T(2,128)}, u32[]{:S(2)}) copy-start(f32[2,384]{1,0:T(2,128)} %wave_in.1) | copy-start | bytes 9220
  4.3 1.3 %collective-permute-start.2 = (f32[2,384]{1,0:T(2,128)S(1)}, f32[2,384]{1,0:T(2,128)S(1)}, u32[]{:S(2)}, u32[]{:S(2)}) collective-permute-start(f32[2,384]{1,0:T(2,128)S(1)} %collective-permute-done.refs_3_), channel_id=1, source_target_pairs={{0,1},{1,0},{2,3},{3,2},{4,5},{5,4},{6,7},{7,6},{8,9},{9,8},{10,11... | collective-permute-start | bytes 9224 | tf_op jit(solution)/shard_map/ppermute | solution.py:167
  4.5 0.7 %copy-start.1 = (s32[128,2]{0,1:T(2,128)S(1)}, s32[128,2]{0,1:T(2,128)}, u32[]{:S(2)}) copy-start(s32[128,2]{0,1:T(2,128)} %param.8) | copy-start | bytes 3076
  4.5 0.7 %copy-start.3 = (f32[64]{0:T(128)S(1)}, f32[64]{0:T(128)}, u32[]{:S(2)}) copy-start(f32[64]{0:T(128)} %param.6) | copy-start | bytes 772
  6.5 4.4 %collective-permute-start.3 = (bf16[2,16,384]{2,1,0:T(8,128)(2,1)S(1)}, bf16[2,16,384]{2,1,0:T(8,128)(2,1)S(1)}, u32[]{:S(2)}, u32[]{:S(2)}) collective-permute-start(bf16[2,16,384]{2,1,0:T(8,128)(2,1)S(1)} %get-tuple-element.25), channel_id=1, source_target_pairs={{0,13},{1,12},{2,15},{3,14},{4,9},{5,8},{6,11},{7,10},{8,5},{9,4},... | collective-permute-start | bytes 73736 | tf_op jit(solution)/shard_map/ppermute | solution.py:167
  9.3 3.3 %collective-permute-start.8 = (bf16[2,16,384]{2,1,0:T(8,128)(2,1)S(1)}, bf16[2,16,384]{2,1,0:T(8,128)(2,1)S(1)}, u32[]{:S(2)}, u32[]{:S(2)}) collective-permute-start(bf16[2,16,384]{2,1,0:T(8,128)(2,1)S(1)} %get-tuple-element.28), channel_id=1, source_target_pairs={{0,9},{1,8},{2,11},{3,10},{4,13},{5,12},{6,15},{7,14},{8,1},{9,0},... | collective-permute-start | bytes 73736 | tf_op jit(solution)/shard_map/ppermute | solution.py:167
  9.6 3.3 %collective-permute-start.7 = (bf16[2,16,384]{2,1,0:T(8,128)(2,1)S(1)}, bf16[2,16,384]{2,1,0:T(8,128)(2,1)S(1)}, u32[]{:S(2)}, u32[]{:S(2)}) collective-permute-start(bf16[2,16,384]{2,1,0:T(8,128)(2,1)S(1)} %get-tuple-element.27), channel_id=1, source_target_pairs={{0,5},{1,4},{2,7},{3,6},{4,1},{5,0},{6,3},{7,2},{8,13},{9,12},{10,... | collective-permute-start | bytes 73736 | tf_op jit(solution)/shard_map/ppermute | solution.py:167
  10.9 2.0 %collective-permute-start.6 = (f32[2,16,128]{2,1,0:T(8,128)S(1)}, f32[2,16,128]{2,1,0:T(8,128)S(1)}, u32[]{:S(2)}, u32[]{:S(2)}) collective-permute-start(f32[2,16,128]{2,1,0:T(8,128)S(1)} %get-tuple-element.32), channel_id=1, source_target_pairs={{0,1},{1,0},{2,3},{3,2},{4,5},{5,4},{6,7},{7,6},{8,9},{9,8},{10,11... | collective-permute-start | bytes 49160 | tf_op jit(solution)/shard_map/ppermute | solution.py:167
  11.0 1.8 %collective-permute-start.5 = (f32[2,16,128]{2,1,0:T(8,128)S(1)}, f32[2,16,128]{2,1,0:T(8,128)S(1)}, u32[]{:S(2)}, u32[]{:S(2)}) collective-permute-start(f32[2,16,128]{2,1,0:T(8,128)S(1)} %get-tuple-element.33), channel_id=1, source_target_pairs={{0,1},{1,0},{2,3},{3,2},{4,5},{5,4},{6,7},{7,6},{8,9},{9,8},{10,11... | collective-permute-start | bytes 49160 | tf_op jit(solution)/shard_map/ppermute | solution.py:167
  11.4 1.5 %collective-permute-start.4 = (f32[2,16,128]{2,1,0:T(8,128)S(1)}, f32[2,16,128]{2,1,0:T(8,128)S(1)}, u32[]{:S(2)}, u32[]{:S(2)}) collective-permute-start(f32[2,16,128]{2,1,0:T(8,128)S(1)} %get-tuple-element.31), channel_id=1, source_target_pairs={{0,1},{1,0},{2,3},{3,2},{4,5},{5,4},{6,7},{7,6},{8,9},{9,8},{10,11... | collective-permute-start | bytes 49160 | tf_op jit(solution)/shard_map/ppermute | solution.py:167
  12.9 4.2 %collective-permute-start.11 = (f32[1,16,384]{2,1,0:T(8,128)S(1)}, f32[1,16,384]{2,1,0:T(8,128)S(1)}, u32[]{:S(2)}, u32[]{:S(2)}) collective-permute-start(f32[1,16,384]{2,1,0:T(8,128)S(1)} %constant_dynamic-slice_fusion.1), channel_id=1, source_target_pairs={{0,17},{1,16},{2,19},{3,18},{4,21},{5,20},{6,23},{7,22},{8,25},{9,... | collective-permute-start | bytes 73736 | tf_op jit(solution)/shard_map/ppermute | solution.py:167
  15.5 1.2 %collective-permute-start.10 = (f32[1,8,384]{2,1,0:T(8,128)S(1)}, f32[1,8,384]{2,1,0:T(8,128)S(1)}, u32[]{:S(2)}, u32[]{:S(2)}) collective-permute-start(f32[1,8,384]{2,1,0:T(8,128)S(1)} %get-tuple-element.30), channel_id=1, source_target_pairs={{0,1},{1,0},{2,3},{3,2},{4,5},{5,4},{6,7},{7,6},{8,9},{9,8},{10,11... | collective-permute-start | bytes 36872 | tf_op jit(solution)/shard_map/ppermute | solution.py:167
  15.7 1.2 %collective-permute-start.9 = (f32[1,8,384]{2,1,0:T(8,128)S(1)}, f32[1,8,384]{2,1,0:T(8,128)S(1)}, u32[]{:S(2)}, u32[]{:S(2)}) collective-permute-start(f32[1,8,384]{2,1,0:T(8,128)S(1)} %get-tuple-element.29), channel_id=1, source_target_pairs={{0,1},{1,0},{2,3},{3,2},{4,5},{5,4},{6,7},{7,6},{8,9},{9,8},{10,11... | collective-permute-start | bytes 36872 | tf_op jit(solution)/shard_map/ppermute | solution.py:167

commit v12 on v10

--- a/solution.py
+++ b/solution.py
@@ -240,7 +240,7 @@
     for number, reach in enumerate(rounds):
         turn = 1 if number < turns else 0
         if number == 0:
-            moved = [(distance, send[distance - 1]) for distance in range(1, parts)]
+            moved = [(distance, send[distance - 1]) for distance in (*range(parts - 2, 0, -1), parts - 1)]
         else:
             bit = reach // 2
             pairs = stack.reshape(stack.shape[0] // 2, 2, owned, out_len)

time: 17.9 us -> 17.9 us (level)
  no operation moved by 1% of the time
where the time goes in v12:
time: 17.9 us; the launch traced here: 17.8 us
  starting transfers between devices  10.4 us (58%)
  waiting for transfers between devices  3.14 us (18%)
  local copies, waits for them, and re-layouts  1.87 us (10%)
  Pallas kernels  1.65 us (9%)
  other arithmetic  0.63 us (4%)
    ppermute x12, starting transfers between devices, flip(): return lax.ppermute(value, ('sta', 'tpl'), pairs)  10.4 us
    ppermute x12, waiting for transfers between devices, flip(): return lax.ppermute(value, ('sta', 'tpl'), pairs)  3.14 us
    transpose x1, local copies, waits for them, and re-layouts, shards(): templates.transpose(1, 0, 2)  1.16 us
    pallas_call x1, Pallas kernels, shards(): pl.pallas_call(functools.partial(send_kernel, segments), out_shape=(*[jax...  0.97 us
    unnamed x8, local copies, waits for them, and re-layouts  0.68 us
    add x2, other arithmetic, shards(): stack = stack + piece.astype(jnp.float32)  0.63 us
    pallas_call x1, Pallas kernels, shards(): pl.pallas_call(keep_kernel, out_shape=jax.ShapeDtypeStruct((owners // par...  0.41 us
  transfers between devices with their start and end apart: 12, of which 6 were waited for; matrix products, arithmetic and copies ran while one was open for 7% of the time, Pallas kernels for 4%

profile of v12, /device:TPU:0, one launch (start us, length us, event | category | flops | bytes accessed | tf_op | source)
XLA Modules:
  0.0 17.8 jit_solution(18100482380592871477)
XLA Ops:
  0.0 2.4 %collective-permute-start = (f32[2,384]{1,0:T(2,128)}, f32[2,384]{1,0:T(2,128)S(1)}, u32[]{:S(2)}, u32[]{:S(2)}) collective-permute-start(f32[2,384]{1,0:T(2,128)} %wave_in.1), channel_id=1, source_target_pairs={{0,3},{1,2},{2,1},{3,0},{4,7},{5,6},{6,5},{7,4},{8,11},{9,10},{10,... | collective-permute-start | bytes 9224 | tf_op jit(solution)/shard_map/ppermute | solution.py:167
  2.4 0.7 %collective-permute-start.1 = (f32[2,384]{1,0:T(2,128)}, f32[2,384]{1,0:T(2,128)S(1)}, u32[]{:S(2)}, u32[]{:S(2)}) collective-permute-start(f32[2,384]{1,0:T(2,128)} %wave_in.1), channel_id=1, source_target_pairs={{0,1},{1,0},{2,3},{3,2},{4,5},{5,4},{6,7},{7,6},{8,9},{9,8},{10,11... | collective-permute-start | bytes 9224 | tf_op jit(solution)/shard_map/ppermute | solution.py:167
  3.1 1.2 %copy.6 = bf16[2,128,1024]{2,1,0:T(8,128)(2,1)S(1)} copy(bf16[2,128,1024]{2,0,1:T(2,128)(2,1)} %bitcast.10) | data formatting | bytes 1048576 | tf_op jit(solution)/shard_map/transpose | solution.py:185
  4.3 0.3 %collective-permute-start.2 = (f32[2,384]{1,0:T(2,128)S(1)}, f32[2,384]{1,0:T(2,128)S(1)}, u32[]{:S(2)}, u32[]{:S(2)}) collective-permute-start(f32[2,384]{1,0:T(2,128)S(1)} %collective-permute-done.refs_3_), channel_id=1, source_target_pairs={{0,1},{1,0},{2,3},{3,2},{4,5},{5,4},{6,7},{7,6},{8,9},{9,8},{10,11... | collective-permute-start | bytes 9224 | tf_op jit(solution)/shard_map/ppermute | solution.py:167
  4.6 0.4 %copy-done = f32[2,384]{1,0:T(2,128)S(1)} copy-done((f32[2,384]{1,0:T(2,128)S(1)}, f32[2,384]{1,0:T(2,128)}, u32[]{:S(2)}) %copy-start) | copy-done | bytes 3096
  4.9 0.3 %copy-done.1 = s32[128,2]{0,1:T(2,128)S(1)} copy-done((s32[128,2]{0,1:T(2,128)S(1)}, s32[128,2]{0,1:T(2,128)}, u32[]{:S(2)}) %copy-start.1) | copy-done | bytes 1048
  5.2 0.3 %columns.1 = (f32[2,384]{1,0:T(2,128)S(1)}, f32[256,128]{1,0:T(8,128)S(1)}, f32[2,4,32,128]{3,2,1,0:T(8,128)S(1)}, s32[2,4,32,128]{3,2,1,0:T(8,128)S(1)}) custom-call(f32[2,384]{1,0:T(2,128)S(1)} %copy-done, f32[1,64]{1,0:T(1,128)S(1)} %bitcast.9, s32[2,128]{1,0:T(2,128)S(1)} %bitcast.7, s32[2,128]{1,0:T(2,128)S(1)} %bitcast.8), custom_call_target="tpu_custom_call" | custom-call | flops 1048576 | bytes 1048576 | tf_op jit(solution)/shard_map/columns/pallas_call | solution.py:186
  5.5 1.0 %send_parts.1 = (bf16[2,16,384]{2,1,0:T(8,128)(2,1)S(1)}, bf16[2,16,384]{2,1,0:T(8,128)(2,1)S(1)}, bf16[2,16,384]{2,1,0:T(8,128)(2,1)S(1)}, bf16[2,128,1536]{2,1,0:T(8,128)(2,1)S(1)}, f32[2,512]{1,0:T(2,128)S(1)}) custom-call(f32[2,384]{1,0:T(2,128)S(1)} %get-tuple-element.20.refs_0_, f32[2,384]{1,0:T(2,128)S(1)} %collective-permute-done.1.refs_1_, ...), custom_call_target="tpu_custom_call" | custom-call | flops 1048576 | bytes 1048576 | tf_op jit(solution)/shard_map/send_parts/pallas_call | solution.py:210
  6.5 2.8 %collective-permute-start.3 = (bf16[2,16,384]{2,1,0:T(8,128)(2,1)S(1)}, bf16[2,16,384]{2,1,0:T(8,128)(2,1)S(1)}, u32[]{:S(2)}, u32[]{:S(2)}) collective-permute-start(bf16[2,16,384]{2,1,0:T(8,128)(2,1)S(1)} %get-tuple-element.25), channel_id=1, source_target_pairs={{0,13},{1,12},{2,15},{3,14},{4,9},{5,8},{6,11},{7,10},{8,5},{9,4},... | collective-permute-start | bytes 73736 | tf_op jit(solution)/shard_map/ppermute | solution.py:167
  9.3 0.3 %collective-permute-start.8 = (bf16[2,16,384]{2,1,0:T(8,128)(2,1)S(1)}, bf16[2,16,384]{2,1,0:T(8,128)(2,1)S(1)}, u32[]{:S(2)}, u32[]{:S(2)}) collective-permute-start(bf16[2,16,384]{2,1,0:T(8,128)(2,1)S(1)} %get-tuple-element.28), channel_id=1, source_target_pairs={{0,5},{1,4},{2,7},{3,6},{4,1},{5,0},{6,3},{7,2},{8,13},{9,12},{10,... | collective-permute-start | bytes 73736 | tf_op jit(solution)/shard_map/ppermute | solution.py:167
  9.8 0.4 %keep_part.1 = f32[2,16,384]{2,1,0:T(8,128)S(1)} custom-call(bf16[2,2,4,16,1024]{4,3,2,1,0:T(8,128)(2,1)S(1)} %bitcast.6, f32[2,4,32,128]{3,2,1,0:T(8,128)S(1)} %get-tuple-element.18.refs_6_.used_ref, s32[2,4,32,128]{3,2,1,0:T(8,128)S(1)} %get-tuple-element.19.refs_7_.shift_ref, bf16[2,128,1536]{2,1,0:T(8,128)(2,1)S(1)} %get-tuple-element.23.hankel_ref, ...), custom_call_target="tpu_custom_call" | custom-call | flops 1048576 | bytes 1048576 | tf_op jit(solution)/shard_map/keep_part/pallas_call | solution.py:228
  10.2 0.7 %collective-permute-done.3 = bf16[2,16,384]{2,1,0:T(8,128)(2,1)S(1)} collective-permute-done((bf16[2,16,384]{2,1,0:T(8,128)(2,1)S(1)}, bf16[2,16,384]{2,1,0:T(8,128)(2,1)S(1)}, u32[]{:S(2)}, u32[]{:S(2)}) %collective-permute-start.3) | collective-permute-done | bytes 24608 | tf_op jit(solution)/shard_map/ppermute | solution.py:167
  10.9 0.2 collective-permute-start.6
  11.0 0.3 %collective-permute-start.5 = (f32[2,16,128]{2,1,0:T(8,128)S(1)}, f32[2,16,128]{2,1,0:T(8,128)S(1)}, u32[]{:S(2)}, u32[]{:S(2)}) collective-permute-start(f32[2,16,128]{2,1,0:T(8,128)S(1)} %get-tuple-element.33), channel_id=1, source_target_pairs={{0,1},{1,0},{2,3},{3,2},{4,5},{5,4},{6,7},{7,6},{8,9},{9,8},{10,11... | collective-permute-start | bytes 49160 | tf_op jit(solution)/shard_map/ppermute | solution.py:167
  11.4 0.2 collective-permute-start.4
  11.6 1.0 %collective-permute-done.8 = bf16[2,16,384]{2,1,0:T(8,128)(2,1)S(1)} collective-permute-done((bf16[2,16,384]{2,1,0:T(8,128)(2,1)S(1)}, bf16[2,16,384]{2,1,0:T(8,128)(2,1)S(1)}, u32[]{:S(2)}, u32[]{:S(2)}) %collective-permute-start.8) | collective-permute-done | bytes 24608 | tf_op jit(solution)/shard_map/ppermute | solution.py:167
  12.6 0.3 %collective-permute-done.7 = bf16[2,16,384]{2,1,0:T(8,128)(2,1)S(1)} collective-permute-done((bf16[2,16,384]{2,1,0:T(8,128)(2,1)S(1)}, bf16[2,16,384]{2,1,0:T(8,128)(2,1)S(1)}, u32[]{:S(2)}, u32[]{:S(2)}) %collective-permute-start.7) | collective-permute-done | bytes 24608 | tf_op jit(solution)/shard_map/ppermute | solution.py:167
  12.9 2.6 %collective-permute-start.11 = (f32[1,16,384]{2,1,0:T(8,128)S(1)}, f32[1,16,384]{2,1,0:T(8,128)S(1)}, u32[]{:S(2)}, u32[]{:S(2)}) collective-permute-start(f32[1,16,384]{2,1,0:T(8,128)S(1)} %constant_dynamic-slice_fusion.1), channel_id=1, source_target_pairs={{0,17},{1,16},{2,19},{3,18},{4,21},{5,20},{6,23},{7,22},{8,25},{9,... | collective-permute-start | bytes 73736 | tf_op jit(solution)/shard_map/ppermute | solution.py:167
  15.5 0.2 %collective-permute-start.10 = (f32[1,8,384]{2,1,0:T(8,128)S(1)}, f32[1,8,384]{2,1,0:T(8,128)S(1)}, u32[]{:S(2)}, u32[]{:S(2)}) collective-permute-start(f32[1,8,384]{2,1,0:T(8,128)S(1)} %get-tuple-element.30), channel_id=1, source_target_pairs={{0,1},{1,0},{2,3},{3,2},{4,5},{5,4},{6,7},{7,6},{8,9},{9,8},{10,11... | collective-permute-start | bytes 36872 | tf_op jit(solution)/shard_map/ppermute | solution.py:167
  15.7 0.3 %collective-permute-start.9 = (f32[1,8,384]{2,1,0:T(8,128)S(1)}, f32[1,8,384]{2,1,0:T(8,128)S(1)}, u32[]{:S(2)}, u32[]{:S(2)}) collective-permute-start(f32[1,8,384]{2,1,0:T(8,128)S(1)} %get-tuple-element.29), channel_id=1, source_target_pairs={{0,1},{1,0},{2,3},{3,2},{4,5},{5,4},{6,7},{7,6},{8,9},{9,8},{10,11... | collective-permute-start | bytes 36872 | tf_op jit(solution)/shard_map/ppermute | solution.py:167
  16.0 0.7 %collective-permute-done.10 = f32[1,8,384]{2,1,0:T(8,128)S(1)} collective-permute-done((f32[1,8,384]{2,1,0:T(8,128)S(1)}, f32[1,8,384]{2,1,0:T(8,128)S(1)}, u32[]{:S(2)}, u32[]{:S(2)}) %collective-permute-start.10) | collective-permute-done | bytes 12320 | tf_op jit(solution)/shard_map/ppermute | solution.py:167
  16.7 0.2 %collective-permute-done.9 = f32[1,8,384]{2,1,0:T(8,128)S(1)} collective-permute-done((f32[1,8,384]{2,1,0:T(8,128)S(1)}, f32[1,8,384]{2,1,0:T(8,128)S(1)}, u32[]{:S(2)}, u32[]{:S(2)}) %collective-permute-start.9) | collective-permute-done | bytes 12320 | tf_op jit(solution)/shard_map/ppermute | solution.py:167
  16.9 0.3 %collective-permute-done.11 = f32[1,16,384]{2,1,0:T(8,128)S(1)} collective-permute-done((f32[1,16,384]{2,1,0:T(8,128)S(1)}, f32[1,16,384]{2,1,0:T(8,128)S(1)}, u32[]{:S(2)}, u32[]{:S(2)}) %collective-permute-start.11) | collective-permute-done | bytes 24608 | tf_op jit(solution)/shard_map/ppermute | solution.py:167
  17.2 0.6 %maximum_add_fusion.1 = f32[1,16,384]{2,1,0:T(8,128)} fusion(f32[1,16,384]{2,1,0:T(8,128)S(1)} %collective-permute-done.11, f32[1,8,384]{2,1,0:T(8,128)S(1)} %collective-permute-done.10, f32[1,8,384]{2,1,0:T(8,128)S(1)} %collective-permute-done.9), kind=kLoop, calls=%fused_computation.3 | loop fusion | flops 12288 | bytes 73728 | tf_op jit(solution)/shard_map/add | solution.py:261
  (17 shorter events, 0.2 us)
Async XLA Ops:
  0.0 4.2 %collective-permute-start = (f32[2,384]{1,0:T(2,128)}, f32[2,384]{1,0:T(2,128)S(1)}, u32[]{:S(2)}, u32[]{:S(2)}) collective-permute-start(f32[2,384]{1,0:T(2,128)} %wave_in.1), channel_id=1, source_target_pairs={{0,3},{1,2},{2,1},{3,0},{4,7},{5,6},{6,5},{7,4},{8,11},{9,10},{10,... | collective-permute-start | bytes 9224 | tf_op jit(solution)/shard_map/ppermute | solution.py:167
  2.4 3.1 %collective-permute-start.1 = (f32[2,384]{1,0:T(2,128)}, f32[2,384]{1,0:T(2,128)S(1)}, u32[]{:S(2)}, u32[]{:S(2)}) collective-permute-start(f32[2,384]{1,0:T(2,128)} %wave_in.1), channel_id=1, source_target_pairs={{0,1},{1,0},{2,3},{3,2},{4,5},{5,4},{6,7},{7,6},{8,9},{9,8},{10,11... | collective-permute-start | bytes 9224 | tf_op jit(solution)/shard_map/ppermute | solution.py:167
  3.1 1.5 %copy-start.2 = (s32[128,2]{0,1:T(2,128)S(1)}, s32[128,2]{0,1:T(2,128)}, u32[]{:S(2)}) copy-start(s32[128,2]{0,1:T(2,128)} %param.9) | copy-start | bytes 3076
  4.2 0.7 %copy-start = (f32[2,384]{1,0:T(2,128)S(1)}, f32[2,384]{1,0:T(2,128)}, u32[]{:S(2)}) copy-start(f32[2,384]{1,0:T(2,128)} %wave_in.1) | copy-start | bytes 9220
  4.3 1.3 %collective-permute-start.2 = (f32[2,384]{1,0:T(2,128)S(1)}, f32[2,384]{1,0:T(2,128)S(1)}, u32[]{:S(2)}, u32[]{:S(2)}) collective-permute-start(f32[2,384]{1,0:T(2,128)S(1)} %collective-permute-done.refs_3_), channel_id=1, source_target_pairs={{0,1},{1,0},{2,3},{3,2},{4,5},{5,4},{6,7},{7,6},{8,9},{9,8},{10,11... | collective-permute-start | bytes 9224 | tf_op jit(solution)/shard_map/ppermute | solution.py:167
  4.5 0.7 %copy-start.1 = (s32[128,2]{0,1:T(2,128)S(1)}, s32[128,2]{0,1:T(2,128)}, u32[]{:S(2)}) copy-start(s32[128,2]{0,1:T(2,128)} %param.8) | copy-start | bytes 3076
  4.5 0.7 %copy-start.3 = (f32[64]{0:T(128)S(1)}, f32[64]{0:T(128)}, u32[]{:S(2)}) copy-start(f32[64]{0:T(128)} %param.6) | copy-start | bytes 772
  6.5 4.4 %collective-permute-start.3 = (bf16[2,16,384]{2,1,0:T(8,128)(2,1)S(1)}, bf16[2,16,384]{2,1,0:T(8,128)(2,1)S(1)}, u32[]{:S(2)}, u32[]{:S(2)}) collective-permute-start(bf16[2,16,384]{2,1,0:T(8,128)(2,1)S(1)} %get-tuple-element.25), channel_id=1, source_target_pairs={{0,13},{1,12},{2,15},{3,14},{4,9},{5,8},{6,11},{7,10},{8,5},{9,4},... | collective-permute-start | bytes 73736 | tf_op jit(solution)/shard_map/ppermute | solution.py:167
  9.3 3.3 %collective-permute-start.8 = (bf16[2,16,384]{2,1,0:T(8,128)(2,1)S(1)}, bf16[2,16,384]{2,1,0:T(8,128)(2,1)S(1)}, u32[]{:S(2)}, u32[]{:S(2)}) collective-permute-start(bf16[2,16,384]{2,1,0:T(8,128)(2,1)S(1)} %get-tuple-element.28), channel_id=1, source_target_pairs={{0,5},{1,4},{2,7},{3,6},{4,1},{5,0},{6,3},{7,2},{8,13},{9,12},{10,... | collective-permute-start | bytes 73736 | tf_op jit(solution)/shard_map/ppermute | solution.py:167
  9.6 3.3 %collective-permute-start.7 = (bf16[2,16,384]{2,1,0:T(8,128)(2,1)S(1)}, bf16[2,16,384]{2,1,0:T(8,128)(2,1)S(1)}, u32[]{:S(2)}, u32[]{:S(2)}) collective-permute-start(bf16[2,16,384]{2,1,0:T(8,128)(2,1)S(1)} %get-tuple-element.27), channel_id=1, source_target_pairs={{0,9},{1,8},{2,11},{3,10},{4,13},{5,12},{6,15},{7,14},{8,1},{9,0},... | collective-permute-start | bytes 73736 | tf_op jit(solution)/shard_map/ppermute | solution.py:167
  10.9 2.0 %collective-permute-start.6 = (f32[2,16,128]{2,1,0:T(8,128)S(1)}, f32[2,16,128]{2,1,0:T(8,128)S(1)}, u32[]{:S(2)}, u32[]{:S(2)}) collective-permute-start(f32[2,16,128]{2,1,0:T(8,128)S(1)} %get-tuple-element.32), channel_id=1, source_target_pairs={{0,1},{1,0},{2,3},{3,2},{4,5},{5,4},{6,7},{7,6},{8,9},{9,8},{10,11... | collective-permute-start | bytes 49160 | tf_op jit(solution)/shard_map/ppermute | solution.py:167
  11.0 1.8 %collective-permute-start.5 = (f32[2,16,128]{2,1,0:T(8,128)S(1)}, f32[2,16,128]{2,1,0:T(8,128)S(1)}, u32[]{:S(2)}, u32[]{:S(2)}) collective-permute-start(f32[2,16,128]{2,1,0:T(8,128)S(1)} %get-tuple-element.33), channel_id=1, source_target_pairs={{0,1},{1,0},{2,3},{3,2},{4,5},{5,4},{6,7},{7,6},{8,9},{9,8},{10,11... | collective-permute-start | bytes 49160 | tf_op jit(solution)/shard_map/ppermute | solution.py:167
  11.4 1.5 %collective-permute-start.4 = (f32[2,16,128]{2,1,0:T(8,128)S(1)}, f32[2,16,128]{2,1,0:T(8,128)S(1)}, u32[]{:S(2)}, u32[]{:S(2)}) collective-permute-start(f32[2,16,128]{2,1,0:T(8,128)S(1)} %get-tuple-element.31), channel_id=1, source_target_pairs={{0,1},{1,0},{2,3},{3,2},{4,5},{5,4},{6,7},{7,6},{8,9},{9,8},{10,11... | collective-permute-start | bytes 49160 | tf_op jit(solution)/shard_map/ppermute | solution.py:167
  12.9 4.2 %collective-permute-start.11 = (f32[1,16,384]{2,1,0:T(8,128)S(1)}, f32[1,16,384]{2,1,0:T(8,128)S(1)}, u32[]{:S(2)}, u32[]{:S(2)}) collective-permute-start(f32[1,16,384]{2,1,0:T(8,128)S(1)} %constant_dynamic-slice_fusion.1), channel_id=1, source_target_pairs={{0,17},{1,16},{2,19},{3,18},{4,21},{5,20},{6,23},{7,22},{8,25},{9,... | collective-permute-start | bytes 73736 | tf_op jit(solution)/shard_map/ppermute | solution.py:167
  15.5 1.2 %collective-permute-start.10 = (f32[1,8,384]{2,1,0:T(8,128)S(1)}, f32[1,8,384]{2,1,0:T(8,128)S(1)}, u32[]{:S(2)}, u32[]{:S(2)}) collective-permute-start(f32[1,8,384]{2,1,0:T(8,128)S(1)} %get-tuple-element.30), channel_id=1, source_target_pairs={{0,1},{1,0},{2,3},{3,2},{4,5},{5,4},{6,7},{7,6},{8,9},{9,8},{10,11... | collective-permute-start | bytes 36872 | tf_op jit(solution)/shard_map/ppermute | solution.py:167
  15.7 1.2 %collective-permute-start.9 = (f32[1,8,384]{2,1,0:T(8,128)S(1)}, f32[1,8,384]{2,1,0:T(8,128)S(1)}, u32[]{:S(2)}, u32[]{:S(2)}) collective-permute-start(f32[1,8,384]{2,1,0:T(8,128)S(1)} %get-tuple-element.29), channel_id=1, source_target_pairs={{0,1},{1,0},{2,3},{3,2},{4,5},{5,4},{6,7},{7,6},{8,9},{9,8},{10,11... | collective-permute-start | bytes 36872 | tf_op jit(solution)/shard_map/ppermute | solution.py:167
